TPU v7x, 256 devices: a whole 4x4x8 slice. The times are simulated.
256 devices in a mesh: prompt: 16 (over z, x_lo), sample: 16 (over x_hi, y, core).
Axes of the slice: x: 4 (x_hi: 2, x_lo: 2; x = x_hi * 2 + x_lo), y: 4, z: 8, core: 2. Of those that a mesh axis runs over, the one named last changes fastest.
Arguments:
- queries: bfloat16 [16, 16, 32, 2048], P('prompt', 'sample'), may hold values from -12 to 12
- out_grad: bfloat16 [16, 16, 32, 2048], P('prompt', 'sample'), may hold values from -6 to 6
- advantage: float32 [16, 16], P('prompt', 'sample'), may hold values from -4 to 4
- comp_len: int32 [16, 16], P('prompt', 'sample'), may hold values from 1 to 32
- prefix_keys: bfloat16 [16, 2048, 512], P('prompt', 'sample'), may hold values from -4 to 4
- prefix_values: bfloat16 [16, 2048, 512], P('prompt', 'sample'), may hold values from -6 to 6
- own_keys: bfloat16 [16, 16, 32, 512], P('prompt', 'sample'), may hold values from -10 to 10
- own_values: bfloat16 [16, 16, 32, 512], P('prompt', 'sample'), may hold values from -6 to 6
- prompt_len: int32 [16], P('prompt'), may hold values from 512 to 2048
Outputs:
- query_grad: bfloat16 [16, 16, 32, 2048], P('prompt', 'sample')
- prefix_key_grad: bfloat16 [16, 2048, 512], P('prompt', 'sample')
- prefix_value_grad: bfloat16 [16, 2048, 512], P('prompt', 'sample')
- own_key_grad: bfloat16 [16, 16, 32, 512], P('prompt', 'sample')
- own_value_grad: bfloat16 [16, 16, 32, 512], P('prompt', 'sample')
All inputs are finite; a program needn't handle non-finite values.
Results may differ from a plain program's by a relative error of at most 0.0075.
Values may be sent and summed in bfloat16 or wider, within the bound.
No kernel may reach another device: no remote copies, remote signals or barrier semaphores. Data moves between devices by JAX's collectives and lax.ppermute only.
A program may use at most 64 MiB of HBM per device.

v0:
```python
import math

import jax
import jax.numpy as jnp
from jax import lax
from jax.sharding import PartitionSpec as P

HD = 128


MASKED = -1e30


def group_terms(
    all_q, all_g, key_rows, value_rows, key_ok, kv_group, group_size, head_dim, softmax_scale
):
    start_col = kv_group * group_size * head_dim
    end_col = start_col + group_size * head_dim
    row_count = all_q.shape[0]
    q_part = all_q[:, start_col:end_col].reshape(row_count, group_size, head_dim)
    g_part = all_g[:, start_col:end_col].reshape(row_count, group_size, head_dim)
    k_part = key_rows[:, kv_group * head_dim : (kv_group + 1) * head_dim]
    v_part = value_rows[:, kv_group * head_dim : (kv_group + 1) * head_dim]
    scores = (
        jnp.einsum("rxd,jd->xrj", q_part, k_part, preferred_element_type=jnp.float32)
        * softmax_scale
    )
    scores = jnp.where(key_ok[None, None, :], scores, MASKED)
    slopes = jnp.einsum("rxd,jd->xrj", g_part, v_part, preferred_element_type=jnp.float32)
    return (q_part, g_part, k_part, scores, slopes)


def per_device(
    queries,
    out_grad,
    advantage,
    comp_len,
    prefix_keys,
    prefix_values,
    own_keys,
    own_values,
    prompt_len,
):
    comp_count = queries.shape[1]
    slice_len = queries.shape[2]
    q_width = queries.shape[3]
    key_count = prefix_keys.shape[1]
    kv_width = prefix_keys.shape[2]
    head_dim = HD
    kv_heads = kv_width // head_dim
    group_size = q_width // head_dim // kv_heads
    softmax_scale = 1.0 / math.sqrt(head_dim)
    own_count = comp_count * slice_len
    positions = lax.iota(jnp.int32, slice_len)
    valid_mask = (positions[None, :] < comp_len[0][:, None]).astype(jnp.float32)
    token_weight = valid_mask * advantage[0][:, None]
    weighted = (out_grad[0].astype(jnp.float32) * token_weight[:, :, None]).astype(jnp.bfloat16)
    token_total = lax.psum(jnp.sum(comp_len.astype(jnp.float32)), ("prompt", "sample"))
    own_q = queries[0].reshape(own_count, q_width)
    own_g = weighted.reshape(own_count, q_width)
    all_q, all_g = (
        lax.all_gather(own_q, "sample", axis=0, tiled=True),
        lax.all_gather(own_g, "sample", axis=0, tiled=True),
    )
    row_count = all_q.shape[0]
    row_start = lax.axis_index("sample") * own_count
    root = jnp.zeros((), jnp.int32)
    key_rows = prefix_keys[0]
    value_rows = prefix_values[0]
    key_ok = lax.axis_index("sample") * key_count + lax.iota(jnp.int32, key_count) < prompt_len[0]
    q_five = queries[0].reshape(comp_count, slice_len, kv_heads, group_size, head_dim)
    g_five = weighted.reshape(comp_count, slice_len, kv_heads, group_size, head_dim)
    own_k = own_keys[0].reshape(comp_count, slice_len, kv_heads, head_dim)
    own_v = own_values[0].reshape(comp_count, slice_len, kv_heads, head_dim)
    causal = positions[None, :] <= positions[:, None]
    own_scores = (
        jnp.einsum("ctgxd,cugd->gxctu", q_five, own_k, preferred_element_type=jnp.float32)
        * softmax_scale
    )
    own_scores = jnp.where(causal, own_scores, MASKED)
    own_slopes = jnp.einsum("ctgxd,cugd->gxctu", g_five, own_v, preferred_element_type=jnp.float32)
    own_max = jnp.max(own_scores, axis=-1)
    own_exp = jnp.exp(own_scores - own_max[..., None])
    stat_shape = (kv_heads, group_size, row_count)
    own_rows_shape = (kv_heads, group_size, own_count)
    own_max_rows = lax.dynamic_update_slice(
        jnp.full(stat_shape, MASKED, jnp.float32),
        own_max.reshape(own_rows_shape),
        (root, root, row_start),
    )
    own_sum_rows = lax.dynamic_update_slice(
        jnp.zeros(stat_shape, jnp.float32),
        jnp.sum(own_exp, axis=-1).reshape(own_rows_shape),
        (root, root, row_start),
    )
    own_dot_rows = lax.dynamic_update_slice(
        jnp.zeros(stat_shape, jnp.float32),
        jnp.sum(own_exp * own_slopes, axis=-1).reshape(own_rows_shape),
        (root, root, row_start),
    )
    max_list, sum_list, dot_list = ([], [], [])
    for kv_group in range(kv_heads):
        terms = group_terms(
            all_q,
            all_g,
            key_rows,
            value_rows,
            key_ok,
            kv_group,
            group_size,
            head_dim,
            softmax_scale,
        )
        group_max = jnp.max(terms[3], axis=-1)
        group_exp = jnp.exp(terms[3] - group_max[..., None])
        max_list.append(group_max)
        sum_list.append(jnp.sum(group_exp, axis=-1))
        dot_list.append(jnp.sum(group_exp * terms[4], axis=-1))
    pre_max = jnp.stack(max_list)
    local_max = jnp.maximum(pre_max, own_max_rows)
    pre_shift = jnp.exp(pre_max - local_max)
    own_shift = jnp.exp(own_max_rows - local_max)
    local_sum = jnp.stack(sum_list) * pre_shift + own_sum_rows * own_shift
    local_dot = jnp.stack(dot_list) * pre_shift + own_dot_rows * own_shift
    row_max_all = lax.pmax(local_max.astype(jnp.bfloat16), "sample").astype(local_max.dtype)
    global_shift = jnp.exp(local_max - row_max_all)
    row_sum_all, row_dot_all = lax.psum(
        (local_sum * global_shift, local_dot * global_shift), "sample"
    )
    inv_sum = 1.0 / row_sum_all
    row_mean = row_dot_all * inv_sum
    key_grads, value_grads, query_terms = ([], [], [])
    for kv_group in range(kv_heads):
        q_part, g_part, k_part, scores, slopes = group_terms(
            all_q,
            all_g,
            key_rows,
            value_rows,
            key_ok,
            kv_group,
            group_size,
            head_dim,
            softmax_scale,
        )
        probs = jnp.exp(scores - row_max_all[kv_group][:, :, None]) * inv_sum[kv_group][:, :, None]
        dscore = (probs * (slopes - row_mean[kv_group][:, :, None])).astype(jnp.bfloat16)
        value_grads.append(
            jnp.einsum(
                "xrj,rxd->jd",
                probs.astype(jnp.bfloat16),
                g_part,
                preferred_element_type=jnp.float32,
            )
        )
        key_grads.append(
            jnp.einsum("xrj,rxd->jd", dscore, q_part, preferred_element_type=jnp.float32)
            * softmax_scale
        )
    mine_max = lax.dynamic_slice_in_dim(row_max_all, row_start, own_count, axis=2)
    mine_inv = lax.dynamic_slice_in_dim(inv_sum, row_start, own_count, axis=2)
    mine_mean = lax.dynamic_slice_in_dim(row_mean, row_start, own_count, axis=2)
    q_four = own_q.reshape(own_count, kv_heads, group_size, head_dim)
    g_four = own_g.reshape(own_count, kv_heads, group_size, head_dim)
    piece_k = lax.all_gather(key_rows, "sample", axis=0, tiled=True)
    piece_v = lax.all_gather(value_rows, "sample", axis=0, tiled=True)
    piece_len = piece_k.shape[0]
    k_three = piece_k.reshape(piece_len, kv_heads, head_dim)
    v_three = piece_v.reshape(piece_len, kv_heads, head_dim)
    piece_scores = (
        jnp.einsum("rgxd,jgd->gxrj", q_four, k_three, preferred_element_type=jnp.float32)
        * softmax_scale
    )
    piece_ok = lax.iota(jnp.int32, piece_len) < prompt_len[0]
    piece_scores = jnp.where(piece_ok[None, None, None, :], piece_scores, MASKED)
    piece_probs = jnp.exp(piece_scores - mine_max[..., None]) * mine_inv[..., None]
    piece_slopes = jnp.einsum("rgxd,jgd->gxrj", g_four, v_three, preferred_element_type=jnp.float32)
    piece_dscore = (piece_probs * (piece_slopes - mine_mean[..., None])).astype(jnp.bfloat16)
    update = jnp.einsum("gxrj,jgd->rgxd", piece_dscore, k_three, preferred_element_type=jnp.float32)
    query_sum = update.reshape(own_count, q_width) * softmax_scale
    own_grid = (kv_heads, group_size, comp_count, slice_len)
    own_probs = (
        jnp.exp(own_scores - mine_max.reshape(own_grid)[..., None])
        * mine_inv.reshape(own_grid)[..., None]
    )
    own_dscore = (own_probs * (own_slopes - mine_mean.reshape(own_grid)[..., None])).astype(
        jnp.bfloat16
    )
    own_query_term = (
        jnp.einsum(
            "gxctu,cugd->ctgxd", own_dscore, own_k, preferred_element_type=jnp.float32
        ).reshape(own_count, q_width)
        * softmax_scale
    )
    own_key_term = (
        jnp.einsum("gxctu,ctgxd->cugd", own_dscore, q_five, preferred_element_type=jnp.float32)
        * softmax_scale
    )
    own_value_term = jnp.einsum(
        "gxctu,ctgxd->cugd",
        own_probs.astype(jnp.bfloat16),
        g_five,
        preferred_element_type=jnp.float32,
    )
    slot_total = lax.axis_size("prompt") * lax.axis_size("sample") * own_count
    loss_scale = slot_total * math.sqrt(key_count * lax.axis_size("sample")) / (4.0 * token_total)
    query_out = (
        ((query_sum + own_query_term) * loss_scale)
        .astype(jnp.bfloat16)
        .reshape(1, comp_count, slice_len, q_width)
    )
    key_out = (jnp.concatenate(key_grads, axis=1) * loss_scale).astype(jnp.bfloat16)[None]
    value_out = (jnp.concatenate(value_grads, axis=1) * loss_scale).astype(jnp.bfloat16)[None]
    own_key_out = (
        (own_key_term * loss_scale).astype(jnp.bfloat16).reshape(1, comp_count, slice_len, kv_width)
    )
    own_value_out = (
        (own_value_term * loss_scale)
        .astype(jnp.bfloat16)
        .reshape(1, comp_count, slice_len, kv_width)
    )
    return (query_out, key_out, value_out, own_key_out, own_value_out)


def solution(mesh):
    in_specs = (
        P("prompt", "sample", None, None),
        P("prompt", "sample", None, None),
        P("prompt", "sample"),
        P("prompt", "sample"),
        P("prompt", "sample", None),
        P("prompt", "sample", None),
        P("prompt", "sample", None, None),
        P("prompt", "sample", None, None),
        P("prompt"),
    )
    out_specs = (
        P("prompt", "sample", None, None),
        P("prompt", "sample", None),
        P("prompt", "sample", None),
        P("prompt", "sample", None, None),
        P("prompt", "sample", None, None),
    )
    return jax.shard_map(
        per_device, mesh=mesh, in_specs=in_specs, out_specs=out_specs, check_vma=False
    )
```

profile of v0, /device:TPU:4, one launch (start us, length us, event | category | flops | bytes accessed | tf_op | source)
XLA Modules:
  0.0 401.8 jit_solution(14053936075004838599)
XLA Ops:
  8.5 1.6 fusion.66
  10.2 0.7 all-gather.12.cloned.1.call-update
  11.0 1.7 copy.112
  12.7 1.0 reshape_reshape_squeeze.3
  13.7 1.1 reshape.354
  14.9 0.8 reshape.343
  16.3 0.8 reshape.349
  17.8 0.6 copy-done.17
  18.4 1.0 fusion.70
  21.1 43.4 %all-gather.8.cloned.1.call-done = bf16[512,2048]{1,0:T(8,128)(2,1)} async-done(((bf16[32,2048]{1,0:T(8,128)(2,1)}), bf16[512,2048]{1,0:T(8,128)(2,1)}) %all-gather.8.cloned.1.call-update) | async-done | bytes 2097168 | tf_op jit(solution)/shard_map/all_gather | solution.py:63
  64.4 1.7 fusion.93
  66.1 1.0 copy.190
  67.1 1.0 copy.191
  68.1 1.0 copy.192
  69.1 1.0 copy.193
  70.1 48.5 %all-gather.12.cloned.1.call-done = bf16[1,1,512,2048]{3,2,1,0:T(8,128)(2,1)} async-done(((bf16[1,1,32,2048]{3,2,1,0:T(8,128)(2,1)}), bf16[1,1,512,2048]{3,2,1,0:T(8,128)(2,1)}) %all-gather.12.cloned.1.call-update) | async-done | bytes 2097168 | tf_op jit(solution)/shard_map/all_gather | solution.py:62
  118.7 2.9 copy.115
  121.7 0.7 copy-done.19
  123.4 1.3 fusion.98
  125.9 70.4 %pmax.7 = bf16[4,4,512]{2,1,0:T(4,128)(2,1)S(1)} all-reduce(bf16[4,4,512]{2,1,0:T(4,128)(2,1)} %fusion.91), channel_id=1, replica_groups=mesh['prompt'=16,'sample'=16] {'sample'}, use_global_device_ids=true, to_apply=%region_5.6 | all-reduce | flops 8192 | bytes 32768 | tf_op jit(solution)/shard_map/pmax | solution.py:125
  196.3 2.8 fusion.32
  199.2 1.3 fusion.33
  200.5 1.3 fusion.34
  201.8 1.4 fusion.35
  203.2 0.7 fusion.82
  203.9 0.7 fusion.84
  204.6 1.7 copy.123
  206.3 75.0 %psum.23 = f32[]{:T(128)} all-reduce(f32[]{:T(128)} %bitcast.66), channel_id=1, replica_groups=mesh['prompt'=16,'sample'=16] {'prompt','sample'}, use_global_device_ids=true, to_apply=%region_18.19 | all-reduce | flops 1 | bytes 8 | tf_op jit(solution)/shard_map/psum | solution.py:58
  283.3 4.2 %fusion.79 = f32[4,2048,32,4]{1,2,3,0:T(8,128)} fusion(bf16[2048,4,128,1]{0,2,3,1:T(8,128)(2,1)} %bitcast.302, bf16[32,4,4,128]{3,2,1,0:T(4,128)(2,1)S(1)} %reshape_reshape_squeeze.3), kind=kOutput, calls=%fused_computation.122 | convolution fusion | flops 268435456 | bytes 6422528 | tf_op jit(solution)/shard_map/rgxd,jgd->gxrj/dot_general | solution.py:170
  287.5 46.5 %all-reduce.3.cloned.1.call-done = (f32[4,4,512]{2,1,0:T(4,128)}, f32[4,4,512]{2,1,0:T(4,128)}) async-done(((f32[4,4,512]{2,1,0:T(4,128)}, f32[4,4,512]{2,1,0:T(4,128)}), (f32[4,4,512]{2,1,0:T(4,128)}, f32[4,4,512]{2,1,0:T(4,128)})) %all-reduce.3.cloned.1.call-update) | async-done | bytes 65552 | tf_op jit(solution)/shard_map/psum | solution.py:127
  334.0 0.8 broadcast_divide_fusion
  335.4 0.7 constant_dynamic-slice_fusion
  336.1 1.1 fusion.31
  337.8 1.4 reshape.353
  339.2 1.5 slice_bitcast_fusion.25
  340.8 1.8 convolution_bitcast_fusion.10
  342.6 1.0 convolution_bitcast_fusion.9
  343.6 1.1 convolution_bitcast_fusion.8
  345.1 0.7 fusion.65
  345.8 1.7 copy.152
  347.5 2.3 fusion.25
  351.8 0.8 copy.151
  352.6 1.0 fusion.74
  353.7 1.0 fusion.13
  354.8 33.6 %all-gather.14.cloned.1.call-done = bf16[1,2048,512]{1,2,0:T(8,128)(2,1)} async-done(((bf16[1,128,512]{1,2,0:T(8,128)(2,1)}), bf16[1,2048,512]{1,2,0:T(8,128)(2,1)}) %all-gather.14.cloned.1.call-update) | async-done | bytes 2097168 | tf_op jit(solution)/shard_map/all_gather | solution.py:165
  388.5 4.9 %fusion.16 = f32[32,4,4,128]{3,0,2,1:T(8,128)S(1)} fusion(bf16[2048,4,128,1]{0,2,3,1:T(8,128)(2,1)S(1)} %bitcast.303, f32[4,2048,32,4]{1,2,3,0:T(8,128)} %fusion.79, bf16[32,4,4,128]{3,0,2,1:T(8,128)(2,1)S(1)} %copy-done.18, bf16[2048,4,128,1]{0,2,3,1:T(8,128)(2,1)} %bitcast.336, f32[4,4,32]{2,1,0:T(4,128)S(1)} %copy-done.53, ...), kind=kOutput, calls=%fused_computation.29 | convolution fusion | flops 544276480 | bytes 8790016 | tf_op jit(solution)/shard_map/gxrj,jgd->rgxd/dot_general | solution.py:178
  393.9 0.6 reshape.351
  394.6 0.7 fusion.68
  (149 shorter events, 10.4 us)
Async XLA Ops:
  7.2 57.3 %all-gather.8.cloned.1.call-start = ((), (), s32[]{:S(2)}) async-start(), calls=%async_computation | async-start | bytes 2228224 | tf_op jit(solution)/shard_map/all_gather | solution.py:63
  10.2 108.5 %all-gather.12.cloned.1.call-start = ((), (), s32[]{:S(2)}) async-start(), calls=%async_computation.2 | async-start | bytes 2228224 | tf_op jit(solution)/shard_map/all_gather | solution.py:62
  10.9 272.3 %all-gather.10.cloned.1.call-start = ((), (), s32[]{:S(2)}) async-start(), calls=%async_computation.1 | async-start | bytes 2228224 | tf_op jit(solution)/shard_map/all_gather | solution.py:164
  12.7 321.3 %all-reduce.3.cloned.1.call-start = ((), (), s32[]{:S(2)}) async-start(), calls=%async_computation.4 | async-start | bytes 131072 | tf_op jit(solution)/shard_map/psum | solution.py:127
  15.6 1.8 copy-start.24
  17.7 2.8 copy-start.20
  121.7 1.7 copy-start.6
  121.7 1.7 copy-start.8
  121.7 1.7 copy-start.10
  121.7 1.7 copy-start.12
  122.7 2.0 copy-start.25
  122.7 2.6 copy-start.21
  123.1 1.7 copy-start.27
  196.3 2.8 copy-start
  196.3 2.8 copy-start.23
  196.3 2.8 copy-start.26
  196.3 4.1 %copy-start.2 = (bf16[512,512]{0,1:T(8,128)(2,1)S(1)}, bf16[512,512]{0,1:T(8,128)(2,1)}, u32[]{:S(2)}) copy-start(bf16[512,512]{0,1:T(8,128)(2,1)} %copy.192) | copy-start | bytes 1572868
  196.3 4.1 %copy-start.28 = (f32[4,512]{1,0:T(4,128)S(1)}, f32[4,512]{1,0:T(4,128)}, u32[]{:S(2)}) copy-start(f32[4,512]{1,0:T(4,128)} %copy-done.27) | copy-start | bytes 24580
  199.1 2.7 copy-start.4
  199.2 2.7 copy-start.30
  200.4 2.7 copy-start.22
  200.5 2.7 copy-start.32
  200.5 2.7 copy-start.38
  201.8 2.0 copy-start.36
  204.5 183.9 %all-gather.14.cloned.1.call-start = ((), (), s32[]{:S(2)}) async-start(), calls=%async_computation.3 | async-start | bytes 2228224 | tf_op jit(solution)/shard_map/all_gather | solution.py:165
  282.6 53.4 %copy-start.46 = (f32[4,4,32]{2,1,0:T(4,128)}, f32[4,4,32]{2,1,0:T(4,128)S(1)}, u32[]{:S(2)}) copy-start(f32[4,4,32]{2,1,0:T(4,128)S(1)} %constant_dynamic-slice_fusion.2) | copy-start | bytes 6148
  339.2 3.3 copy-start.1
  339.2 4.4 %copy-start.3 = (bf16[512,512]{0,1:T(8,128)(2,1)S(1)}, bf16[512,512]{0,1:T(8,128)(2,1)}, u32[]{:S(2)}) copy-start(bf16[512,512]{0,1:T(8,128)(2,1)} %copy.192) | copy-start | bytes 1572868
  340.7 1.8 copy-start.41
  340.7 4.0 copy-start.39
  340.7 4.0 copy-start.5
  340.8 4.0 copy-start.42
  347.4 2.3 copy-start.11
  347.4 2.4 copy-start.15
  347.4 2.4 copy-start.40
  347.4 2.4 copy-start.45
  347.4 2.4 copy-start.52
  347.4 2.9 copy-start.9
  347.5 2.9 copy-start.14
  347.5 2.9 copy-start.44
  347.5 2.9 copy-start.51
  349.8 1.5 copy-start.13
  350.8 1.8 copy-start.47
  351.3 37.1 %copy-start.16 = (bf16[1,2048,512]{1,2,0:T(8,128)(2,1)S(1)}, bf16[1,2048,512]{1,2,0:T(8,128)(2,1)}, u32[]{:S(2)}) copy-start(bf16[1,2048,512]{1,2,0:T(8,128)(2,1)} %all-gather.10.cloned.1.call-done) | copy-start | bytes 6291460
  351.8 36.7 %copy-start.18 = (bf16[32,4,4,128]{3,0,2,1:T(8,128)(2,1)S(1)}, bf16[32,4,4,128]{3,0,2,1:T(8,128)(2,1)}, u32[]{:S(2)}) copy-start(bf16[32,4,4,128]{3,0,2,1:T(8,128)(2,1)} %copy-done.17) | copy-start | bytes 393220
  351.8 36.7 %copy-start.49 = (f32[4,4,32]{2,1,0:T(4,128)S(1)}, f32[4,4,32]{2,1,0:T(4,128)}, u32[]{:S(2)}) copy-start(f32[4,4,32]{2,1,0:T(4,128)} %copy-done.48) | copy-start | bytes 6148
  351.8 36.6 %copy-start.53 = (f32[4,4,32]{2,1,0:T(4,128)S(1)}, f32[4,4,32]{2,1,0:T(4,128)}, u32[]{:S(2)}) copy-start(f32[4,4,32]{2,1,0:T(4,128)} %get-tuple-element.74) | copy-start | bytes 6148
  351.8 36.6 %copy-start.54 = (pred[2048]{0:T(1024)(128)(4,1)S(1)}, pred[2048]{0:T(1024)(128)(4,1)}, u32[]{:S(2)}) copy-start(pred[2048]{0:T(1024)(128)(4,1)} %iota_compare_fusion.1) | copy-start | bytes 6148
  (12 other events, 11.8 us)
Sparse Core Ops, SparseCore 0:
  11.3 53.0 all-gather.7
  67.2 51.4 all-gather.11
  121.8 51.0 all-gather.9
  204.7 129.2 all-reduce.2
  336.7 51.6 all-gather.13
where the time goes:
time: 407 us; the launch traced here: 402 us
  waiting for transfers between devices  173 us (43%)
  blocking collectives  145 us (36%)
  matrix products  29.7 us (7%)
  local copies, waits for them, and re-layouts  29.1 us (7%)
  between operations  17.2 us (4%)
  other arithmetic  7.58 us (2%)
    psum x1, blocking collectives, per_device(): lax.psum(jnp.sum(comp_len.astype(jnp.float32)), ('prompt', 'sample'))  75 us
    pmax x1, blocking collectives, per_device(): lax.pmax(local_max.astype(jnp.bfloat16), 'sample').astype(local_max.dtype)  70.4 us
    all_gather x1, waiting for transfers between devices, per_device(): lax.all_gather(own_q, 'sample', axis=0, tiled=True)  48.5 us
    psum x1, waiting for transfers between devices, per_device(): lax.psum((local_sum * global_shift, local_dot * global_shift), 'sample')  46.5 us
    all_gather x1, waiting for transfers between devices, per_device(): lax.all_gather(own_g, 'sample', axis=0, tiled=True)  43.4 us
    all_gather x1, waiting for transfers between devices, per_device(): piece_v = lax.all_gather(value_rows, 'sample', axis=0, tiled=True)  33.6 us
    unnamed x118, local copies, waits for them, and re-layouts  14.2 us
  transfers between devices with their start and end apart: 5, of which 4 were waited for; matrix products, arithmetic and copies ran while one was open for 13% of the time, Pallas kernels for 0%

commit v1 on v0

v1 whole, which is shorter than its diff:
```python
import functools
import math

import jax
import jax.numpy as jnp
from jax import lax
from jax.experimental import pallas as pl
from jax.experimental.pallas import tpu as pltpu
from jax.sharding import PartitionSpec as P

HD = 128
MASKED = -1e30
VMEM_LIMIT = 24 * 1024 * 1024
NT = (((1,), (1,)), ((), ()))
NN = (((1,), (0,)), ((), ()))


def dot(a, b, dims):
    return lax.dot_general(a, b, dims, preferred_element_type=jnp.float32)


def pack_kernel(len_ref, adv_ref, q_ref, g_ref, out_ref):
    tokens, width = q_ref.shape
    heads = width // HD
    at = lax.broadcasted_iota(jnp.int32, (tokens, HD), 0)
    weight = jnp.where(at < len_ref[0], adv_ref[0], 0.0)
    for h in range(heads):
        cols = slice(h * HD, (h + 1) * HD)
        out_ref[h * tokens : (h + 1) * tokens, :] = q_ref[:, cols]
        out_ref[(heads + h) * tokens : (heads + h + 1) * tokens, :] = (
            g_ref[:, cols].astype(jnp.float32) * weight
        ).astype(jnp.bfloat16)


def rows_of(refs, start, size):
    return jnp.concatenate([r[start : start + size, :] for r in refs], axis=0)


def cols_of(refs, g):
    return jnp.concatenate([r[:, g * HD : (g + 1) * HD] for r in refs], axis=0)


def key_bias(info_ref, block):
    at = lax.broadcasted_iota(jnp.int32, (block, 1), 0)
    return jnp.concatenate(
        [
            jnp.where(at + info_ref[1 + k] * block < info_ref[0], 0.0, MASKED)
            for k in range(4)
        ],
        axis=0,
    )


def own_mask(tokens, rows):
    u = lax.broadcasted_iota(jnp.int32, (tokens, rows), 0)
    t = lax.broadcasted_iota(jnp.int32, (tokens, rows), 1) % tokens
    return u <= t


def stats_kernel(to_log2, info_ref, tot_ref, *refs):
    qg, ks, vs = refs[0:4], refs[4:8], refs[8:12]
    ok_ref, ov_ref, out_ref = refs[12:15]
    block = ks[0].shape[0]
    groups = ks[0].shape[1] // HD
    tokens = ok_ref.shape[0]
    all_rows = qg[0].shape[0] // 2
    rows = all_rows // groups
    bias = key_bias(info_ref, block)
    causal = own_mask(tokens, rows)
    out_ref[48:56, :] = jnp.zeros((8, HD), jnp.float32) + tot_ref[0]
    for g in range(groups):
        q = rows_of(qg, g * rows, rows)
        w = rows_of(qg, all_rows + g * rows, rows)
        score = dot(cols_of(ks, g), q, NT) * to_log2 + bias
        slope = dot(cols_of(vs, g), w, NT)
        own_cols = slice(g * HD, (g + 1) * HD)
        own_score = dot(ok_ref[:, own_cols], q[:rows], NT) * to_log2
        own_score = jnp.where(causal, own_score, MASKED)
        own_slope = dot(ov_ref[:, own_cols], w[:rows], NT)
        top = jnp.max(score, axis=0, keepdims=True)
        own_top = jnp.maximum(
            top[:, :rows], jnp.max(own_score, axis=0, keepdims=True)
        )
        top = jnp.concatenate([own_top, top[:, rows:]], axis=1)
        e = jnp.exp2(score - top)
        total = jnp.sum(e, axis=0, keepdims=True)
        mixed = jnp.sum(e * slope, axis=0, keepdims=True)
        own_e = jnp.exp2(own_score - own_top)
        own_total = jnp.sum(own_e, axis=0, keepdims=True)
        own_mixed = jnp.sum(own_e * own_slope, axis=0, keepdims=True)
        for s in range(4):
            lanes = slice(s * rows, (s + 1) * rows)
            at = s * 4 + g
            out_ref[at : at + 1, :] = top[:, lanes]
            extra = (own_total, own_mixed) if s == 0 else (0.0, 0.0)
            out_ref[16 + at : 17 + at, :] = total[:, lanes] + extra[0]
            out_ref[32 + at : 33 + at, :] = mixed[:, lanes] + extra[1]


def grads_kernel(to_log2, info_ref, *refs):
    qg, ks, vs = refs[0:4], refs[4:8], refs[8:12]
    ok_ref, ov_ref = refs[12:14]
    stats = refs[14:18]
    dq_own, dq_far, dq_sib, dkv_own = refs[18:22]
    dkv_out = refs[22:25]
    own_out, tot_out = refs[25:27]
    block = ks[0].shape[0]
    groups = ks[0].shape[1] // HD
    tokens = ok_ref.shape[0]
    all_rows = qg[0].shape[0] // 2
    rows = all_rows // groups
    bias = key_bias(info_ref, block)
    causal = own_mask(tokens, rows)
    shifts, means = [], []
    for s in range(4):
        tops = [stats[e][(s ^ e) * 4 : (s ^ e) * 4 + 4, :] for e in range(4)]
        top = functools.reduce(jnp.maximum, tops)
        total, mixed = 0.0, 0.0
        for e in range(4):
            factor = jnp.exp2(tops[e] - top)
            at = (s ^ e) * 4
            total += stats[e][16 + at : 20 + at, :] * factor
            mixed += stats[e][32 + at : 36 + at, :] * factor
        shifts.append(top + jnp.log2(total))
        means.append(mixed / total)
    shift = jnp.concatenate(shifts, axis=1)
    mean = jnp.concatenate(means, axis=1)
    count = sum(stats[e][48:56, :] for e in range(4))
    tot_out[...] = count
    high = jnp.floor(count * (1.0 / 256.0))
    marks = jnp.concatenate([high, count - high * 256.0], axis=0).astype(jnp.bfloat16)
    half = groups * block
    for ref in dkv_out:
        ref[2 * half : 2 * half + 16, :] = marks
    for g in range(groups):
        q = rows_of(qg, g * rows, rows)
        w = rows_of(qg, all_rows + g * rows, rows)
        k = cols_of(ks, g)
        sh, mn = shift[g : g + 1, :], mean[g : g + 1, :]
        score = dot(k, q, NT) * to_log2 + bias
        slope = dot(cols_of(vs, g), w, NT)
        p = jnp.exp2(score - sh)
        ds = (p * (slope - mn)).astype(jnp.bfloat16)
        dv = dot(p.astype(jnp.bfloat16), w, NN)
        dk = dot(ds, q, NN)
        dq = dot(k.T, ds, NN)
        own_cols = slice(g * HD, (g + 1) * HD)
        own_k = ok_ref[:, own_cols]
        own_score = dot(own_k, q[:rows], NT) * to_log2
        own_score = jnp.where(causal, own_score, MASKED)
        own_slope = dot(ov_ref[:, own_cols], w[:rows], NT)
        own_p = jnp.exp2(own_score - sh[:, :rows])
        own_ds = (own_p * (own_slope - mn[:, :rows])).astype(jnp.bfloat16)
        own_out[:tokens, own_cols] = dot(own_ds, q[:rows], NN)
        own_out[tokens:, own_cols] = dot(own_p.astype(jnp.bfloat16), w[:rows], NN)
        own_dq = dot(own_k.T, own_ds, NN)
        at = slice(g * HD, (g + 1) * HD)
        dq_own[at, :] = dq[:, :rows] + own_dq
        dq_far[at, :] = dq[:, 2 * rows : 3 * rows]
        dq_sib[at, :] = dq[:, rows : 2 * rows].astype(jnp.bfloat16)
        dq_sib[half_at(dq_sib, g), :] = dq[:, 3 * rows :].astype(jnp.bfloat16)
        here = slice(g * block, (g + 1) * block)
        there = slice(half + g * block, half + (g + 1) * block)
        dkv_own[here, :] = dk[:block]
        dkv_own[there, :] = dv[:block]
        for e in range(3):
            part = slice((e + 1) * block, (e + 2) * block)
            dkv_out[e][here, :] = dk[part].astype(jnp.bfloat16)
            dkv_out[e][there, :] = dv[part].astype(jnp.bfloat16)


def half_at(ref, g):
    half = ref.shape[0] // 2
    return slice(half + g * HD, half + (g + 1) * HD)


def finish_kernel(loss_top, softmax_scale, *refs):
    dq_own, dq_core, dq_x, dkv_own, r1, r2, r3, own_ref, tot_ref = refs[:9]
    q_out, k_out, v_out, ok_out, ov_out = refs[9:]
    block = k_out.shape[0]
    groups = k_out.shape[1] // HD
    tokens = ok_out.shape[0]
    per_group = q_out.shape[1] // HD // groups
    half = groups * block
    f32 = jnp.float32
    count = tot_ref[...]
    for r in (r1, r2, r3):
        marks = r[2 * half : 2 * half + 16, :].astype(f32)
        count = count + marks[:8] * 256.0 + marks[8:]
    scale = loss_top / count[:1, :]
    key_scale = scale * softmax_scale
    for g in range(groups):
        cols = slice(g * HD, (g + 1) * HD)
        dq = (
            dq_own[cols, :]
            + dq_core[cols, :].astype(f32)
            + dq_x[cols, :].astype(f32)
        ).T * key_scale
        for x in range(per_group):
            h = g * per_group + x
            q_out[:, h * HD : (h + 1) * HD] = dq[x * tokens : (x + 1) * tokens].astype(
                jnp.bfloat16
            )
        for out, start, by in ((k_out, 0, key_scale), (v_out, half, scale)):
            at = slice(start + g * block, start + (g + 1) * block)
            term = (dkv_own[at, :] + r1[at, :].astype(f32)) + (
                r2[at, :].astype(f32) + r3[at, :].astype(f32)
            )
            out[:, cols] = (term * by).astype(jnp.bfloat16)
        ok_out[:, cols] = (own_ref[:tokens, cols] * key_scale).astype(jnp.bfloat16)
        ov_out[:, cols] = (own_ref[tokens:, cols] * scale).astype(jnp.bfloat16)


def per_device(
    queries,
    out_grad,
    advantage,
    comp_len,
    prefix_keys,
    prefix_values,
    own_keys,
    own_values,
    prompt_len,
):
    samples = lax.axis_size("sample")
    prompts = lax.axis_size("prompt")
    tokens, width = queries.shape[2], queries.shape[3]
    block, kv_width = prefix_keys.shape[1], prefix_keys.shape[2]
    groups = kv_width // HD
    softmax_scale = 1.0 / math.sqrt(HD)
    to_log2 = softmax_scale * math.log2(math.e)
    loss_top = prompts * samples * tokens * math.sqrt(block * samples) / 4.0
    bf16, f32 = jnp.bfloat16, jnp.float32
    vmem = pl.BlockSpec(memory_space=pltpu.VMEM)
    smem = pl.BlockSpec(memory_space=pltpu.SMEM)
    params = pltpu.CompilerParams(vmem_limit_bytes=VMEM_LIMIT)
    shape = jax.ShapeDtypeStruct

    def swap(array, mask):
        return lax.ppermute(array, "sample", [(i, i ^ mask) for i in range(samples)])

    k0, v0 = prefix_keys[0], prefix_values[0]
    ks = [k0] + [swap(k0, 2 * e) for e in (1, 2, 3)]
    vs = [v0] + [swap(v0, 2 * e) for e in (1, 2, 3)]
    all_rows = width // HD * tokens
    qg0 = pl.pallas_call(
        pack_kernel,
        out_shape=shape((2 * all_rows, HD), bf16),
        in_specs=[smem, smem, vmem, vmem],
        out_specs=vmem,
        compiler_params=params,
        name="pack",
    )(comp_len[0], advantage[0], queries[0, 0], out_grad[0, 0])
    qg1 = swap(qg0, 1)
    qg2 = swap(qg0, 8)
    qg3 = swap(qg2, 1)
    qg = [qg0, qg1, qg2, qg3]
    counts = lax.all_to_all(
        jnp.broadcast_to(comp_len[0].astype(f32)[None], (prompts, 1)),
        "prompt",
        0,
        0,
        tiled=True,
    )
    count = jnp.sum(counts, axis=0)
    me = lax.axis_index("sample")
    info = jnp.stack([prompt_len[0]] + [me ^ (2 * e) for e in range(4)]).astype(jnp.int32)
    own_k, own_v = own_keys[0, 0], own_values[0, 0]
    stats0 = pl.pallas_call(
        functools.partial(stats_kernel, to_log2),
        out_shape=shape((56, HD), f32),
        in_specs=[smem, smem] + [vmem] * 14,
        out_specs=vmem,
        compiler_params=params,
        name="stats",
    )(info, count, *qg, *ks, *vs, own_k, own_v)
    stats = [stats0, swap(stats0, 1), swap(stats0, 8), swap(stats0, 9)]
    kv_rows = 2 * groups * block
    dq_rows = width // HD // 4 * HD
    outs = pl.pallas_call(
        functools.partial(grads_kernel, to_log2),
        out_shape=[
            shape((dq_rows, HD), f32),
            shape((dq_rows, HD), f32),
            shape((2 * dq_rows, HD), bf16),
            shape((kv_rows, HD), f32),
        ]
        + [shape((kv_rows + 16, HD), bf16)] * 3
        + [shape((2 * tokens, kv_width), f32), shape((8, HD), f32)],
        in_specs=[smem] + [vmem] * 18,
        out_specs=[vmem] * 9,
        compiler_params=params,
        name="grads",
    )(info, *qg, *ks, *vs, own_k, own_v, *stats)
    dq_own, dq_far, dq_sib, dkv_own = outs[:4]
    dq_core = swap(dq_sib, 1)
    dq_x = swap((dq_far + dq_core[dq_rows:].astype(f32)).astype(bf16), 8)
    received = [swap(outs[3 + e], 2 * e) for e in (1, 2, 3)]
    q_out, k_out, v_out, ok_out, ov_out = pl.pallas_call(
        functools.partial(finish_kernel, loss_top, softmax_scale),
        out_shape=[
            shape((tokens, width), bf16),
            shape((block, kv_width), bf16),
            shape((block, kv_width), bf16),
            shape((tokens, kv_width), bf16),
            shape((tokens, kv_width), bf16),
        ],
        in_specs=[vmem] * 9,
        out_specs=[vmem] * 5,
        compiler_params=params,
        name="finish",
    )(dq_own, dq_core, dq_x, dkv_own, *received, outs[7], outs[8])
    return (q_out[None, None], k_out[None], v_out[None], ok_out[None, None], ov_out[None, None])


def solution(mesh):
    in_specs = (
        P("prompt", "sample", None, None),
        P("prompt", "sample", None, None),
        P("prompt", "sample"),
        P("prompt", "sample"),
        P("prompt", "sample", None),
        P("prompt", "sample", None),
        P("prompt", "sample", None, None),
        P("prompt", "sample", None, None),
        P("prompt"),
    )
    out_specs = (
        P("prompt", "sample", None, None),
        P("prompt", "sample", None),
        P("prompt", "sample", None),
        P("prompt", "sample", None, None),
        P("prompt", "sample", None, None),
    )
    return jax.shard_map(
        per_device, mesh=mesh, in_specs=in_specs, out_specs=out_specs, check_vma=False
    )
```

time: 407 us -> 71.9 us (0.18)
  waiting for transfers between devices: 173 us -> 26.8 us
  blocking collectives: 145 us -> 0 us
  starting transfers between devices: 0.2 us -> 30.1 us
  matrix products: 29.7 us -> 0 us
  local copies, waits for them, and re-layouts: 29.1 us -> 2.5 us
  between operations: 17.2 us -> 2.67 us
  Pallas kernels: 0 us -> 7.89 us
  other arithmetic: 7.58 us -> 0.65 us
    all_gather x4 -> x0, waiting for transfers between devices: 125 us -> none  [the longest x1 48.5 us: per_device(): lax.all_gather(own_q, 'sample', axis=0, tiled=True)]
    psum x1 -> x0, blocking collectives: 75 us -> none  [per_device(): lax.psum(jnp.sum(comp_len.astype(jnp.float32)), ('prompt', 'sample'))]
    pmax x1 -> x0, blocking collectives: 70.4 us -> none  [per_device(): lax.pmax(local_max.astype(jnp.bfloat16), 'sample').astype(local_max.dtype)]
    psum x1 -> x0, waiting for transfers between devices: 46.5 us -> none  [per_device(): lax.psum((local_sum * global_shift, local_dot * global_shift), 'sample')]
    dot_general x23 -> x0, matrix products: 29.7 us -> none  [the longest x4 6.75 us: group_terms(): jnp.einsum('rxd,jd->xrj', g_part, v_part, preferred_element_type=jnp.floa...]
    ppermute x0 -> x17, starting transfers between devices: none -> 21.4 us  [swap(): lax.ppermute(array, 'sample', [(i, i ^ mask) for i in range(samples)])]
    ppermute x0 -> x17, waiting for transfers between devices: none -> 19.1 us  [swap(): lax.ppermute(array, 'sample', [(i, i ^ mask) for i in range(samples)])]
    unnamed x118 -> x12, local copies, waits for them, and re-layouts: 14.2 us -> 1.82 us
  transfers between devices with their start and end apart: 5 -> 18, of which waited for: 4 -> 8; matrix products, arithmetic and copies ran while one was open for 13% -> 2% of each run, Pallas kernels for 0% -> 0%
where the time goes in v1:
time: 71.9 us; the launch traced here: 70.6 us
  starting transfers between devices  30.1 us (42%)
  waiting for transfers between devices  26.8 us (37%)
  Pallas kernels  7.89 us (11%)
  between operations  2.67 us (4%)
  local copies, waits for them, and re-layouts  2.5 us (3%)
    ppermute x17, starting transfers between devices, swap(): lax.ppermute(array, 'sample', [(i, i ^ mask) for i in range(samples)])  21.4 us
    ppermute x17, waiting for transfers between devices, swap(): lax.ppermute(array, 'sample', [(i, i ^ mask) for i in range(samples)])  19.1 us
    all_to_all x1, starting transfers between devices, per_device(): lax.all_to_all(jnp.broadcast_to(comp_len[0].astype(f32)[None], (prompts,...  8.72 us
    all_to_all x1, waiting for transfers between devices, per_device(): lax.all_to_all(jnp.broadcast_to(comp_len[0].astype(f32)[None], (prompts,...  7.68 us
    pallas_call x1, Pallas kernels, per_device(): pl.pallas_call(functools.partial(grads_kernel, to_log2), out_shape=[shape...  3.92 us
    pallas_call x1, Pallas kernels, per_device(): pl.pallas_call(functools.partial(stats_kernel, to_log2), out_shape=shape(...  3.03 us
    unnamed x12, local copies, waits for them, and re-layouts  1.82 us
  transfers between devices with their start and end apart: 18, of which 8 were waited for; matrix products, arithmetic and copies ran while one was open for 2% of the time, Pallas kernels for 0%

profile of v1, /device:TPU:4, one launch (start us, length us, event | category | flops | bytes accessed | tf_op | source)
XLA Modules:
  0.0 70.6 jit_solution(10778987492861077819)
XLA Ops:
  1.9 0.0 copy-start.4
  1.9 0.9 %copy-done.4 = bf16[1,1,32,2048]{3,2,1,0:T(8,128)(2,1)S(1)} copy-done((bf16[1,1,32,2048]{3,2,1,0:T(8,128)(2,1)S(1)}, bf16[1,1,32,2048]{3,2,1,0:T(8,128)(2,1)}, u32[]{:S(2)}) %copy-start.4) | copy-done | bytes 131096
  2.8 0.9 %copy-done.5 = bf16[1,1,32,2048]{3,2,1,0:T(8,128)(2,1)S(1)} copy-done((bf16[1,1,32,2048]{3,2,1,0:T(8,128)(2,1)S(1)}, bf16[1,1,32,2048]{3,2,1,0:T(8,128)(2,1)}, u32[]{:S(2)}) %copy-start.5) | copy-done | bytes 131096
  3.8 2.3 %collective-permute-start.1 = (bf16[1024,128]{1,0:T(8,128)(2,1)S(1)}, bf16[1024,128]{1,0:T(8,128)(2,1)S(1)}, u32[]{:S(2)}, u32[]{:S(2)}) collective-permute-start(bf16[1024,128]{1,0:T(8,128)(2,1)S(1)} %pack.1.refs_0_), channel_id=1, source_target_pairs={{0,8},{1,9},{2,10},{3,11},{4,12},{5,13},{6,14},{7,15},{8,0},{9,1},... | collective-permute-start | bytes 786440 | tf_op jit(solution)/shard_map/ppermute | solution.py:240
  6.1 0.0 copy-done
  6.1 1.5 %collective-permute-start.5 = (bf16[128,512]{1,0:T(8,128)(2,1)S(1)}, bf16[128,512]{1,0:T(8,128)(2,1)S(1)}, u32[]{:S(2)}, u32[]{:S(2)}) collective-permute-start(bf16[128,512]{1,0:T(8,128)(2,1)S(1)} %bitcast.22), channel_id=1, source_target_pairs={{0,6},{1,7},{2,4},{3,5},{4,2},{5,3},{6,0},{7,1},{8,14},{9,15},{10,... | collective-permute-start | bytes 393224 | tf_op jit(solution)/shard_map/ppermute | solution.py:240
  7.7 0.6 collective-permute-start.4
  8.3 1.9 %collective-permute-start.3 = (bf16[128,512]{1,0:T(8,128)(2,1)S(1)}, bf16[128,512]{1,0:T(8,128)(2,1)S(1)}, u32[]{:S(2)}, u32[]{:S(2)}) collective-permute-start(bf16[128,512]{1,0:T(8,128)(2,1)S(1)} %bitcast.24), channel_id=1, source_target_pairs={{0,2},{1,3},{2,0},{3,1},{4,6},{5,7},{6,4},{7,5},{8,10},{9,11},{10,... | collective-permute-start | bytes 393224 | tf_op jit(solution)/shard_map/ppermute | solution.py:240
  10.2 0.0 collective-permute-start
  10.2 3.2 %collective-permute-done.1.refs_2_ = bf16[1024,128]{1,0:T(8,128)(2,1)S(1)} collective-permute-done((bf16[1024,128]{1,0:T(8,128)(2,1)S(1)}, bf16[1024,128]{1,0:T(8,128)(2,1)S(1)}, u32[]{:S(2)}, u32[]{:S(2)}) %collective-permute-start.1) | collective-permute-done | bytes 262176 | tf_op jit(solution)/shard_map/ppermute | solution.py:240
  13.4 0.0 collective-permute-start.2
  13.4 1.2 %collective-permute-done.5.refs_7_ = bf16[128,512]{1,0:T(8,128)(2,1)S(1)} collective-permute-done((bf16[128,512]{1,0:T(8,128)(2,1)S(1)}, bf16[128,512]{1,0:T(8,128)(2,1)S(1)}, u32[]{:S(2)}, u32[]{:S(2)}) %collective-permute-start.5) | collective-permute-done | bytes 131104 | tf_op jit(solution)/shard_map/ppermute | solution.py:240
  14.6 0.0 copy-done.1
  14.6 2.3 %collective-permute-start.8 = (bf16[128,512]{1,0:T(8,128)(2,1)S(1)}, bf16[128,512]{1,0:T(8,128)(2,1)S(1)}, u32[]{:S(2)}, u32[]{:S(2)}) collective-permute-start(bf16[128,512]{1,0:T(8,128)(2,1)S(1)} %bitcast.27), channel_id=1, source_target_pairs={{0,6},{1,7},{2,4},{3,5},{4,2},{5,3},{6,0},{7,1},{8,14},{9,15},{10,... | collective-permute-start | bytes 393224 | tf_op jit(solution)/shard_map/ppermute | solution.py:240
  16.9 0.0 collective-permute-done.4.refs_6_
  16.9 0.2 collective-permute-start.7
  17.2 0.0 collective-permute-done.3.refs_5_
  17.2 1.5 %collective-permute-start.6 = (bf16[128,512]{1,0:T(8,128)(2,1)S(1)}, bf16[128,512]{1,0:T(8,128)(2,1)S(1)}, u32[]{:S(2)}, u32[]{:S(2)}) collective-permute-start(bf16[128,512]{1,0:T(8,128)(2,1)S(1)} %bitcast.29), channel_id=1, source_target_pairs={{0,2},{1,3},{2,0},{3,1},{4,6},{5,7},{6,4},{7,5},{8,10},{9,11},{10,... | collective-permute-start | bytes 393224 | tf_op jit(solution)/shard_map/ppermute | solution.py:240
  18.7 0.6 broadcast_in_dim.24
  19.3 8.7 %all-to-all-start = ((f32[16,1,1]{2,1,0:T(1,128)}), f32[16,1,1]{2,1,0:T(1,128)S(1)}, u32[]{:S(2)}, u32[]{:S(2)}) async-start(f32[16,1,1]{2,1,0:T(1,128)} %broadcast_in_dim.24), calls=%async_computation | async-start | bytes 16384 | tf_op jit(solution)/shard_map/all_to_all | solution.py:258
  28.7 0.1 stack.19.info_ref
  28.8 7.7 %all-to-all-done = f32[16,1,1]{2,1,0:T(1,128)S(1)} async-done(((f32[16,1,1]{2,1,0:T(1,128)}), f32[16,1,1]{2,1,0:T(1,128)S(1)}, u32[]{:S(2)}, u32[]{:S(2)}) %all-to-all-start) | async-done | bytes 96 | tf_op jit(solution)/shard_map/all_to_all | solution.py:258
  36.5 0.6 reduce_sum.11
  37.1 0.0 collective-permute-done.8.refs_11_
  37.1 0.0 collective-permute-done.7.refs_10_
  37.1 0.0 collective-permute-done.6.refs_9_
  37.1 0.0 collective-permute-done.refs_1_
  37.1 0.0 collective-permute-done.2.refs_3_
  37.1 0.0 copy-done.2
  37.1 3.0 %stats.1.refs_14_ = f32[56,128]{1,0:T(8,128)S(1)} custom-call(s32[5]{0:T(128)S(1)} %stack.19.info_ref, f32[1]{0:T(128)} %bitcast.13.tot_ref, bf16[1024,128]{1,0:T(8,128)(2,1)S(1)} %pack.1.refs_0_, bf16[1024,128]{1,0:T(8,128)(2,1)S(1)} %collective-permute-done.refs_1_, bf16[1024,128]{1,0:T(8,128)(2,1)S(1)} %collective-permute-done.1.refs_2_, ...), custom_call_target="tpu_custom_call" | custom-call | tf_op jit(solution)/shard_map/stats/pallas_call | solution.py:269
  40.2 0.1 collective-permute-start.11
  40.3 1.6 %collective-permute-start.10 = (f32[56,128]{1,0:T(8,128)S(1)}, f32[56,128]{1,0:T(8,128)S(1)}, u32[]{:S(2)}, u32[]{:S(2)}) collective-permute-start(f32[56,128]{1,0:T(8,128)S(1)} %stats.1.refs_14_), channel_id=1, source_target_pairs={{0,8},{1,9},{2,10},{3,11},{4,12},{5,13},{6,14},{7,15},{8,0},{9,1},... | collective-permute-start | bytes 86024 | tf_op jit(solution)/shard_map/ppermute | solution.py:240
  41.9 1.7 %collective-permute-start.9 = (f32[56,128]{1,0:T(8,128)S(1)}, f32[56,128]{1,0:T(8,128)S(1)}, u32[]{:S(2)}, u32[]{:S(2)}) collective-permute-start(f32[56,128]{1,0:T(8,128)S(1)} %stats.1.refs_14_), channel_id=1, source_target_pairs={{0,1},{1,0},{2,3},{3,2},{4,5},{5,4},{6,7},{7,6},{8,9},{9,8},{10,11... | collective-permute-start | bytes 86024 | tf_op jit(solution)/shard_map/ppermute | solution.py:240
  43.6 1.4 %collective-permute-done.11.refs_17_ = f32[56,128]{1,0:T(8,128)S(1)} collective-permute-done((f32[56,128]{1,0:T(8,128)S(1)}, f32[56,128]{1,0:T(8,128)S(1)}, u32[]{:S(2)}, u32[]{:S(2)}) %collective-permute-start.11) | collective-permute-done | bytes 28704 | tf_op jit(solution)/shard_map/ppermute | solution.py:240
  45.1 0.7 collective-permute-done.10.refs_16_
  45.7 0.0 collective-permute-done.9.refs_15_
  45.7 3.9 %grads.1 = (f32[512,128]{1,0:T(8,128)S(1)}, f32[512,128]{1,0:T(8,128)S(1)}, bf16[1024,128]{1,0:T(8,128)(2,1)S(1)}, f32[1024,128]{1,0:T(8,128)S(1)}, bf16[1040,12...) custom-call(s32[5]{0:T(128)S(1)} %stack.19.info_ref, ...), custom_call_target="tpu_custom_call" | custom-call | tf_op jit(solution)/shard_map/grads/pallas_call | solution.py:280
  49.6 0.7 collective-permute-start.12
  50.3 1.2 %collective-permute-start.14 = (bf16[1040,128]{1,0:T(8,128)(2,1)S(1)}, bf16[1040,128]{1,0:T(8,128)(2,1)S(1)}, u32[]{:S(2)}, u32[]{:S(2)}) collective-permute-start(bf16[1040,128]{1,0:T(8,128)(2,1)S(1)} %get-tuple-element.23), channel_id=1, source_target_pairs={{0,2},{1,3},{2,0},{3,1},{4,6},{5,7},{6,4},{7,5},{8,10},{9,11},{10,... | collective-permute-start | bytes 798728 | tf_op jit(solution)/shard_map/ppermute | solution.py:240
  51.5 3.4 %collective-permute-start.15 = (bf16[1040,128]{1,0:T(8,128)(2,1)S(1)}, bf16[1040,128]{1,0:T(8,128)(2,1)S(1)}, u32[]{:S(2)}, u32[]{:S(2)}) collective-permute-start(bf16[1040,128]{1,0:T(8,128)(2,1)S(1)} %get-tuple-element.24), channel_id=1, source_target_pairs={{0,4},{1,5},{2,6},{3,7},{4,0},{5,1},{6,2},{7,3},{8,12},{9,13},{10,... | collective-permute-start | bytes 798728 | tf_op jit(solution)/shard_map/ppermute | solution.py:240
  54.9 0.1 collective-permute-start.16
  55.0 0.0 collective-permute-done.12.refs_1_
  55.0 2.1 %collective-permute-start.13 = (bf16[512,128]{1,0:T(8,128)(2,1)S(1)}, bf16[512,128]{1,0:T(8,128)(2,1)S(1)}, u32[]{:S(2)}, u32[]{:S(2)}) collective-permute-start(bf16[512,128]{1,0:T(8,128)(2,1)S(1)} %add_convert_fusion), channel_id=1, source_target_pairs={{0,8},{1,9},{2,10},{3,11},{4,12},{5,13},{6,14},{7,15},{8,0},{9,1},... | collective-permute-start | bytes 393224 | tf_op jit(solution)/shard_map/ppermute | solution.py:240
  57.1 2.4 %collective-permute-done.14.refs_4_ = bf16[1040,128]{1,0:T(8,128)(2,1)S(1)} collective-permute-done((bf16[1040,128]{1,0:T(8,128)(2,1)S(1)}, bf16[1040,128]{1,0:T(8,128)(2,1)S(1)}, u32[]{:S(2)}, u32[]{:S(2)}) %collective-permute-start.14) | collective-permute-done | bytes 266272 | tf_op jit(solution)/shard_map/ppermute | solution.py:240
  59.5 7.6 %collective-permute-done.15.refs_5_ = bf16[1040,128]{1,0:T(8,128)(2,1)S(1)} collective-permute-done((bf16[1040,128]{1,0:T(8,128)(2,1)S(1)}, bf16[1040,128]{1,0:T(8,128)(2,1)S(1)}, u32[]{:S(2)}, u32[]{:S(2)}) %collective-permute-start.15) | collective-permute-done | bytes 266272 | tf_op jit(solution)/shard_map/ppermute | solution.py:240
  67.1 2.6 %collective-permute-done.16.refs_6_ = bf16[1040,128]{1,0:T(8,128)(2,1)S(1)} collective-permute-done((bf16[1040,128]{1,0:T(8,128)(2,1)S(1)}, bf16[1040,128]{1,0:T(8,128)(2,1)S(1)}, u32[]{:S(2)}, u32[]{:S(2)}) %collective-permute-start.16) | collective-permute-done | bytes 266272 | tf_op jit(solution)/shard_map/ppermute | solution.py:240
  69.7 0.0 collective-permute-done.13.refs_2_
  69.7 0.9 %finish.1 = (bf16[32,2048]{1,0:T(8,128)(2,1)}, bf16[128,512]{1,0:T(8,128)(2,1)}, bf16[128,512]{1,0:T(8,128)(2,1)}, bf16[32,512]{1,0:T(8,128)(2,1)}, bf16[32,512]{1,0:T(8,128)(2,1)}) custom-call(f32[512,128]{1,0:T(8,128)S(1)} %get-tuple-element.19.refs_0_, bf16[1024,128]{1,0:T(8,128)(2,1)S(1)} %collective-permute-done.12.refs_1_, ...), custom_call_target="tpu_custom_call" | custom-call | tf_op jit(solution)/shard_map/finish/pallas_call | solution.py:299
  (8 shorter events, 0.1 us)
Async XLA Ops:
  1.9 0.9 %copy-start.4 = (bf16[1,1,32,2048]{3,2,1,0:T(8,128)(2,1)S(1)}, bf16[1,1,32,2048]{3,2,1,0:T(8,128)(2,1)}, u32[]{:S(2)}) copy-start(bf16[1,1,32,2048]{3,2,1,0:T(8,128)(2,1)} %param.9) | copy-start | bytes 393220
  2.8 0.9 %copy-start.5 = (bf16[1,1,32,2048]{3,2,1,0:T(8,128)(2,1)S(1)}, bf16[1,1,32,2048]{3,2,1,0:T(8,128)(2,1)}, u32[]{:S(2)}) copy-start(bf16[1,1,32,2048]{3,2,1,0:T(8,128)(2,1)} %param.10) | copy-start | bytes 393220
  3.7 2.4 %copy-start = (bf16[1,128,512]{2,1,0:T(8,128)(2,1)S(1)}, bf16[1,128,512]{2,1,0:T(8,128)(2,1)}, u32[]{:S(2)}) copy-start(bf16[1,128,512]{2,1,0:T(8,128)(2,1)} %param.13) | copy-start | bytes 393220
  3.7 10.9 %copy-start.1 = (bf16[1,128,512]{2,1,0:T(8,128)(2,1)S(1)}, bf16[1,128,512]{2,1,0:T(8,128)(2,1)}, u32[]{:S(2)}) copy-start(bf16[1,128,512]{2,1,0:T(8,128)(2,1)} %param.14) | copy-start | bytes 393220
  3.8 9.6 %collective-permute-start.1 = (bf16[1024,128]{1,0:T(8,128)(2,1)S(1)}, bf16[1024,128]{1,0:T(8,128)(2,1)S(1)}, u32[]{:S(2)}, u32[]{:S(2)}) collective-permute-start(bf16[1024,128]{1,0:T(8,128)(2,1)S(1)} %pack.1.refs_0_), channel_id=1, source_target_pairs={{0,8},{1,9},{2,10},{3,11},{4,12},{5,13},{6,14},{7,15},{8,0},{9,1},... | collective-permute-start | bytes 786440 | tf_op jit(solution)/shard_map/ppermute | solution.py:240
  6.1 8.5 %collective-permute-start.5 = (bf16[128,512]{1,0:T(8,128)(2,1)S(1)}, bf16[128,512]{1,0:T(8,128)(2,1)S(1)}, u32[]{:S(2)}, u32[]{:S(2)}) collective-permute-start(bf16[128,512]{1,0:T(8,128)(2,1)S(1)} %bitcast.22), channel_id=1, source_target_pairs={{0,6},{1,7},{2,4},{3,5},{4,2},{5,3},{6,0},{7,1},{8,14},{9,15},{10,... | collective-permute-start | bytes 393224 | tf_op jit(solution)/shard_map/ppermute | solution.py:240
  7.7 9.3 %collective-permute-start.4 = (bf16[128,512]{1,0:T(8,128)(2,1)S(1)}, bf16[128,512]{1,0:T(8,128)(2,1)S(1)}, u32[]{:S(2)}, u32[]{:S(2)}) collective-permute-start(bf16[128,512]{1,0:T(8,128)(2,1)S(1)} %bitcast.23), channel_id=1, source_target_pairs={{0,4},{1,5},{2,6},{3,7},{4,0},{5,1},{6,2},{7,3},{8,12},{9,13},{10,... | collective-permute-start | bytes 393224 | tf_op jit(solution)/shard_map/ppermute | solution.py:240
  8.3 8.9 %collective-permute-start.3 = (bf16[128,512]{1,0:T(8,128)(2,1)S(1)}, bf16[128,512]{1,0:T(8,128)(2,1)S(1)}, u32[]{:S(2)}, u32[]{:S(2)}) collective-permute-start(bf16[128,512]{1,0:T(8,128)(2,1)S(1)} %bitcast.24), channel_id=1, source_target_pairs={{0,2},{1,3},{2,0},{3,1},{4,6},{5,7},{6,4},{7,5},{8,10},{9,11},{10,... | collective-permute-start | bytes 393224 | tf_op jit(solution)/shard_map/ppermute | solution.py:240
  10.2 26.9 %collective-permute-start = (bf16[1024,128]{1,0:T(8,128)(2,1)S(1)}, bf16[1024,128]{1,0:T(8,128)(2,1)S(1)}, u32[]{:S(2)}, u32[]{:S(2)}) collective-permute-start(bf16[1024,128]{1,0:T(8,128)(2,1)S(1)} %pack.1.refs_0_), channel_id=1, source_target_pairs={{0,1},{1,0},{2,3},{3,2},{4,5},{5,4},{6,7},{7,6},{8,9},{9,8},{10,11... | collective-permute-start | bytes 786440 | tf_op jit(solution)/shard_map/ppermute | solution.py:240
  13.4 23.7 %collective-permute-start.2 = (bf16[1024,128]{1,0:T(8,128)(2,1)S(1)}, bf16[1024,128]{1,0:T(8,128)(2,1)S(1)}, u32[]{:S(2)}, u32[]{:S(2)}) collective-permute-start(bf16[1024,128]{1,0:T(8,128)(2,1)S(1)} %collective-permute-done.1.refs_2_), channel_id=1, source_target_pairs={{0,1},{1,0},{2,3},{3,2},{4,5},{5,4},{6,7},{7,6},{8,9},{9,8},{10,11... | collective-permute-start | bytes 786440 | tf_op jit(solution)/shard_map/ppermute | solution.py:240
  14.6 22.5 %collective-permute-start.8 = (bf16[128,512]{1,0:T(8,128)(2,1)S(1)}, bf16[128,512]{1,0:T(8,128)(2,1)S(1)}, u32[]{:S(2)}, u32[]{:S(2)}) collective-permute-start(bf16[128,512]{1,0:T(8,128)(2,1)S(1)} %bitcast.27), channel_id=1, source_target_pairs={{0,6},{1,7},{2,4},{3,5},{4,2},{5,3},{6,0},{7,1},{8,14},{9,15},{10,... | collective-permute-start | bytes 393224 | tf_op jit(solution)/shard_map/ppermute | solution.py:240
  16.9 20.2 %collective-permute-start.7 = (bf16[128,512]{1,0:T(8,128)(2,1)S(1)}, bf16[128,512]{1,0:T(8,128)(2,1)S(1)}, u32[]{:S(2)}, u32[]{:S(2)}) collective-permute-start(bf16[128,512]{1,0:T(8,128)(2,1)S(1)} %bitcast.28), channel_id=1, source_target_pairs={{0,4},{1,5},{2,6},{3,7},{4,0},{5,1},{6,2},{7,3},{8,12},{9,13},{10,... | collective-permute-start | bytes 393224 | tf_op jit(solution)/shard_map/ppermute | solution.py:240
  17.2 19.9 %collective-permute-start.6 = (bf16[128,512]{1,0:T(8,128)(2,1)S(1)}, bf16[128,512]{1,0:T(8,128)(2,1)S(1)}, u32[]{:S(2)}, u32[]{:S(2)}) collective-permute-start(bf16[128,512]{1,0:T(8,128)(2,1)S(1)} %bitcast.29), channel_id=1, source_target_pairs={{0,2},{1,3},{2,0},{3,1},{4,6},{5,7},{6,4},{7,5},{8,10},{9,11},{10,... | collective-permute-start | bytes 393224 | tf_op jit(solution)/shard_map/ppermute | solution.py:240
  18.7 18.4 %copy-start.2 = (bf16[1,1,32,512]{3,2,1,0:T(8,128)(2,1)S(1)}, bf16[1,1,32,512]{3,2,1,0:T(8,128)(2,1)}, u32[]{:S(2)}) copy-start(bf16[1,1,32,512]{3,2,1,0:T(8,128)(2,1)} %param.15) | copy-start | bytes 98308
  18.7 18.4 %copy-start.3 = (bf16[1,1,32,512]{3,2,1,0:T(8,128)(2,1)S(1)}, bf16[1,1,32,512]{3,2,1,0:T(8,128)(2,1)}, u32[]{:S(2)}) copy-start(bf16[1,1,32,512]{3,2,1,0:T(8,128)(2,1)} %param.16) | copy-start | bytes 98308
  19.3 17.1 %all-to-all-start = ((f32[16,1,1]{2,1,0:T(1,128)}), f32[16,1,1]{2,1,0:T(1,128)S(1)}, u32[]{:S(2)}, u32[]{:S(2)}) async-start(f32[16,1,1]{2,1,0:T(1,128)} %broadcast_in_dim.24), calls=%async_computation | async-start | bytes 16384 | tf_op jit(solution)/shard_map/all_to_all | solution.py:258
  40.2 4.9 %collective-permute-start.11 = (f32[56,128]{1,0:T(8,128)S(1)}, f32[56,128]{1,0:T(8,128)S(1)}, u32[]{:S(2)}, u32[]{:S(2)}) collective-permute-start(f32[56,128]{1,0:T(8,128)S(1)} %stats.1.refs_14_), channel_id=1, source_target_pairs={{0,9},{1,8},{2,11},{3,10},{4,13},{5,12},{6,15},{7,14},{8,1},{9,0},... | collective-permute-start | bytes 86024 | tf_op jit(solution)/shard_map/ppermute | solution.py:240
  40.3 5.5 %collective-permute-start.10 = (f32[56,128]{1,0:T(8,128)S(1)}, f32[56,128]{1,0:T(8,128)S(1)}, u32[]{:S(2)}, u32[]{:S(2)}) collective-permute-start(f32[56,128]{1,0:T(8,128)S(1)} %stats.1.refs_14_), channel_id=1, source_target_pairs={{0,8},{1,9},{2,10},{3,11},{4,12},{5,13},{6,14},{7,15},{8,0},{9,1},... | collective-permute-start | bytes 86024 | tf_op jit(solution)/shard_map/ppermute | solution.py:240
  41.9 3.9 %collective-permute-start.9 = (f32[56,128]{1,0:T(8,128)S(1)}, f32[56,128]{1,0:T(8,128)S(1)}, u32[]{:S(2)}, u32[]{:S(2)}) collective-permute-start(f32[56,128]{1,0:T(8,128)S(1)} %stats.1.refs_14_), channel_id=1, source_target_pairs={{0,1},{1,0},{2,3},{3,2},{4,5},{5,4},{6,7},{7,6},{8,9},{9,8},{10,11... | collective-permute-start | bytes 86024 | tf_op jit(solution)/shard_map/ppermute | solution.py:240
  49.6 5.4 %collective-permute-start.12 = (bf16[1024,128]{1,0:T(8,128)(2,1)S(1)}, bf16[1024,128]{1,0:T(8,128)(2,1)S(1)}, u32[]{:S(2)}, u32[]{:S(2)}) collective-permute-start(bf16[1024,128]{1,0:T(8,128)(2,1)S(1)} %get-tuple-element.20), channel_id=1, source_target_pairs={{0,1},{1,0},{2,3},{3,2},{4,5},{5,4},{6,7},{7,6},{8,9},{9,8},{10,11... | collective-permute-start | bytes 786440 | tf_op jit(solution)/shard_map/ppermute | solution.py:240
  50.3 9.2 %collective-permute-start.14 = (bf16[1040,128]{1,0:T(8,128)(2,1)S(1)}, bf16[1040,128]{1,0:T(8,128)(2,1)S(1)}, u32[]{:S(2)}, u32[]{:S(2)}) collective-permute-start(bf16[1040,128]{1,0:T(8,128)(2,1)S(1)} %get-tuple-element.23), channel_id=1, source_target_pairs={{0,2},{1,3},{2,0},{3,1},{4,6},{5,7},{6,4},{7,5},{8,10},{9,11},{10,... | collective-permute-start | bytes 798728 | tf_op jit(solution)/shard_map/ppermute | solution.py:240
  51.5 15.6 %collective-permute-start.15 = (bf16[1040,128]{1,0:T(8,128)(2,1)S(1)}, bf16[1040,128]{1,0:T(8,128)(2,1)S(1)}, u32[]{:S(2)}, u32[]{:S(2)}) collective-permute-start(bf16[1040,128]{1,0:T(8,128)(2,1)S(1)} %get-tuple-element.24), channel_id=1, source_target_pairs={{0,4},{1,5},{2,6},{3,7},{4,0},{5,1},{6,2},{7,3},{8,12},{9,13},{10,... | collective-permute-start | bytes 798728 | tf_op jit(solution)/shard_map/ppermute | solution.py:240
  54.9 14.8 %collective-permute-start.16 = (bf16[1040,128]{1,0:T(8,128)(2,1)S(1)}, bf16[1040,128]{1,0:T(8,128)(2,1)S(1)}, u32[]{:S(2)}, u32[]{:S(2)}) collective-permute-start(bf16[1040,128]{1,0:T(8,128)(2,1)S(1)} %get-tuple-element.25), channel_id=1, source_target_pairs={{0,6},{1,7},{2,4},{3,5},{4,2},{5,3},{6,0},{7,1},{8,14},{9,15},{10,... | collective-permute-start | bytes 798728 | tf_op jit(solution)/shard_map/ppermute | solution.py:240
  55.0 14.7 %collective-permute-start.13 = (bf16[512,128]{1,0:T(8,128)(2,1)S(1)}, bf16[512,128]{1,0:T(8,128)(2,1)S(1)}, u32[]{:S(2)}, u32[]{:S(2)}) collective-permute-start(bf16[512,128]{1,0:T(8,128)(2,1)S(1)} %add_convert_fusion), channel_id=1, source_target_pairs={{0,8},{1,9},{2,10},{3,11},{4,12},{5,13},{6,14},{7,15},{8,0},{9,1},... | collective-permute-start | bytes 393224 | tf_op jit(solution)/shard_map/ppermute | solution.py:240

commit v2 on v1

--- a/solution.py
+++ b/solution.py
@@ -19,25 +19,19 @@
     return lax.dot_general(a, b, dims, preferred_element_type=jnp.float32)
 
 
-def pack_kernel(len_ref, adv_ref, q_ref, g_ref, out_ref):
-    tokens, width = q_ref.shape
-    heads = width // HD
-    at = lax.broadcasted_iota(jnp.int32, (tokens, HD), 0)
-    weight = jnp.where(at < len_ref[0], adv_ref[0], 0.0)
-    for h in range(heads):
-        cols = slice(h * HD, (h + 1) * HD)
-        out_ref[h * tokens : (h + 1) * tokens, :] = q_ref[:, cols]
-        out_ref[(heads + h) * tokens : (heads + h + 1) * tokens, :] = (
-            g_ref[:, cols].astype(jnp.float32) * weight
-        ).astype(jnp.bfloat16)
-
-
-def rows_of(refs, start, size):
-    return jnp.concatenate([r[start : start + size, :] for r in refs], axis=0)
-
-
-def cols_of(refs, g):
-    return jnp.concatenate([r[:, g * HD : (g + 1) * HD] for r in refs], axis=0)
+def rows_of(refs, kind, g):
+    tokens = refs[0].shape[0] // 2
+    rows = slice(kind * tokens, (kind + 1) * tokens)
+    return jnp.concatenate(
+        [r[rows, h * HD : (h + 1) * HD] for r in refs for h in range(4 * g, 4 * g + 4)], axis=0
+    )
+
+
+def cols_of(refs, start, g):
+    size = (refs[0].shape[0] - 16) // 2
+    return jnp.concatenate(
+        [r[start * size : (start + 1) * size, g * HD : (g + 1) * HD] for r in refs], axis=0
+    )
 
 
 def key_bias(info_ref, block):
@@ -57,26 +51,26 @@
     return u <= t
 
 
-def stats_kernel(to_log2, info_ref, tot_ref, *refs):
-    qg, ks, vs = refs[0:4], refs[4:8], refs[8:12]
-    ok_ref, ov_ref, out_ref = refs[12:15]
-    block = ks[0].shape[0]
-    groups = ks[0].shape[1] // HD
-    tokens = ok_ref.shape[0]
-    all_rows = qg[0].shape[0] // 2
-    rows = all_rows // groups
+def stats_kernel(to_log2, info_ref, *refs):
+    qg, kvs, own_ref, out_ref = refs[0:4], refs[4:8], refs[8], refs[9]
+    block = (kvs[0].shape[0] - 16) // 2
+    groups = kvs[0].shape[1] // HD
+    tokens = own_ref.shape[0] // 2
+    rows = qg[0].shape[1] // HD // groups * tokens
     bias = key_bias(info_ref, block)
     causal = own_mask(tokens, rows)
-    out_ref[48:56, :] = jnp.zeros((8, HD), jnp.float32) + tot_ref[0]
+    out_ref[48:56, :] = sum(
+        r[2 * block : 2 * block + 16, :HD].astype(jnp.float32)[:8] for r in kvs
+    )
     for g in range(groups):
-        q = rows_of(qg, g * rows, rows)
-        w = rows_of(qg, all_rows + g * rows, rows)
-        score = dot(cols_of(ks, g), q, NT) * to_log2 + bias
-        slope = dot(cols_of(vs, g), w, NT)
+        q = rows_of(qg, 0, g)
+        w = rows_of(qg, 1, g)
+        score = dot(cols_of(kvs, 0, g), q, NT) * to_log2 + bias
+        slope = dot(cols_of(kvs, 1, g), w, NT)
         own_cols = slice(g * HD, (g + 1) * HD)
-        own_score = dot(ok_ref[:, own_cols], q[:rows], NT) * to_log2
+        own_score = dot(own_ref[:tokens, own_cols], q[:rows], NT) * to_log2
         own_score = jnp.where(causal, own_score, MASKED)
-        own_slope = dot(ov_ref[:, own_cols], w[:rows], NT)
+        own_slope = dot(own_ref[tokens:, own_cols], w[:rows], NT)
         top = jnp.max(score, axis=0, keepdims=True)
         own_top = jnp.maximum(
             top[:, :rows], jnp.max(own_score, axis=0, keepdims=True)
@@ -98,17 +92,15 @@
 
 
 def grads_kernel(to_log2, info_ref, *refs):
-    qg, ks, vs = refs[0:4], refs[4:8], refs[8:12]
-    ok_ref, ov_ref = refs[12:14]
-    stats = refs[14:18]
-    dq_own, dq_far, dq_sib, dkv_own = refs[18:22]
-    dkv_out = refs[22:25]
-    own_out, tot_out = refs[25:27]
-    block = ks[0].shape[0]
-    groups = ks[0].shape[1] // HD
-    tokens = ok_ref.shape[0]
-    all_rows = qg[0].shape[0] // 2
-    rows = all_rows // groups
+    qg, kvs, own_ref = refs[0:4], refs[4:8], refs[8]
+    stats = refs[9:13]
+    dq_own, dq_far, dq_sib, dkv_own = refs[13:17]
+    dkv_out = refs[17:20]
+    own_out, tot_out = refs[20:22]
+    block = (kvs[0].shape[0] - 16) // 2
+    groups = kvs[0].shape[1] // HD
+    tokens = own_ref.shape[0] // 2
+    rows = qg[0].shape[1] // HD // groups * tokens
     bias = key_bias(info_ref, block)
     causal = own_mask(tokens, rows)
     shifts, means = [], []
@@ -125,30 +117,26 @@
         means.append(mixed / total)
     shift = jnp.concatenate(shifts, axis=1)
     mean = jnp.concatenate(means, axis=1)
-    count = sum(stats[e][48:56, :] for e in range(4))
-    tot_out[...] = count
-    high = jnp.floor(count * (1.0 / 256.0))
-    marks = jnp.concatenate([high, count - high * 256.0], axis=0).astype(jnp.bfloat16)
     half = groups * block
-    for ref in dkv_out:
-        ref[2 * half : 2 * half + 16, :] = marks
+    for i in range(tot_out.shape[0]):
+        tot_out[i] = sum(stats[e][48:49, :] for e in range(4))
     for g in range(groups):
-        q = rows_of(qg, g * rows, rows)
-        w = rows_of(qg, all_rows + g * rows, rows)
-        k = cols_of(ks, g)
+        q = rows_of(qg, 0, g)
+        w = rows_of(qg, 1, g)
+        k = cols_of(kvs, 0, g)
         sh, mn = shift[g : g + 1, :], mean[g : g + 1, :]
         score = dot(k, q, NT) * to_log2 + bias
-        slope = dot(cols_of(vs, g), w, NT)
+        slope = dot(cols_of(kvs, 1, g), w, NT)
         p = jnp.exp2(score - sh)
         ds = (p * (slope - mn)).astype(jnp.bfloat16)
         dv = dot(p.astype(jnp.bfloat16), w, NN)
         dk = dot(ds, q, NN)
         dq = dot(k.T, ds, NN)
         own_cols = slice(g * HD, (g + 1) * HD)
-        own_k = ok_ref[:, own_cols]
+        own_k = own_ref[:tokens, own_cols]
         own_score = dot(own_k, q[:rows], NT) * to_log2
         own_score = jnp.where(causal, own_score, MASKED)
-        own_slope = dot(ov_ref[:, own_cols], w[:rows], NT)
+        own_slope = dot(own_ref[tokens:, own_cols], w[:rows], NT)
         own_p = jnp.exp2(own_score - sh[:, :rows])
         own_ds = (own_p * (own_slope - mn[:, :rows])).astype(jnp.bfloat16)
         own_out[:tokens, own_cols] = dot(own_ds, q[:rows], NN)
@@ -183,10 +171,7 @@
     per_group = q_out.shape[1] // HD // groups
     half = groups * block
     f32 = jnp.float32
-    count = tot_ref[...]
-    for r in (r1, r2, r3):
-        marks = r[2 * half : 2 * half + 16, :].astype(f32)
-        count = count + marks[:8] * 256.0 + marks[8:]
+    count = functools.reduce(jnp.add, [tot_ref[i] for i in range(tot_ref.shape[0])])
     scale = loss_top / count[:1, :]
     key_scale = scale * softmax_scale
     for g in range(groups):
@@ -239,41 +224,28 @@
     def swap(array, mask):
         return lax.ppermute(array, "sample", [(i, i ^ mask) for i in range(samples)])
 
-    k0, v0 = prefix_keys[0], prefix_values[0]
-    ks = [k0] + [swap(k0, 2 * e) for e in (1, 2, 3)]
-    vs = [v0] + [swap(v0, 2 * e) for e in (1, 2, 3)]
-    all_rows = width // HD * tokens
-    qg0 = pl.pallas_call(
-        pack_kernel,
-        out_shape=shape((2 * all_rows, HD), bf16),
-        in_specs=[smem, smem, vmem, vmem],
-        out_specs=vmem,
-        compiler_params=params,
-        name="pack",
-    )(comp_len[0], advantage[0], queries[0, 0], out_grad[0, 0])
+    at = lax.broadcasted_iota(jnp.int32, (tokens, width), 0)
+    weight = jnp.where(at < comp_len[0, 0], advantage[0, 0], 0.0)
+    weighted = (out_grad[0, 0].astype(f32) * weight).astype(bf16)
+    mark = jnp.broadcast_to(comp_len.astype(bf16), (16, kv_width))
+    kv0 = jnp.concatenate([prefix_keys[0], prefix_values[0], mark], axis=0)
+    qg0 = jnp.concatenate([queries[0, 0], weighted], axis=0)
+    own = jnp.concatenate([own_keys[0, 0], own_values[0, 0]], axis=0)
+    qg2 = swap(qg0, 8)
+    kv = [kv0] + [swap(kv0, 2 * e) for e in (1, 2, 3)]
     qg1 = swap(qg0, 1)
-    qg2 = swap(qg0, 8)
     qg3 = swap(qg2, 1)
     qg = [qg0, qg1, qg2, qg3]
-    counts = lax.all_to_all(
-        jnp.broadcast_to(comp_len[0].astype(f32)[None], (prompts, 1)),
-        "prompt",
-        0,
-        0,
-        tiled=True,
-    )
-    count = jnp.sum(counts, axis=0)
     me = lax.axis_index("sample")
     info = jnp.stack([prompt_len[0]] + [me ^ (2 * e) for e in range(4)]).astype(jnp.int32)
-    own_k, own_v = own_keys[0, 0], own_values[0, 0]
     stats0 = pl.pallas_call(
         functools.partial(stats_kernel, to_log2),
         out_shape=shape((56, HD), f32),
-        in_specs=[smem, smem] + [vmem] * 14,
+        in_specs=[smem] + [vmem] * 9,
         out_specs=vmem,
         compiler_params=params,
         name="stats",
-    )(info, count, *qg, *ks, *vs, own_k, own_v)
+    )(info, *qg, *kv, own)
     stats = [stats0, swap(stats0, 1), swap(stats0, 8), swap(stats0, 9)]
     kv_rows = 2 * groups * block
     dq_rows = width // HD // 4 * HD
@@ -285,16 +257,17 @@
             shape((2 * dq_rows, HD), bf16),
             shape((kv_rows, HD), f32),
         ]
-        + [shape((kv_rows + 16, HD), bf16)] * 3
-        + [shape((2 * tokens, kv_width), f32), shape((8, HD), f32)],
-        in_specs=[smem] + [vmem] * 18,
+        + [shape((kv_rows, HD), bf16)] * 3
+        + [shape((2 * tokens, kv_width), f32), shape((prompts, 1, HD), f32)],
+        in_specs=[smem] + [vmem] * 13,
         out_specs=[vmem] * 9,
         compiler_params=params,
         name="grads",
-    )(info, *qg, *ks, *vs, own_k, own_v, *stats)
+    )(info, *qg, *kv, own, *stats)
     dq_own, dq_far, dq_sib, dkv_own = outs[:4]
     dq_core = swap(dq_sib, 1)
     dq_x = swap((dq_far + dq_core[dq_rows:].astype(f32)).astype(bf16), 8)
+    total = lax.all_to_all(outs[8], "prompt", 0, 0, tiled=True)
     received = [swap(outs[3 + e], 2 * e) for e in (1, 2, 3)]
     q_out, k_out, v_out, ok_out, ov_out = pl.pallas_call(
         functools.partial(finish_kernel, loss_top, softmax_scale),
@@ -309,7 +282,7 @@
         out_specs=[vmem] * 5,
         compiler_params=params,
         name="finish",
-    )(dq_own, dq_core, dq_x, dkv_own, *received, outs[7], outs[8])
+    )(dq_own, dq_core, dq_x, dkv_own, *received, outs[7], total)
     return (q_out[None, None], k_out[None], v_out[None], ok_out[None, None], ov_out[None, None])
 
 

time: 71.9 us -> 59.5 us (0.83)
  blocking collectives: 0 us -> 17.4 us
  waiting for transfers between devices: 26.8 us -> 12.7 us
  starting transfers between devices: 30.1 us -> 17.1 us
  local copies, waits for them, and re-layouts: 2.5 us -> 0.13 us
    all_to_all x0 -> x1, blocking collectives: none -> 17.4 us  [per_device(): total = lax.all_to_all(outs[8], 'prompt', 0, 0, tiled=True)]
    all_to_all x1 -> x0, starting transfers between devices: 8.72 us -> none  [per_device(): lax.all_to_all(jnp.broadcast_to(comp_len[0].astype(f32)[None], (prompts,...]
    all_to_all x1 -> x0, waiting for transfers between devices: 7.68 us -> none  [per_device(): lax.all_to_all(jnp.broadcast_to(comp_len[0].astype(f32)[None], (prompts,...]
    ppermute x17 -> x14, waiting for transfers between devices: 19.1 us -> 12.7 us  [swap(): lax.ppermute(array, 'sample', [(i, i ^ mask) for i in range(samples)])]
    ppermute x17 -> x14, starting transfers between devices: 21.4 us -> 17.1 us  [swap(): lax.ppermute(array, 'sample', [(i, i ^ mask) for i in range(samples)])]
    unnamed x12 -> x10, local copies, waits for them, and re-layouts: 1.82 us -> 0.03 us
    convert_element_type x0 -> x1, other arithmetic: none -> 1.03 us  [per_device(): weighted = (out_grad[0, 0].astype(f32) * weight).astype(bf16)]
  transfers between devices with their start and end apart: 18 -> 14, of which waited for: 8 -> 5; matrix products, arithmetic and copies ran while one was open for 2% -> 0% of each run, Pallas kernels for 0% -> 0%
where the time goes in v2:
time: 59.5 us; the launch traced here: 58.5 us
  blocking collectives  17.4 us (29%)
  starting transfers between devices  17.1 us (29%)
  waiting for transfers between devices  12.7 us (21%)
  Pallas kernels  7.24 us (12%)
  between operations  2.71 us (5%)
  other arithmetic  1.2 us (2%)
    all_to_all x1, blocking collectives, per_device(): total = lax.all_to_all(outs[8], 'prompt', 0, 0, tiled=True)  17.4 us
    ppermute x14, starting transfers between devices, swap(): lax.ppermute(array, 'sample', [(i, i ^ mask) for i in range(samples)])  17.1 us
    ppermute x14, waiting for transfers between devices, swap(): lax.ppermute(array, 'sample', [(i, i ^ mask) for i in range(samples)])  12.7 us
    pallas_call x1, Pallas kernels, per_device(): pl.pallas_call(functools.partial(grads_kernel, to_log2), out_shape=[shape...  3.92 us
    pallas_call x1, Pallas kernels, per_device(): pl.pallas_call(functools.partial(stats_kernel, to_log2), out_shape=shape(...  2.41 us
  transfers between devices with their start and end apart: 14, of which 5 were waited for; matrix products, arithmetic and copies ran while one was open for 0% of the time, Pallas kernels for 0%

profile of v2, /device:TPU:4, one launch (start us, length us, event | category | flops | bytes accessed | tf_op | source)
XLA Modules:
  0.0 58.5 jit_solution(1637180828239960893)
XLA Ops:
  1.9 0.0 copy-start
  1.9 1.0 %fusion = bf16[32,2048]{1,0:T(8,128)(2,1)S(1)} fusion(bf16[1,1,32,2048]{3,2,1,0:T(8,128)(2,1)} %param.10, f32[32]{0:T(128)S(1)} %compare_select_fusion), kind=kLoop, calls=%fused_computation.3 | loop fusion | flops 196608 | bytes 262272 | tf_op jit(solution)/shard_map/convert_element_type | solution.py:229
  3.0 0.0 copy-done
  3.0 0.0 copy-start.1
  3.0 0.0 copy-start.2
  3.0 2.3 %collective-permute-start.1 = (bf16[64,2048]{1,0:T(8,128)(2,1)S(1)}, bf16[64,2048]{1,0:T(8,128)(2,1)S(1)}, u32[]{:S(2)}, u32[]{:S(2)}) collective-permute-start(bf16[64,2048]{1,0:T(8,128)(2,1)S(1)} %pad_maximum_fusion.refs_0_), channel_id=1, source_target_pairs={{0,8},{1,9},{2,10},{3,11},{4,12},{5,13},{6,14},{7,15},{8,0},{9,1},... | collective-permute-start | bytes 786440 | tf_op jit(solution)/shard_map/ppermute | solution.py:225
  5.4 0.0 copy-done.1
  5.4 0.0 copy-done.2
  5.4 0.0 copy-start.3
  5.4 0.0 copy-start.4
  5.4 0.1 maximum_maximum_fusion.refs_4_
  5.5 1.6 %collective-permute-start.5 = (bf16[272,512]{1,0:T(8,128)(2,1)S(1)}, bf16[272,512]{1,0:T(8,128)(2,1)S(1)}, u32[]{:S(2)}, u32[]{:S(2)}) collective-permute-start(bf16[272,512]{1,0:T(8,128)(2,1)S(1)} %maximum_maximum_fusion.refs_4_), channel_id=1, source_target_pairs={{0,6},{1,7},{2,4},{3,5},{4,2},{5,3},{6,0},{7,1},{8,14},{9,15},{10,... | collective-permute-start | bytes 835592 | tf_op jit(solution)/shard_map/ppermute | solution.py:225
  7.2 0.6 %collective-permute-start.4 = (bf16[272,512]{1,0:T(8,128)(2,1)S(1)}, bf16[272,512]{1,0:T(8,128)(2,1)S(1)}, u32[]{:S(2)}, u32[]{:S(2)}) collective-permute-start(bf16[272,512]{1,0:T(8,128)(2,1)S(1)} %maximum_maximum_fusion.refs_4_), channel_id=1, source_target_pairs={{0,4},{1,5},{2,6},{3,7},{4,0},{5,1},{6,2},{7,3},{8,12},{9,13},{10,... | collective-permute-start | bytes 835592 | tf_op jit(solution)/shard_map/ppermute | solution.py:225
  7.8 1.9 %collective-permute-start.3 = (bf16[272,512]{1,0:T(8,128)(2,1)S(1)}, bf16[272,512]{1,0:T(8,128)(2,1)S(1)}, u32[]{:S(2)}, u32[]{:S(2)}) collective-permute-start(bf16[272,512]{1,0:T(8,128)(2,1)S(1)} %maximum_maximum_fusion.refs_4_), channel_id=1, source_target_pairs={{0,2},{1,3},{2,0},{3,1},{4,6},{5,7},{6,4},{7,5},{8,10},{9,11},{10,... | collective-permute-start | bytes 835592 | tf_op jit(solution)/shard_map/ppermute | solution.py:225
  9.7 0.0 collective-permute-start
  9.7 3.0 %collective-permute-done.1.refs_2_ = bf16[64,2048]{1,0:T(8,128)(2,1)S(1)} collective-permute-done((bf16[64,2048]{1,0:T(8,128)(2,1)S(1)}, bf16[64,2048]{1,0:T(8,128)(2,1)S(1)}, u32[]{:S(2)}, u32[]{:S(2)}) %collective-permute-start.1) | collective-permute-done | bytes 262176 | tf_op jit(solution)/shard_map/ppermute | solution.py:225
  12.7 0.0 collective-permute-start.2
  13.3 0.1 stack.19.info_ref
  13.4 0.0 copy-done.3
  13.4 0.0 copy-done.4
  13.4 0.0 collective-permute-done.refs_1_
  13.4 6.4 %collective-permute-done.5.refs_7_ = bf16[272,512]{1,0:T(8,128)(2,1)S(1)} collective-permute-done((bf16[272,512]{1,0:T(8,128)(2,1)S(1)}, bf16[272,512]{1,0:T(8,128)(2,1)S(1)}, u32[]{:S(2)}, u32[]{:S(2)}) %collective-permute-start.5) | collective-permute-done | bytes 278560 | tf_op jit(solution)/shard_map/ppermute | solution.py:225
  19.8 0.0 collective-permute-done.4.refs_6_
  19.8 0.7 %collective-permute-done.3.refs_5_ = bf16[272,512]{1,0:T(8,128)(2,1)S(1)} collective-permute-done((bf16[272,512]{1,0:T(8,128)(2,1)S(1)}, bf16[272,512]{1,0:T(8,128)(2,1)S(1)}, u32[]{:S(2)}, u32[]{:S(2)}) %collective-permute-start.3) | collective-permute-done | bytes 278560 | tf_op jit(solution)/shard_map/ppermute | solution.py:225
  20.5 0.0 collective-permute-done.2.refs_3_
  20.5 2.4 %stats.1.refs_9_ = f32[56,128]{1,0:T(8,128)S(1)} custom-call(s32[5]{0:T(128)S(1)} %stack.19.info_ref, bf16[64,2048]{1,0:T(8,128)(2,1)S(1)} %pad_maximum_fusion.refs_0_, bf16[64,2048]{1,0:T(8,128)(2,1)S(1)} %collective-permute-done.refs_1_, bf16[64,2048]{1,0:T(8,128)(2,1)S(1)} %collective-permute-done.1.refs_2_, ...), custom_call_target="tpu_custom_call" | custom-call | tf_op jit(solution)/shard_map/stats/pallas_call | solution.py:241
  22.9 0.7 %collective-permute-start.8 = (f32[56,128]{1,0:T(8,128)S(1)}, f32[56,128]{1,0:T(8,128)S(1)}, u32[]{:S(2)}, u32[]{:S(2)}) collective-permute-start(f32[56,128]{1,0:T(8,128)S(1)} %stats.1.refs_9_), channel_id=1, source_target_pairs={{0,9},{1,8},{2,11},{3,10},{4,13},{5,12},{6,15},{7,14},{8,1},{9,0},... | collective-permute-start | bytes 86024 | tf_op jit(solution)/shard_map/ppermute | solution.py:225
  23.7 1.9 %collective-permute-start.7 = (f32[56,128]{1,0:T(8,128)S(1)}, f32[56,128]{1,0:T(8,128)S(1)}, u32[]{:S(2)}, u32[]{:S(2)}) collective-permute-start(f32[56,128]{1,0:T(8,128)S(1)} %stats.1.refs_9_), channel_id=1, source_target_pairs={{0,8},{1,9},{2,10},{3,11},{4,12},{5,13},{6,14},{7,15},{8,0},{9,1},... | collective-permute-start | bytes 86024 | tf_op jit(solution)/shard_map/ppermute | solution.py:225
  25.6 0.8 %collective-permute-start.6 = (f32[56,128]{1,0:T(8,128)S(1)}, f32[56,128]{1,0:T(8,128)S(1)}, u32[]{:S(2)}, u32[]{:S(2)}) collective-permute-start(f32[56,128]{1,0:T(8,128)S(1)} %stats.1.refs_9_), channel_id=1, source_target_pairs={{0,1},{1,0},{2,3},{3,2},{4,5},{5,4},{6,7},{7,6},{8,9},{9,8},{10,11... | collective-permute-start | bytes 86024 | tf_op jit(solution)/shard_map/ppermute | solution.py:225
  26.4 1.4 %collective-permute-done.8.refs_12_ = f32[56,128]{1,0:T(8,128)S(1)} collective-permute-done((f32[56,128]{1,0:T(8,128)S(1)}, f32[56,128]{1,0:T(8,128)S(1)}, u32[]{:S(2)}, u32[]{:S(2)}) %collective-permute-start.8) | collective-permute-done | bytes 28704 | tf_op jit(solution)/shard_map/ppermute | solution.py:225
  27.8 1.2 %collective-permute-done.7.refs_11_ = f32[56,128]{1,0:T(8,128)S(1)} collective-permute-done((f32[56,128]{1,0:T(8,128)S(1)}, f32[56,128]{1,0:T(8,128)S(1)}, u32[]{:S(2)}, u32[]{:S(2)}) %collective-permute-start.7) | collective-permute-done | bytes 28704 | tf_op jit(solution)/shard_map/ppermute | solution.py:225
  29.0 0.0 collective-permute-done.6.refs_10_
  29.0 3.9 %grads.1 = (f32[512,128]{1,0:T(8,128)S(1)}, f32[512,128]{1,0:T(8,128)S(1)}, bf16[1024,128]{1,0:T(8,128)(2,1)S(1)}, f32[1024,128]{1,0:T(8,128)S(1)}, bf16[1024,12...) custom-call(s32[5]{0:T(128)S(1)} %stack.19.info_ref, ...), custom_call_target="tpu_custom_call" | custom-call | tf_op jit(solution)/shard_map/grads/pallas_call | solution.py:252
  33.0 0.9 %collective-permute-start.9 = (bf16[1024,128]{1,0:T(8,128)(2,1)S(1)}, bf16[1024,128]{1,0:T(8,128)(2,1)S(1)}, u32[]{:S(2)}, u32[]{:S(2)}) collective-permute-start(bf16[1024,128]{1,0:T(8,128)(2,1)S(1)} %get-tuple-element.20), channel_id=1, source_target_pairs={{0,1},{1,0},{2,3},{3,2},{4,5},{5,4},{6,7},{7,6},{8,9},{9,8},{10,11... | collective-permute-start | bytes 786440 | tf_op jit(solution)/shard_map/ppermute | solution.py:225
  33.8 1.4 %collective-permute-start.11 = (bf16[1024,128]{1,0:T(8,128)(2,1)S(1)}, bf16[1024,128]{1,0:T(8,128)(2,1)S(1)}, u32[]{:S(2)}, u32[]{:S(2)}) collective-permute-start(bf16[1024,128]{1,0:T(8,128)(2,1)S(1)} %get-tuple-element.23), channel_id=1, source_target_pairs={{0,2},{1,3},{2,0},{3,1},{4,6},{5,7},{6,4},{7,5},{8,10},{9,11},{10,... | collective-permute-start | bytes 786440 | tf_op jit(solution)/shard_map/ppermute | solution.py:225
  35.3 2.9 %collective-permute-start.12 = (bf16[1024,128]{1,0:T(8,128)(2,1)S(1)}, bf16[1024,128]{1,0:T(8,128)(2,1)S(1)}, u32[]{:S(2)}, u32[]{:S(2)}) collective-permute-start(bf16[1024,128]{1,0:T(8,128)(2,1)S(1)} %get-tuple-element.24), channel_id=1, source_target_pairs={{0,4},{1,5},{2,6},{3,7},{4,0},{5,1},{6,2},{7,3},{8,12},{9,13},{10,... | collective-permute-start | bytes 786440 | tf_op jit(solution)/shard_map/ppermute | solution.py:225
  38.2 0.4 collective-permute-start.13
  38.5 0.0 collective-permute-done.9.refs_1_
  38.6 1.6 %collective-permute-start.10 = (bf16[512,128]{1,0:T(8,128)(2,1)S(1)}, bf16[512,128]{1,0:T(8,128)(2,1)S(1)}, u32[]{:S(2)}, u32[]{:S(2)}) collective-permute-start(bf16[512,128]{1,0:T(8,128)(2,1)S(1)} %add_convert_fusion), channel_id=1, source_target_pairs={{0,8},{1,9},{2,10},{3,11},{4,12},{5,13},{6,14},{7,15},{8,0},{9,1},... | collective-permute-start | bytes 393224 | tf_op jit(solution)/shard_map/ppermute | solution.py:225
  40.2 17.4 %all_to_all.5.refs_8_ = f32[16,1,128]{2,1,0:T(1,128)S(1)} all-to-all(f32[16,1,128]{2,1,0:T(1,128)S(1)} %get-tuple-element.27), channel_id=1, replica_groups=mesh['prompt'=16,'sample'=16] {'prompt'}, dimensions={0} | all-to-all | bytes 16384 | tf_op jit(solution)/shard_map/all_to_all | solution.py:270
  57.6 0.0 collective-permute-done.11.refs_4_
  57.6 0.0 collective-permute-done.12.refs_5_
  57.6 0.0 collective-permute-done.13.refs_6_
  57.6 0.0 collective-permute-done.10.refs_2_
  57.6 0.9 %finish.1 = (bf16[32,2048]{1,0:T(8,128)(2,1)}, bf16[128,512]{1,0:T(8,128)(2,1)}, bf16[128,512]{1,0:T(8,128)(2,1)}, bf16[32,512]{1,0:T(8,128)(2,1)}, bf16[32,512]{1,0:T(8,128)(2,1)}) custom-call(f32[512,128]{1,0:T(8,128)S(1)} %get-tuple-element.19.refs_0_, bf16[1024,128]{1,0:T(8,128)(2,1)S(1)} %collective-permute-done.9.refs_1_, ...), custom_call_target="tpu_custom_call" | custom-call | tf_op jit(solution)/shard_map/finish/pallas_call | solution.py:272
  (6 shorter events, 0.1 us)
Async XLA Ops:
  1.9 1.0 %copy-start = (bf16[1,1,32,2048]{3,2,1,0:T(8,128)(2,1)S(1)}, bf16[1,1,32,2048]{3,2,1,0:T(8,128)(2,1)}, u32[]{:S(2)}) copy-start(bf16[1,1,32,2048]{3,2,1,0:T(8,128)(2,1)} %param.9) | copy-start | bytes 393220
  3.0 2.4 %copy-start.1 = (bf16[1,128,512]{2,1,0:T(8,128)(2,1)S(1)}, bf16[1,128,512]{2,1,0:T(8,128)(2,1)}, u32[]{:S(2)}) copy-start(bf16[1,128,512]{2,1,0:T(8,128)(2,1)} %param.14) | copy-start | bytes 393220
  3.0 2.4 %copy-start.2 = (bf16[1,128,512]{2,1,0:T(8,128)(2,1)S(1)}, bf16[1,128,512]{2,1,0:T(8,128)(2,1)}, u32[]{:S(2)}) copy-start(bf16[1,128,512]{2,1,0:T(8,128)(2,1)} %param.13) | copy-start | bytes 393220
  3.0 9.6 %collective-permute-start.1 = (bf16[64,2048]{1,0:T(8,128)(2,1)S(1)}, bf16[64,2048]{1,0:T(8,128)(2,1)S(1)}, u32[]{:S(2)}, u32[]{:S(2)}) collective-permute-start(bf16[64,2048]{1,0:T(8,128)(2,1)S(1)} %pad_maximum_fusion.refs_0_), channel_id=1, source_target_pairs={{0,8},{1,9},{2,10},{3,11},{4,12},{5,13},{6,14},{7,15},{8,0},{9,1},... | collective-permute-start | bytes 786440 | tf_op jit(solution)/shard_map/ppermute | solution.py:225
  5.4 8.0 %copy-start.3 = (bf16[1,1,32,512]{3,2,1,0:T(8,128)(2,1)S(1)}, bf16[1,1,32,512]{3,2,1,0:T(8,128)(2,1)}, u32[]{:S(2)}) copy-start(bf16[1,1,32,512]{3,2,1,0:T(8,128)(2,1)} %param.16) | copy-start | bytes 98308
  5.4 8.0 %copy-start.4 = (bf16[1,1,32,512]{3,2,1,0:T(8,128)(2,1)S(1)}, bf16[1,1,32,512]{3,2,1,0:T(8,128)(2,1)}, u32[]{:S(2)}) copy-start(bf16[1,1,32,512]{3,2,1,0:T(8,128)(2,1)} %param.15) | copy-start | bytes 98308
  5.5 14.3 %collective-permute-start.5 = (bf16[272,512]{1,0:T(8,128)(2,1)S(1)}, bf16[272,512]{1,0:T(8,128)(2,1)S(1)}, u32[]{:S(2)}, u32[]{:S(2)}) collective-permute-start(bf16[272,512]{1,0:T(8,128)(2,1)S(1)} %maximum_maximum_fusion.refs_4_), channel_id=1, source_target_pairs={{0,6},{1,7},{2,4},{3,5},{4,2},{5,3},{6,0},{7,1},{8,14},{9,15},{10,... | collective-permute-start | bytes 835592 | tf_op jit(solution)/shard_map/ppermute | solution.py:225
  7.2 12.6 %collective-permute-start.4 = (bf16[272,512]{1,0:T(8,128)(2,1)S(1)}, bf16[272,512]{1,0:T(8,128)(2,1)S(1)}, u32[]{:S(2)}, u32[]{:S(2)}) collective-permute-start(bf16[272,512]{1,0:T(8,128)(2,1)S(1)} %maximum_maximum_fusion.refs_4_), channel_id=1, source_target_pairs={{0,4},{1,5},{2,6},{3,7},{4,0},{5,1},{6,2},{7,3},{8,12},{9,13},{10,... | collective-permute-start | bytes 835592 | tf_op jit(solution)/shard_map/ppermute | solution.py:225
  7.8 12.7 %collective-permute-start.3 = (bf16[272,512]{1,0:T(8,128)(2,1)S(1)}, bf16[272,512]{1,0:T(8,128)(2,1)S(1)}, u32[]{:S(2)}, u32[]{:S(2)}) collective-permute-start(bf16[272,512]{1,0:T(8,128)(2,1)S(1)} %maximum_maximum_fusion.refs_4_), channel_id=1, source_target_pairs={{0,2},{1,3},{2,0},{3,1},{4,6},{5,7},{6,4},{7,5},{8,10},{9,11},{10,... | collective-permute-start | bytes 835592 | tf_op jit(solution)/shard_map/ppermute | solution.py:225
  9.7 3.7 %collective-permute-start = (bf16[64,2048]{1,0:T(8,128)(2,1)S(1)}, bf16[64,2048]{1,0:T(8,128)(2,1)S(1)}, u32[]{:S(2)}, u32[]{:S(2)}) collective-permute-start(bf16[64,2048]{1,0:T(8,128)(2,1)S(1)} %pad_maximum_fusion.refs_0_), channel_id=1, source_target_pairs={{0,1},{1,0},{2,3},{3,2},{4,5},{5,4},{6,7},{7,6},{8,9},{9,8},{10,11... | collective-permute-start | bytes 786440 | tf_op jit(solution)/shard_map/ppermute | solution.py:225
  12.7 7.8 %collective-permute-start.2 = (bf16[64,2048]{1,0:T(8,128)(2,1)S(1)}, bf16[64,2048]{1,0:T(8,128)(2,1)S(1)}, u32[]{:S(2)}, u32[]{:S(2)}) collective-permute-start(bf16[64,2048]{1,0:T(8,128)(2,1)S(1)} %collective-permute-done.1.refs_2_), channel_id=1, source_target_pairs={{0,1},{1,0},{2,3},{3,2},{4,5},{5,4},{6,7},{7,6},{8,9},{9,8},{10,11... | collective-permute-start | bytes 786440 | tf_op jit(solution)/shard_map/ppermute | solution.py:225
  22.9 4.9 %collective-permute-start.8 = (f32[56,128]{1,0:T(8,128)S(1)}, f32[56,128]{1,0:T(8,128)S(1)}, u32[]{:S(2)}, u32[]{:S(2)}) collective-permute-start(f32[56,128]{1,0:T(8,128)S(1)} %stats.1.refs_9_), channel_id=1, source_target_pairs={{0,9},{1,8},{2,11},{3,10},{4,13},{5,12},{6,15},{7,14},{8,1},{9,0},... | collective-permute-start | bytes 86024 | tf_op jit(solution)/shard_map/ppermute | solution.py:225
  23.7 5.4 %collective-permute-start.7 = (f32[56,128]{1,0:T(8,128)S(1)}, f32[56,128]{1,0:T(8,128)S(1)}, u32[]{:S(2)}, u32[]{:S(2)}) collective-permute-start(f32[56,128]{1,0:T(8,128)S(1)} %stats.1.refs_9_), channel_id=1, source_target_pairs={{0,8},{1,9},{2,10},{3,11},{4,12},{5,13},{6,14},{7,15},{8,0},{9,1},... | collective-permute-start | bytes 86024 | tf_op jit(solution)/shard_map/ppermute | solution.py:225
  25.6 3.4 %collective-permute-start.6 = (f32[56,128]{1,0:T(8,128)S(1)}, f32[56,128]{1,0:T(8,128)S(1)}, u32[]{:S(2)}, u32[]{:S(2)}) collective-permute-start(f32[56,128]{1,0:T(8,128)S(1)} %stats.1.refs_9_), channel_id=1, source_target_pairs={{0,1},{1,0},{2,3},{3,2},{4,5},{5,4},{6,7},{7,6},{8,9},{9,8},{10,11... | collective-permute-start | bytes 86024 | tf_op jit(solution)/shard_map/ppermute | solution.py:225
  33.0 5.6 %collective-permute-start.9 = (bf16[1024,128]{1,0:T(8,128)(2,1)S(1)}, bf16[1024,128]{1,0:T(8,128)(2,1)S(1)}, u32[]{:S(2)}, u32[]{:S(2)}) collective-permute-start(bf16[1024,128]{1,0:T(8,128)(2,1)S(1)} %get-tuple-element.20), channel_id=1, source_target_pairs={{0,1},{1,0},{2,3},{3,2},{4,5},{5,4},{6,7},{7,6},{8,9},{9,8},{10,11... | collective-permute-start | bytes 786440 | tf_op jit(solution)/shard_map/ppermute | solution.py:225
  33.8 23.7 %collective-permute-start.11 = (bf16[1024,128]{1,0:T(8,128)(2,1)S(1)}, bf16[1024,128]{1,0:T(8,128)(2,1)S(1)}, u32[]{:S(2)}, u32[]{:S(2)}) collective-permute-start(bf16[1024,128]{1,0:T(8,128)(2,1)S(1)} %get-tuple-element.23), channel_id=1, source_target_pairs={{0,2},{1,3},{2,0},{3,1},{4,6},{5,7},{6,4},{7,5},{8,10},{9,11},{10,... | collective-permute-start | bytes 786440 | tf_op jit(solution)/shard_map/ppermute | solution.py:225
  35.3 22.3 %collective-permute-start.12 = (bf16[1024,128]{1,0:T(8,128)(2,1)S(1)}, bf16[1024,128]{1,0:T(8,128)(2,1)S(1)}, u32[]{:S(2)}, u32[]{:S(2)}) collective-permute-start(bf16[1024,128]{1,0:T(8,128)(2,1)S(1)} %get-tuple-element.24), channel_id=1, source_target_pairs={{0,4},{1,5},{2,6},{3,7},{4,0},{5,1},{6,2},{7,3},{8,12},{9,13},{10,... | collective-permute-start | bytes 786440 | tf_op jit(solution)/shard_map/ppermute | solution.py:225
  38.2 19.4 %collective-permute-start.13 = (bf16[1024,128]{1,0:T(8,128)(2,1)S(1)}, bf16[1024,128]{1,0:T(8,128)(2,1)S(1)}, u32[]{:S(2)}, u32[]{:S(2)}) collective-permute-start(bf16[1024,128]{1,0:T(8,128)(2,1)S(1)} %get-tuple-element.25), channel_id=1, source_target_pairs={{0,6},{1,7},{2,4},{3,5},{4,2},{5,3},{6,0},{7,1},{8,14},{9,15},{10,... | collective-permute-start | bytes 786440 | tf_op jit(solution)/shard_map/ppermute | solution.py:225
  38.6 19.0 %collective-permute-start.10 = (bf16[512,128]{1,0:T(8,128)(2,1)S(1)}, bf16[512,128]{1,0:T(8,128)(2,1)S(1)}, u32[]{:S(2)}, u32[]{:S(2)}) collective-permute-start(bf16[512,128]{1,0:T(8,128)(2,1)S(1)} %add_convert_fusion), channel_id=1, source_target_pairs={{0,8},{1,9},{2,10},{3,11},{4,12},{5,13},{6,14},{7,15},{8,0},{9,1},... | collective-permute-start | bytes 393224 | tf_op jit(solution)/shard_map/ppermute | solution.py:225

commit v3 on v2

--- a/solution.py
+++ b/solution.py
@@ -34,61 +34,78 @@
     )
 
 
-def key_bias(info_ref, block):
+def own_bias(tokens, rows):
+    u = lax.broadcasted_iota(jnp.int32, (tokens, 4 * rows), 0)
+    lane = lax.broadcasted_iota(jnp.int32, (tokens, 4 * rows), 1)
+    return jnp.where((lane < rows) & (u <= lane % tokens), 0.0, MASKED)
+
+
+def block_bias(info_ref, k, block):
     at = lax.broadcasted_iota(jnp.int32, (block, 1), 0)
-    return jnp.concatenate(
-        [
-            jnp.where(at + info_ref[1 + k] * block < info_ref[0], 0.0, MASKED)
-            for k in range(4)
-        ],
-        axis=0,
-    )
-
-
-def own_mask(tokens, rows):
-    u = lax.broadcasted_iota(jnp.int32, (tokens, rows), 0)
-    t = lax.broadcasted_iota(jnp.int32, (tokens, rows), 1) % tokens
-    return u <= t
-
-
-def stats_kernel(to_log2, info_ref, *refs):
-    qg, kvs, own_ref, out_ref = refs[0:4], refs[4:8], refs[8], refs[9]
+    return jnp.where(at + info_ref[1 + k] * block < info_ref[0], 0.0, MASKED)
+
+
+def with_own(blocks, own_ref, part, g):
+    tokens = own_ref.shape[0] // 2
+    own = own_ref[part * tokens : (part + 1) * tokens, g * HD : (g + 1) * HD]
+    return jnp.concatenate([cols_of(blocks, part, g), own], axis=0)
+
+
+def partial_stats(score, slope):
+    top = jnp.max(score, axis=0, keepdims=True)
+    e = jnp.exp2(score - top)
+    total = jnp.sum(e, axis=0, keepdims=True)
+    return top, total, jnp.sum(e * slope, axis=0, keepdims=True)
+
+
+def add_bias(score, bias, own):
+    at = bias.shape[0]
+    return jnp.concatenate([score[:at] + bias, score[at:] + own], axis=0)
+
+
+def join(one, two):
+    top = jnp.maximum(one[0], two[0])
+    f, h = jnp.exp2(one[0] - top), jnp.exp2(two[0] - top)
+    return top, one[1] * f + two[1] * h, one[2] * f + two[2] * h
+
+
+def first_stats_kernel(to_log2, where, info_ref, *refs):
+    qg, kvs, own_ref, out_ref = refs[0:4], refs[4:-2], refs[-2], refs[-1]
     block = (kvs[0].shape[0] - 16) // 2
     groups = kvs[0].shape[1] // HD
     tokens = own_ref.shape[0] // 2
     rows = qg[0].shape[1] // HD // groups * tokens
-    bias = key_bias(info_ref, block)
-    causal = own_mask(tokens, rows)
+    bias = jnp.concatenate([block_bias(info_ref, k, block) for k in where], axis=0)
+    own = own_bias(tokens, rows)
+    out_ref[...] = jnp.zeros_like(out_ref)
+    for g in range(groups):
+        q, w = rows_of(qg, 0, g), rows_of(qg, 1, g)
+        score = dot(with_own(kvs, own_ref, 0, g), q, NT) * to_log2
+        slope = dot(with_own(kvs, own_ref, 1, g), w, NT)
+        for i, value in enumerate(partial_stats(add_bias(score, bias, own), slope)):
+            out_ref[i * groups + g : i * groups + g + 1, :] = value
+
+
+def last_stats_kernel(to_log2, where, info_ref, *refs):
+    qg, kvs, first_ref, out_ref = refs[0:4], refs[4:8], refs[8], refs[9]
+    block = (kvs[0].shape[0] - 16) // 2
+    groups = kvs[0].shape[1] // HD
+    rows = qg[0].shape[1] // HD // groups * (qg[0].shape[0] // 2)
+    bias = jnp.concatenate([block_bias(info_ref, k, block) for k in where], axis=0)
     out_ref[48:56, :] = sum(
         r[2 * block : 2 * block + 16, :HD].astype(jnp.float32)[:8] for r in kvs
     )
     for g in range(groups):
-        q = rows_of(qg, 0, g)
-        w = rows_of(qg, 1, g)
-        score = dot(cols_of(kvs, 0, g), q, NT) * to_log2 + bias
-        slope = dot(cols_of(kvs, 1, g), w, NT)
-        own_cols = slice(g * HD, (g + 1) * HD)
-        own_score = dot(own_ref[:tokens, own_cols], q[:rows], NT) * to_log2
-        own_score = jnp.where(causal, own_score, MASKED)
-        own_slope = dot(own_ref[tokens:, own_cols], w[:rows], NT)
-        top = jnp.max(score, axis=0, keepdims=True)
-        own_top = jnp.maximum(
-            top[:, :rows], jnp.max(own_score, axis=0, keepdims=True)
-        )
-        top = jnp.concatenate([own_top, top[:, rows:]], axis=1)
-        e = jnp.exp2(score - top)
-        total = jnp.sum(e, axis=0, keepdims=True)
-        mixed = jnp.sum(e * slope, axis=0, keepdims=True)
-        own_e = jnp.exp2(own_score - own_top)
-        own_total = jnp.sum(own_e, axis=0, keepdims=True)
-        own_mixed = jnp.sum(own_e * own_slope, axis=0, keepdims=True)
+        q, w = rows_of(qg, 0, g), rows_of(qg, 1, g)
+        blocks = [kvs[k] for k in where]
+        score = dot(cols_of(blocks, 0, g), q, NT) * to_log2 + bias
+        got = partial_stats(score, dot(cols_of(blocks, 1, g), w, NT))
+        before = [first_ref[i * groups + g : i * groups + g + 1, :] for i in range(3)]
+        got = join(before, got)
         for s in range(4):
-            lanes = slice(s * rows, (s + 1) * rows)
-            at = s * 4 + g
-            out_ref[at : at + 1, :] = top[:, lanes]
-            extra = (own_total, own_mixed) if s == 0 else (0.0, 0.0)
-            out_ref[16 + at : 17 + at, :] = total[:, lanes] + extra[0]
-            out_ref[32 + at : 33 + at, :] = mixed[:, lanes] + extra[1]
+            for i in range(3):
+                at = 16 * i + 4 * s + g
+                out_ref[at : at + 1, :] = got[i][:, s * rows : (s + 1) * rows]
 
 
 def grads_kernel(to_log2, info_ref, *refs):
@@ -101,8 +118,8 @@
     groups = kvs[0].shape[1] // HD
     tokens = own_ref.shape[0] // 2
     rows = qg[0].shape[1] // HD // groups * tokens
-    bias = key_bias(info_ref, block)
-    causal = own_mask(tokens, rows)
+    bias = jnp.concatenate([block_bias(info_ref, k, block) for k in range(4)], axis=0)
+    own_rows = own_bias(tokens, rows)
     shifts, means = [], []
     for s in range(4):
         tops = [stats[e][(s ^ e) * 4 : (s ^ e) * 4 + 4, :] for e in range(4)]
@@ -123,27 +140,20 @@
     for g in range(groups):
         q = rows_of(qg, 0, g)
         w = rows_of(qg, 1, g)
-        k = cols_of(kvs, 0, g)
+        k = with_own(kvs, own_ref, 0, g)
         sh, mn = shift[g : g + 1, :], mean[g : g + 1, :]
-        score = dot(k, q, NT) * to_log2 + bias
-        slope = dot(cols_of(kvs, 1, g), w, NT)
+        score = add_bias(dot(k, q, NT) * to_log2, bias, own_rows)
+        slope = dot(with_own(kvs, own_ref, 1, g), w, NT)
         p = jnp.exp2(score - sh)
         ds = (p * (slope - mn)).astype(jnp.bfloat16)
         dv = dot(p.astype(jnp.bfloat16), w, NN)
         dk = dot(ds, q, NN)
         dq = dot(k.T, ds, NN)
         own_cols = slice(g * HD, (g + 1) * HD)
-        own_k = own_ref[:tokens, own_cols]
-        own_score = dot(own_k, q[:rows], NT) * to_log2
-        own_score = jnp.where(causal, own_score, MASKED)
-        own_slope = dot(own_ref[tokens:, own_cols], w[:rows], NT)
-        own_p = jnp.exp2(own_score - sh[:, :rows])
-        own_ds = (own_p * (own_slope - mn[:, :rows])).astype(jnp.bfloat16)
-        own_out[:tokens, own_cols] = dot(own_ds, q[:rows], NN)
-        own_out[tokens:, own_cols] = dot(own_p.astype(jnp.bfloat16), w[:rows], NN)
-        own_dq = dot(own_k.T, own_ds, NN)
+        own_out[:tokens, own_cols] = dk[4 * block :]
+        own_out[tokens:, own_cols] = dv[4 * block :]
         at = slice(g * HD, (g + 1) * HD)
-        dq_own[at, :] = dq[:, :rows] + own_dq
+        dq_own[at, :] = dq[:, :rows]
         dq_far[at, :] = dq[:, 2 * rows : 3 * rows]
         dq_sib[at, :] = dq[:, rows : 2 * rows].astype(jnp.bfloat16)
         dq_sib[half_at(dq_sib, g), :] = dq[:, 3 * rows :].astype(jnp.bfloat16)
@@ -238,14 +248,23 @@
     qg = [qg0, qg1, qg2, qg3]
     me = lax.axis_index("sample")
     info = jnp.stack([prompt_len[0]] + [me ^ (2 * e) for e in range(4)]).astype(jnp.int32)
+    early, late = (0, 1, 3), (2,)
+    first = pl.pallas_call(
+        functools.partial(first_stats_kernel, to_log2, early),
+        out_shape=shape((16, width * 4 * tokens // HD // groups), f32),
+        in_specs=[smem] + [vmem] * (5 + len(early)),
+        out_specs=vmem,
+        compiler_params=params,
+        name="stats_first",
+    )(info, *qg, *[kv[k] for k in early], own)
     stats0 = pl.pallas_call(
-        functools.partial(stats_kernel, to_log2),
+        functools.partial(last_stats_kernel, to_log2, late),
         out_shape=shape((56, HD), f32),
         in_specs=[smem] + [vmem] * 9,
         out_specs=vmem,
         compiler_params=params,
         name="stats",
-    )(info, *qg, *kv, own)
+    )(info, *qg, *kv, first)
     stats = [stats0, swap(stats0, 1), swap(stats0, 8), swap(stats0, 9)]
     kv_rows = 2 * groups * block
     dq_rows = width // HD // 4 * HD

time: 59.5 us -> 58.4 us (0.982)
  waiting for transfers between devices: 12.7 us -> 10.7 us
  starting transfers between devices: 17.1 us -> 17.8 us
    ppermute x14, waiting for transfers between devices: 12.7 us -> 10.7 us  [swap(): lax.ppermute(array, 'sample', [(i, i ^ mask) for i in range(samples)])]
    pallas_call x1 -> x2, Pallas kernels: 2.41 us -> 3.05 us  [the longest x1 1.88 us: per_device(): pl.pallas_call(functools.partial(first_stats_kernel, to_log2, early), out...]
    ppermute x14, starting transfers between devices: 17.1 us -> 17.8 us  [swap(): lax.ppermute(array, 'sample', [(i, i ^ mask) for i in range(samples)])]
  transfers between devices with their start and end apart: 14 -> 14, of which waited for: 5 -> 6; matrix products, arithmetic and copies ran while one was open for 0% -> 0% of each run, Pallas kernels for 0% -> 3%
where the time goes in v3:
time: 58.4 us; the launch traced here: 57.4 us
  starting transfers between devices  17.8 us (30%)
  blocking collectives  17.4 us (30%)
  waiting for transfers between devices  10.7 us (18%)
  Pallas kernels  7.45 us (13%)
  between operations  2.73 us (5%)
  other arithmetic  1.2 us (2%)
    ppermute x14, starting transfers between devices, swap(): lax.ppermute(array, 'sample', [(i, i ^ mask) for i in range(samples)])  17.8 us
    all_to_all x1, blocking collectives, per_device(): total = lax.all_to_all(outs[8], 'prompt', 0, 0, tiled=True)  17.4 us
    ppermute x14, waiting for transfers between devices, swap(): lax.ppermute(array, 'sample', [(i, i ^ mask) for i in range(samples)])  10.7 us
    pallas_call x1, Pallas kernels, per_device(): pl.pallas_call(functools.partial(grads_kernel, to_log2), out_shape=[shape...  3.49 us
    pallas_call x1, Pallas kernels, per_device(): pl.pallas_call(functools.partial(first_stats_kernel, to_log2, early), out...  1.88 us
    pallas_call x1, Pallas kernels, per_device(): pl.pallas_call(functools.partial(last_stats_kernel, to_log2, late), out_s...  1.17 us
  transfers between devices with their start and end apart: 14, of which 6 were waited for; matrix products, arithmetic and copies ran while one was open for 0% of the time, Pallas kernels for 3%

profile of v3, /device:TPU:4, one launch (start us, length us, event | category | flops | bytes accessed | tf_op | source)
XLA Modules:
  0.0 57.4 jit_solution(13559101027586963172)
XLA Ops:
  1.9 0.0 copy-start
  1.9 1.0 %fusion = bf16[32,2048]{1,0:T(8,128)(2,1)S(1)} fusion(bf16[1,1,32,2048]{3,2,1,0:T(8,128)(2,1)} %param.10, f32[32]{0:T(128)S(1)} %compare_select_fusion), kind=kLoop, calls=%fused_computation.3 | loop fusion | flops 196608 | bytes 262272 | tf_op jit(solution)/shard_map/convert_element_type | solution.py:239
  3.0 0.0 copy-done
  3.0 0.0 copy-start.1
  3.0 0.0 copy-start.2
  3.0 2.3 %collective-permute-start.1 = (bf16[64,2048]{1,0:T(8,128)(2,1)S(1)}, bf16[64,2048]{1,0:T(8,128)(2,1)S(1)}, u32[]{:S(2)}, u32[]{:S(2)}) collective-permute-start(bf16[64,2048]{1,0:T(8,128)(2,1)S(1)} %pad_maximum_fusion.refs_0_), channel_id=1, source_target_pairs={{0,8},{1,9},{2,10},{3,11},{4,12},{5,13},{6,14},{7,15},{8,0},{9,1},... | collective-permute-start | bytes 786440 | tf_op jit(solution)/shard_map/ppermute | solution.py:235
  5.4 0.0 copy-done.1
  5.4 0.0 copy-done.2
  5.4 0.0 copy-start.3
  5.4 0.0 copy-start.4
  5.4 0.1 maximum_maximum_fusion.refs_4_
  5.5 1.6 %collective-permute-start.5 = (bf16[272,512]{1,0:T(8,128)(2,1)S(1)}, bf16[272,512]{1,0:T(8,128)(2,1)S(1)}, u32[]{:S(2)}, u32[]{:S(2)}) collective-permute-start(bf16[272,512]{1,0:T(8,128)(2,1)S(1)} %maximum_maximum_fusion.refs_4_), channel_id=1, source_target_pairs={{0,6},{1,7},{2,4},{3,5},{4,2},{5,3},{6,0},{7,1},{8,14},{9,15},{10,... | collective-permute-start | bytes 835592 | tf_op jit(solution)/shard_map/ppermute | solution.py:235
  7.2 0.1 collective-permute-start.3
  7.3 3.0 %collective-permute-start.4 = (bf16[272,512]{1,0:T(8,128)(2,1)S(1)}, bf16[272,512]{1,0:T(8,128)(2,1)S(1)}, u32[]{:S(2)}, u32[]{:S(2)}) collective-permute-start(bf16[272,512]{1,0:T(8,128)(2,1)S(1)} %maximum_maximum_fusion.refs_4_), channel_id=1, source_target_pairs={{0,4},{1,5},{2,6},{3,7},{4,0},{5,1},{6,2},{7,3},{8,12},{9,13},{10,... | collective-permute-start | bytes 835592 | tf_op jit(solution)/shard_map/ppermute | solution.py:235
  10.3 0.0 collective-permute-start
  10.3 2.3 %collective-permute-done.1.refs_2_ = bf16[64,2048]{1,0:T(8,128)(2,1)S(1)} collective-permute-done((bf16[64,2048]{1,0:T(8,128)(2,1)S(1)}, bf16[64,2048]{1,0:T(8,128)(2,1)S(1)}, u32[]{:S(2)}, u32[]{:S(2)}) %collective-permute-start.1) | collective-permute-done | bytes 262176 | tf_op jit(solution)/shard_map/ppermute | solution.py:235
  12.7 0.0 collective-permute-start.2
  13.3 0.1 stack.19.info_ref
  13.4 0.0 copy-done.3
  13.4 0.0 copy-done.4
  13.4 0.0 collective-permute-done.refs_1_
  13.4 1.9 %collective-permute-done.5.refs_6_.refs_7_ = bf16[272,512]{1,0:T(8,128)(2,1)S(1)} collective-permute-done((bf16[272,512]{1,0:T(8,128)(2,1)S(1)}, bf16[272,512]{1,0:T(8,128)(2,1)S(1)}, u32[]{:S(2)}, u32[]{:S(2)}) %collective-permute-start.5) | collective-permute-done | bytes 278560 | tf_op jit(solution)/shard_map/ppermute | solution.py:235
  15.3 1.4 %collective-permute-done.3.refs_5_ = bf16[272,512]{1,0:T(8,128)(2,1)S(1)} collective-permute-done((bf16[272,512]{1,0:T(8,128)(2,1)S(1)}, bf16[272,512]{1,0:T(8,128)(2,1)S(1)}, u32[]{:S(2)}, u32[]{:S(2)}) %collective-permute-start.3) | collective-permute-done | bytes 278560 | tf_op jit(solution)/shard_map/ppermute | solution.py:235
  16.8 0.0 collective-permute-done.2.refs_3_
  16.8 1.9 %stats_first.1.refs_8_ = f32[16,512]{1,0:T(8,128)S(1)} custom-call(s32[5]{0:T(128)S(1)} %stack.19.info_ref, bf16[64,2048]{1,0:T(8,128)(2,1)S(1)} %pad_maximum_fusion.refs_0_, bf16[64,2048]{1,0:T(8,128)(2,1)S(1)} %collective-permute-done.refs_1_, bf16[64,2048]{1,0:T(8,128)(2,1)S(1)} %collective-permute-done.1.refs_2_, ...), custom_call_target="tpu_custom_call" | custom-call | tf_op jit(solution)/shard_map/stats_first/pallas_call | solution.py:252
  18.7 2.4 %collective-permute-done.4.refs_6_ = bf16[272,512]{1,0:T(8,128)(2,1)S(1)} collective-permute-done((bf16[272,512]{1,0:T(8,128)(2,1)S(1)}, bf16[272,512]{1,0:T(8,128)(2,1)S(1)}, u32[]{:S(2)}, u32[]{:S(2)}) %collective-permute-start.4) | collective-permute-done | bytes 278560 | tf_op jit(solution)/shard_map/ppermute | solution.py:235
  21.1 1.2 %stats.1.refs_9_ = f32[56,128]{1,0:T(8,128)S(1)} custom-call(s32[5]{0:T(128)S(1)} %stack.19.info_ref, bf16[64,2048]{1,0:T(8,128)(2,1)S(1)} %pad_maximum_fusion.refs_0_, bf16[64,2048]{1,0:T(8,128)(2,1)S(1)} %collective-permute-done.refs_1_, bf16[64,2048]{1,0:T(8,128)(2,1)S(1)} %collective-permute-done.1.refs_2_, ...), custom_call_target="tpu_custom_call" | custom-call | tf_op jit(solution)/shard_map/stats/pallas_call | solution.py:260
  22.3 0.7 %collective-permute-start.8 = (f32[56,128]{1,0:T(8,128)S(1)}, f32[56,128]{1,0:T(8,128)S(1)}, u32[]{:S(2)}, u32[]{:S(2)}) collective-permute-start(f32[56,128]{1,0:T(8,128)S(1)} %stats.1.refs_9_), channel_id=1, source_target_pairs={{0,9},{1,8},{2,11},{3,10},{4,13},{5,12},{6,15},{7,14},{8,1},{9,0},... | collective-permute-start | bytes 86024 | tf_op jit(solution)/shard_map/ppermute | solution.py:235
  22.9 2.0 %collective-permute-start.7 = (f32[56,128]{1,0:T(8,128)S(1)}, f32[56,128]{1,0:T(8,128)S(1)}, u32[]{:S(2)}, u32[]{:S(2)}) collective-permute-start(f32[56,128]{1,0:T(8,128)S(1)} %stats.1.refs_9_), channel_id=1, source_target_pairs={{0,8},{1,9},{2,10},{3,11},{4,12},{5,13},{6,14},{7,15},{8,0},{9,1},... | collective-permute-start | bytes 86024 | tf_op jit(solution)/shard_map/ppermute | solution.py:235
  24.9 0.8 %collective-permute-start.6 = (f32[56,128]{1,0:T(8,128)S(1)}, f32[56,128]{1,0:T(8,128)S(1)}, u32[]{:S(2)}, u32[]{:S(2)}) collective-permute-start(f32[56,128]{1,0:T(8,128)S(1)} %stats.1.refs_9_), channel_id=1, source_target_pairs={{0,1},{1,0},{2,3},{3,2},{4,5},{5,4},{6,7},{7,6},{8,9},{9,8},{10,11... | collective-permute-start | bytes 86024 | tf_op jit(solution)/shard_map/ppermute | solution.py:235
  25.7 1.4 %collective-permute-done.8.refs_12_ = f32[56,128]{1,0:T(8,128)S(1)} collective-permute-done((f32[56,128]{1,0:T(8,128)S(1)}, f32[56,128]{1,0:T(8,128)S(1)}, u32[]{:S(2)}, u32[]{:S(2)}) %collective-permute-start.8) | collective-permute-done | bytes 28704 | tf_op jit(solution)/shard_map/ppermute | solution.py:235
  27.1 1.2 %collective-permute-done.7.refs_11_ = f32[56,128]{1,0:T(8,128)S(1)} collective-permute-done((f32[56,128]{1,0:T(8,128)S(1)}, f32[56,128]{1,0:T(8,128)S(1)}, u32[]{:S(2)}, u32[]{:S(2)}) %collective-permute-start.7) | collective-permute-done | bytes 28704 | tf_op jit(solution)/shard_map/ppermute | solution.py:235
  28.3 0.0 collective-permute-done.6.refs_10_
  28.3 3.5 %grads.1 = (f32[512,128]{1,0:T(8,128)S(1)}, f32[512,128]{1,0:T(8,128)S(1)}, bf16[1024,128]{1,0:T(8,128)(2,1)S(1)}, f32[1024,128]{1,0:T(8,128)S(1)}, bf16[1024,12...) custom-call(s32[5]{0:T(128)S(1)} %stack.19.info_ref, ...), custom_call_target="tpu_custom_call" | custom-call | tf_op jit(solution)/shard_map/grads/pallas_call | solution.py:271
  31.8 0.9 %collective-permute-start.9 = (bf16[1024,128]{1,0:T(8,128)(2,1)S(1)}, bf16[1024,128]{1,0:T(8,128)(2,1)S(1)}, u32[]{:S(2)}, u32[]{:S(2)}) collective-permute-start(bf16[1024,128]{1,0:T(8,128)(2,1)S(1)} %get-tuple-element.20), channel_id=1, source_target_pairs={{0,1},{1,0},{2,3},{3,2},{4,5},{5,4},{6,7},{7,6},{8,9},{9,8},{10,11... | collective-permute-start | bytes 786440 | tf_op jit(solution)/shard_map/ppermute | solution.py:235
  32.8 0.2 collective-permute-start.11
  33.0 4.1 %collective-permute-start.12 = (bf16[1024,128]{1,0:T(8,128)(2,1)S(1)}, bf16[1024,128]{1,0:T(8,128)(2,1)S(1)}, u32[]{:S(2)}, u32[]{:S(2)}) collective-permute-start(bf16[1024,128]{1,0:T(8,128)(2,1)S(1)} %get-tuple-element.24), channel_id=1, source_target_pairs={{0,4},{1,5},{2,6},{3,7},{4,0},{5,1},{6,2},{7,3},{8,12},{9,13},{10,... | collective-permute-start | bytes 786440 | tf_op jit(solution)/shard_map/ppermute | solution.py:235
  37.1 0.4 collective-permute-start.13
  37.5 0.0 collective-permute-done.9.refs_1_
  37.5 1.5 %collective-permute-start.10 = (bf16[512,128]{1,0:T(8,128)(2,1)S(1)}, bf16[512,128]{1,0:T(8,128)(2,1)S(1)}, u32[]{:S(2)}, u32[]{:S(2)}) collective-permute-start(bf16[512,128]{1,0:T(8,128)(2,1)S(1)} %add_convert_fusion), channel_id=1, source_target_pairs={{0,8},{1,9},{2,10},{3,11},{4,12},{5,13},{6,14},{7,15},{8,0},{9,1},... | collective-permute-start | bytes 393224 | tf_op jit(solution)/shard_map/ppermute | solution.py:235
  39.0 17.4 %all_to_all.5.refs_8_ = f32[16,1,128]{2,1,0:T(1,128)S(1)} all-to-all(f32[16,1,128]{2,1,0:T(1,128)S(1)} %get-tuple-element.27), channel_id=1, replica_groups=mesh['prompt'=16,'sample'=16] {'prompt'}, dimensions={0} | all-to-all | bytes 16384 | tf_op jit(solution)/shard_map/all_to_all | solution.py:289
  56.5 0.0 collective-permute-done.11.refs_4_
  56.5 0.0 collective-permute-done.12.refs_5_
  56.5 0.0 collective-permute-done.13.refs_6_
  56.5 0.0 collective-permute-done.10.refs_2_
  56.5 0.9 %finish.1 = (bf16[32,2048]{1,0:T(8,128)(2,1)}, bf16[128,512]{1,0:T(8,128)(2,1)}, bf16[128,512]{1,0:T(8,128)(2,1)}, bf16[32,512]{1,0:T(8,128)(2,1)}, bf16[32,512]{1,0:T(8,128)(2,1)}) custom-call(f32[512,128]{1,0:T(8,128)S(1)} %get-tuple-element.19.refs_0_, bf16[1024,128]{1,0:T(8,128)(2,1)S(1)} %collective-permute-done.9.refs_1_, ...), custom_call_target="tpu_custom_call" | custom-call | tf_op jit(solution)/shard_map/finish/pallas_call | solution.py:291
  (6 shorter events, 0.1 us)
Async XLA Ops:
  1.9 1.0 %copy-start = (bf16[1,1,32,2048]{3,2,1,0:T(8,128)(2,1)S(1)}, bf16[1,1,32,2048]{3,2,1,0:T(8,128)(2,1)}, u32[]{:S(2)}) copy-start(bf16[1,1,32,2048]{3,2,1,0:T(8,128)(2,1)} %param.9) | copy-start | bytes 393220
  3.0 2.4 %copy-start.1 = (bf16[1,128,512]{2,1,0:T(8,128)(2,1)S(1)}, bf16[1,128,512]{2,1,0:T(8,128)(2,1)}, u32[]{:S(2)}) copy-start(bf16[1,128,512]{2,1,0:T(8,128)(2,1)} %param.14) | copy-start | bytes 393220
  3.0 2.4 %copy-start.2 = (bf16[1,128,512]{2,1,0:T(8,128)(2,1)S(1)}, bf16[1,128,512]{2,1,0:T(8,128)(2,1)}, u32[]{:S(2)}) copy-start(bf16[1,128,512]{2,1,0:T(8,128)(2,1)} %param.13) | copy-start | bytes 393220
  3.0 9.6 %collective-permute-start.1 = (bf16[64,2048]{1,0:T(8,128)(2,1)S(1)}, bf16[64,2048]{1,0:T(8,128)(2,1)S(1)}, u32[]{:S(2)}, u32[]{:S(2)}) collective-permute-start(bf16[64,2048]{1,0:T(8,128)(2,1)S(1)} %pad_maximum_fusion.refs_0_), channel_id=1, source_target_pairs={{0,8},{1,9},{2,10},{3,11},{4,12},{5,13},{6,14},{7,15},{8,0},{9,1},... | collective-permute-start | bytes 786440 | tf_op jit(solution)/shard_map/ppermute | solution.py:235
  5.4 8.0 %copy-start.3 = (bf16[1,1,32,512]{3,2,1,0:T(8,128)(2,1)S(1)}, bf16[1,1,32,512]{3,2,1,0:T(8,128)(2,1)}, u32[]{:S(2)}) copy-start(bf16[1,1,32,512]{3,2,1,0:T(8,128)(2,1)} %param.16) | copy-start | bytes 98308
  5.4 8.0 %copy-start.4 = (bf16[1,1,32,512]{3,2,1,0:T(8,128)(2,1)S(1)}, bf16[1,1,32,512]{3,2,1,0:T(8,128)(2,1)}, u32[]{:S(2)}) copy-start(bf16[1,1,32,512]{3,2,1,0:T(8,128)(2,1)} %param.15) | copy-start | bytes 98308
  5.5 9.8 %collective-permute-start.5 = (bf16[272,512]{1,0:T(8,128)(2,1)S(1)}, bf16[272,512]{1,0:T(8,128)(2,1)S(1)}, u32[]{:S(2)}, u32[]{:S(2)}) collective-permute-start(bf16[272,512]{1,0:T(8,128)(2,1)S(1)} %maximum_maximum_fusion.refs_4_), channel_id=1, source_target_pairs={{0,6},{1,7},{2,4},{3,5},{4,2},{5,3},{6,0},{7,1},{8,14},{9,15},{10,... | collective-permute-start | bytes 835592 | tf_op jit(solution)/shard_map/ppermute | solution.py:235
  7.2 9.6 %collective-permute-start.3 = (bf16[272,512]{1,0:T(8,128)(2,1)S(1)}, bf16[272,512]{1,0:T(8,128)(2,1)S(1)}, u32[]{:S(2)}, u32[]{:S(2)}) collective-permute-start(bf16[272,512]{1,0:T(8,128)(2,1)S(1)} %maximum_maximum_fusion.refs_4_), channel_id=1, source_target_pairs={{0,2},{1,3},{2,0},{3,1},{4,6},{5,7},{6,4},{7,5},{8,10},{9,11},{10,... | collective-permute-start | bytes 835592 | tf_op jit(solution)/shard_map/ppermute | solution.py:235
  7.3 13.8 %collective-permute-start.4 = (bf16[272,512]{1,0:T(8,128)(2,1)S(1)}, bf16[272,512]{1,0:T(8,128)(2,1)S(1)}, u32[]{:S(2)}, u32[]{:S(2)}) collective-permute-start(bf16[272,512]{1,0:T(8,128)(2,1)S(1)} %maximum_maximum_fusion.refs_4_), channel_id=1, source_target_pairs={{0,4},{1,5},{2,6},{3,7},{4,0},{5,1},{6,2},{7,3},{8,12},{9,13},{10,... | collective-permute-start | bytes 835592 | tf_op jit(solution)/shard_map/ppermute | solution.py:235
  10.3 3.1 %collective-permute-start = (bf16[64,2048]{1,0:T(8,128)(2,1)S(1)}, bf16[64,2048]{1,0:T(8,128)(2,1)S(1)}, u32[]{:S(2)}, u32[]{:S(2)}) collective-permute-start(bf16[64,2048]{1,0:T(8,128)(2,1)S(1)} %pad_maximum_fusion.refs_0_), channel_id=1, source_target_pairs={{0,1},{1,0},{2,3},{3,2},{4,5},{5,4},{6,7},{7,6},{8,9},{9,8},{10,11... | collective-permute-start | bytes 786440 | tf_op jit(solution)/shard_map/ppermute | solution.py:235
  12.7 4.1 %collective-permute-start.2 = (bf16[64,2048]{1,0:T(8,128)(2,1)S(1)}, bf16[64,2048]{1,0:T(8,128)(2,1)S(1)}, u32[]{:S(2)}, u32[]{:S(2)}) collective-permute-start(bf16[64,2048]{1,0:T(8,128)(2,1)S(1)} %collective-permute-done.1.refs_2_), channel_id=1, source_target_pairs={{0,1},{1,0},{2,3},{3,2},{4,5},{5,4},{6,7},{7,6},{8,9},{9,8},{10,11... | collective-permute-start | bytes 786440 | tf_op jit(solution)/shard_map/ppermute | solution.py:235
  22.3 4.9 %collective-permute-start.8 = (f32[56,128]{1,0:T(8,128)S(1)}, f32[56,128]{1,0:T(8,128)S(1)}, u32[]{:S(2)}, u32[]{:S(2)}) collective-permute-start(f32[56,128]{1,0:T(8,128)S(1)} %stats.1.refs_9_), channel_id=1, source_target_pairs={{0,9},{1,8},{2,11},{3,10},{4,13},{5,12},{6,15},{7,14},{8,1},{9,0},... | collective-permute-start | bytes 86024 | tf_op jit(solution)/shard_map/ppermute | solution.py:235
  22.9 5.4 %collective-permute-start.7 = (f32[56,128]{1,0:T(8,128)S(1)}, f32[56,128]{1,0:T(8,128)S(1)}, u32[]{:S(2)}, u32[]{:S(2)}) collective-permute-start(f32[56,128]{1,0:T(8,128)S(1)} %stats.1.refs_9_), channel_id=1, source_target_pairs={{0,8},{1,9},{2,10},{3,11},{4,12},{5,13},{6,14},{7,15},{8,0},{9,1},... | collective-permute-start | bytes 86024 | tf_op jit(solution)/shard_map/ppermute | solution.py:235
  24.9 3.4 %collective-permute-start.6 = (f32[56,128]{1,0:T(8,128)S(1)}, f32[56,128]{1,0:T(8,128)S(1)}, u32[]{:S(2)}, u32[]{:S(2)}) collective-permute-start(f32[56,128]{1,0:T(8,128)S(1)} %stats.1.refs_9_), channel_id=1, source_target_pairs={{0,1},{1,0},{2,3},{3,2},{4,5},{5,4},{6,7},{7,6},{8,9},{9,8},{10,11... | collective-permute-start | bytes 86024 | tf_op jit(solution)/shard_map/ppermute | solution.py:235
  31.8 5.6 %collective-permute-start.9 = (bf16[1024,128]{1,0:T(8,128)(2,1)S(1)}, bf16[1024,128]{1,0:T(8,128)(2,1)S(1)}, u32[]{:S(2)}, u32[]{:S(2)}) collective-permute-start(bf16[1024,128]{1,0:T(8,128)(2,1)S(1)} %get-tuple-element.20), channel_id=1, source_target_pairs={{0,1},{1,0},{2,3},{3,2},{4,5},{5,4},{6,7},{7,6},{8,9},{9,8},{10,11... | collective-permute-start | bytes 786440 | tf_op jit(solution)/shard_map/ppermute | solution.py:235
  32.8 23.7 %collective-permute-start.11 = (bf16[1024,128]{1,0:T(8,128)(2,1)S(1)}, bf16[1024,128]{1,0:T(8,128)(2,1)S(1)}, u32[]{:S(2)}, u32[]{:S(2)}) collective-permute-start(bf16[1024,128]{1,0:T(8,128)(2,1)S(1)} %get-tuple-element.23), channel_id=1, source_target_pairs={{0,2},{1,3},{2,0},{3,1},{4,6},{5,7},{6,4},{7,5},{8,10},{9,11},{10,... | collective-permute-start | bytes 786440 | tf_op jit(solution)/shard_map/ppermute | solution.py:235
  33.0 23.5 %collective-permute-start.12 = (bf16[1024,128]{1,0:T(8,128)(2,1)S(1)}, bf16[1024,128]{1,0:T(8,128)(2,1)S(1)}, u32[]{:S(2)}, u32[]{:S(2)}) collective-permute-start(bf16[1024,128]{1,0:T(8,128)(2,1)S(1)} %get-tuple-element.24), channel_id=1, source_target_pairs={{0,4},{1,5},{2,6},{3,7},{4,0},{5,1},{6,2},{7,3},{8,12},{9,13},{10,... | collective-permute-start | bytes 786440 | tf_op jit(solution)/shard_map/ppermute | solution.py:235
  37.1 19.4 %collective-permute-start.13 = (bf16[1024,128]{1,0:T(8,128)(2,1)S(1)}, bf16[1024,128]{1,0:T(8,128)(2,1)S(1)}, u32[]{:S(2)}, u32[]{:S(2)}) collective-permute-start(bf16[1024,128]{1,0:T(8,128)(2,1)S(1)} %get-tuple-element.25), channel_id=1, source_target_pairs={{0,6},{1,7},{2,4},{3,5},{4,2},{5,3},{6,0},{7,1},{8,14},{9,15},{10,... | collective-permute-start | bytes 786440 | tf_op jit(solution)/shard_map/ppermute | solution.py:235
  37.5 19.0 %collective-permute-start.10 = (bf16[512,128]{1,0:T(8,128)(2,1)S(1)}, bf16[512,128]{1,0:T(8,128)(2,1)S(1)}, u32[]{:S(2)}, u32[]{:S(2)}) collective-permute-start(bf16[512,128]{1,0:T(8,128)(2,1)S(1)} %add_convert_fusion), channel_id=1, source_target_pairs={{0,8},{1,9},{2,10},{3,11},{4,12},{5,13},{6,14},{7,15},{8,0},{9,1},... | collective-permute-start | bytes 393224 | tf_op jit(solution)/shard_map/ppermute | solution.py:235

commit v4 on v3

--- a/solution.py
+++ b/solution.py
@@ -67,6 +67,10 @@
     top = jnp.maximum(one[0], two[0])
     f, h = jnp.exp2(one[0] - top), jnp.exp2(two[0] - top)
     return top, one[1] * f + two[1] * h, one[2] * f + two[2] * h
+
+
+def pass_kernel(*refs):
+    pass
 
 
 def first_stats_kernel(to_log2, where, info_ref, *refs):
@@ -243,12 +247,22 @@
     own = jnp.concatenate([own_keys[0, 0], own_values[0, 0]], axis=0)
     qg2 = swap(qg0, 8)
     kv = [kv0] + [swap(kv0, 2 * e) for e in (1, 2, 3)]
+    kv[2], = pl.pallas_call(
+        pass_kernel,
+        out_shape=[shape(kv0.shape, bf16)] * 1,
+        in_specs=[pl.BlockSpec(memory_space=pl.ANY)] * 1,
+        out_specs=[pl.BlockSpec(memory_space=pl.ANY)] * 1,
+        input_output_aliases={0: 0},
+        cost_estimate=pl.CostEstimate(flops=20000000000, bytes_accessed=0, transcendentals=0),
+        compiler_params=params,
+        name="rows_here",
+    )(kv[2])
     qg1 = swap(qg0, 1)
     qg3 = swap(qg2, 1)
     qg = [qg0, qg1, qg2, qg3]
     me = lax.axis_index("sample")
     info = jnp.stack([prompt_len[0]] + [me ^ (2 * e) for e in range(4)]).astype(jnp.int32)
-    early, late = (0, 1, 3), (2,)
+    early, late = (0, 2), (1, 3)
     first = pl.pallas_call(
         functools.partial(first_stats_kernel, to_log2, early),
         out_shape=shape((16, width * 4 * tokens // HD // groups), f32),

time: 58.4 us -> 57.2 us (0.979); the launches traced: 57.4 us -> 57 us
  starting transfers between devices: 17.8 us -> 16.7 us
  local copies, waits for them, and re-layouts: 0.13 us -> 0.92 us
    ppermute x14, starting transfers between devices: 17.8 us -> 16.7 us  [swap(): lax.ppermute(array, 'sample', [(i, i ^ mask) for i in range(samples)])]
    concatenate x1, other arithmetic: 0.11 us -> 1.11 us  [per_device(): kv0 = jnp.concatenate([prefix_keys[0], prefix_values[0], mark], axis=0)]
    convert_element_type x1, other arithmetic: 1.03 us -> 0.09 us  [per_device(): weighted = (out_grad[0, 0].astype(f32) * weight).astype(bf16)]
    unnamed x10 -> x8, local copies, waits for them, and re-layouts: 0.03 us -> 0.82 us
  transfers between devices with their start and end apart: 14 -> 14, of which waited for: 6 -> 4; matrix products, arithmetic and copies ran while one was open for 0% -> 0% of each run, Pallas kernels for 3% -> 3%
where the time goes in v4:
time: 57.2 us; the launch traced here: 57 us
  blocking collectives  17.5 us (31%)
  starting transfers between devices  16.7 us (29%)
  waiting for transfers between devices  10.4 us (18%)
  Pallas kernels  7.42 us (13%)
  between operations  2.73 us (5%)
  other arithmetic  1.26 us (2%)
  local copies, waits for them, and re-layouts  0.92 us (2%)
    all_to_all x1, blocking collectives, per_device(): total = lax.all_to_all(outs[8], 'prompt', 0, 0, tiled=True)  17.5 us
    ppermute x14, starting transfers between devices, swap(): lax.ppermute(array, 'sample', [(i, i ^ mask) for i in range(samples)])  16.7 us
    ppermute x14, waiting for transfers between devices, swap(): lax.ppermute(array, 'sample', [(i, i ^ mask) for i in range(samples)])  10.4 us
    pallas_call x1, Pallas kernels, per_device(): pl.pallas_call(functools.partial(grads_kernel, to_log2), out_shape=[shape...  3.49 us
    pallas_call x1, Pallas kernels, per_device(): pl.pallas_call(functools.partial(first_stats_kernel, to_log2, early), out...  1.53 us
    pallas_call x1, Pallas kernels, per_device(): pl.pallas_call(functools.partial(last_stats_kernel, to_log2, late), out_s...  1.49 us
  transfers between devices with their start and end apart: 14, of which 4 were waited for; matrix products, arithmetic and copies ran while one was open for 0% of the time, Pallas kernels for 3%

profile of v4, /device:TPU:4, one launch (start us, length us, event | category | flops | bytes accessed | tf_op | source)
XLA Modules:
  0.0 57.0 jit_solution(15248246512839990657)
XLA Ops:
  1.3 0.0 copy-start
  1.3 1.1 %maximum_maximum_fusion.refs_4_ = bf16[272,512]{1,0:T(8,128)(2,1)S(1)} fusion(bf16[128,512]{1,0:T(8,128)(2,1)} %bitcast.22, bf16[128,512]{1,0:T(8,128)(2,1)} %bitcast.23, bf16[272]{0:T(512)(128)(2,1)S(1)} %pad.4.clone), kind=kLoop, calls=%fused_computation | loop fusion | flops 835584 | bytes 541216 | tf_op jit(solution)/shard_map/concatenate | solution.py:245
  2.4 3.3 %collective-permute-start.4 = (bf16[272,512]{1,0:T(8,128)(2,1)S(1)}, bf16[272,512]{1,0:T(8,128)(2,1)S(1)}, u32[]{:S(2)}, u32[]{:S(2)}) collective-permute-start(bf16[272,512]{1,0:T(8,128)(2,1)S(1)} %maximum_maximum_fusion.refs_4_), channel_id=1, source_target_pairs={{0,4},{1,5},{2,6},{3,7},{4,0},{5,1},{6,2},{7,3},{8,12},{9,13},{10,... | collective-permute-start | bytes 835592 | tf_op jit(solution)/shard_map/ppermute | solution.py:239
  6.4 0.0 copy-done
  6.4 0.0 copy-start.1
  6.4 0.1 fusion
  6.5 0.8 %copy-done.1 = bf16[1,1,32,2048]{3,2,1,0:T(8,128)(2,1)S(1)} copy-done((bf16[1,1,32,2048]{3,2,1,0:T(8,128)(2,1)S(1)}, bf16[1,1,32,2048]{3,2,1,0:T(8,128)(2,1)}, u32[]{:S(2)}) %copy-start.1) | copy-done | bytes 131096
  7.3 0.0 copy-start.2
  7.3 0.0 copy-start.3
  7.3 0.6 %collective-permute-start.1 = (bf16[64,2048]{1,0:T(8,128)(2,1)S(1)}, bf16[64,2048]{1,0:T(8,128)(2,1)S(1)}, u32[]{:S(2)}, u32[]{:S(2)}) collective-permute-start(bf16[64,2048]{1,0:T(8,128)(2,1)S(1)} %pad_maximum_fusion.refs_0_), channel_id=1, source_target_pairs={{0,8},{1,9},{2,10},{3,11},{4,12},{5,13},{6,14},{7,15},{8,0},{9,1},... | collective-permute-start | bytes 786440 | tf_op jit(solution)/shard_map/ppermute | solution.py:239
  7.9 0.0 collective-permute-start
  7.9 1.1 %collective-permute-start.5 = (bf16[272,512]{1,0:T(8,128)(2,1)S(1)}, bf16[272,512]{1,0:T(8,128)(2,1)S(1)}, u32[]{:S(2)}, u32[]{:S(2)}) collective-permute-start(bf16[272,512]{1,0:T(8,128)(2,1)S(1)} %maximum_maximum_fusion.refs_4_), channel_id=1, source_target_pairs={{0,6},{1,7},{2,4},{3,5},{4,2},{5,3},{6,0},{7,1},{8,14},{9,15},{10,... | collective-permute-start | bytes 835592 | tf_op jit(solution)/shard_map/ppermute | solution.py:239
  9.0 1.0 %collective-permute-start.3 = (bf16[272,512]{1,0:T(8,128)(2,1)S(1)}, bf16[272,512]{1,0:T(8,128)(2,1)S(1)}, u32[]{:S(2)}, u32[]{:S(2)}) collective-permute-start(bf16[272,512]{1,0:T(8,128)(2,1)S(1)} %maximum_maximum_fusion.refs_4_), channel_id=1, source_target_pairs={{0,2},{1,3},{2,0},{3,1},{4,6},{5,7},{6,4},{7,5},{8,10},{9,11},{10,... | collective-permute-start | bytes 835592 | tf_op jit(solution)/shard_map/ppermute | solution.py:239
  10.6 0.1 stack.19.info_ref
  10.7 0.0 copy-done.2
  10.7 0.0 copy-done.3
  10.7 6.0 %collective-permute-done.1.refs_2_ = bf16[64,2048]{1,0:T(8,128)(2,1)S(1)} collective-permute-done((bf16[64,2048]{1,0:T(8,128)(2,1)S(1)}, bf16[64,2048]{1,0:T(8,128)(2,1)S(1)}, u32[]{:S(2)}, u32[]{:S(2)}) %collective-permute-start.1) | collective-permute-done | bytes 262176 | tf_op jit(solution)/shard_map/ppermute | solution.py:239
  16.7 0.0 collective-permute-start.2
  16.7 0.0 collective-permute-done.4.refs_0_
  16.7 0.0 collective-permute-done.refs_1_
  16.7 1.5 %collective-permute-done.2.refs_3_ = bf16[64,2048]{1,0:T(8,128)(2,1)S(1)} collective-permute-done((bf16[64,2048]{1,0:T(8,128)(2,1)S(1)}, bf16[64,2048]{1,0:T(8,128)(2,1)S(1)}, u32[]{:S(2)}, u32[]{:S(2)}) %collective-permute-start.2) | collective-permute-done | bytes 262176 | tf_op jit(solution)/shard_map/ppermute | solution.py:239
  18.2 1.5 %stats_first.1.refs_8_ = f32[16,512]{1,0:T(8,128)S(1)} custom-call(s32[5]{0:T(128)S(1)} %stack.19.info_ref, bf16[64,2048]{1,0:T(8,128)(2,1)S(1)} %pad_maximum_fusion.refs_0_, bf16[64,2048]{1,0:T(8,128)(2,1)S(1)} %collective-permute-done.refs_1_, bf16[64,2048]{1,0:T(8,128)(2,1)S(1)} %collective-permute-done.1.refs_2_, ...), custom_call_target="tpu_custom_call" | custom-call | tf_op jit(solution)/shard_map/stats_first/pallas_call | solution.py:266
  19.8 0.0 collective-permute-done.5.refs_7_
  19.8 0.0 collective-permute-done.3.refs_5_
  19.8 1.5 %stats.1.refs_9_ = f32[56,128]{1,0:T(8,128)S(1)} custom-call(s32[5]{0:T(128)S(1)} %stack.19.info_ref, bf16[64,2048]{1,0:T(8,128)(2,1)S(1)} %pad_maximum_fusion.refs_0_, bf16[64,2048]{1,0:T(8,128)(2,1)S(1)} %collective-permute-done.refs_1_, bf16[64,2048]{1,0:T(8,128)(2,1)S(1)} %collective-permute-done.1.refs_2_, ...), custom_call_target="tpu_custom_call" | custom-call | tf_op jit(solution)/shard_map/stats/pallas_call | solution.py:274
  21.3 0.9 %collective-permute-start.8 = (f32[56,128]{1,0:T(8,128)S(1)}, f32[56,128]{1,0:T(8,128)S(1)}, u32[]{:S(2)}, u32[]{:S(2)}) collective-permute-start(f32[56,128]{1,0:T(8,128)S(1)} %stats.1.refs_9_), channel_id=1, source_target_pairs={{0,9},{1,8},{2,11},{3,10},{4,13},{5,12},{6,15},{7,14},{8,1},{9,0},... | collective-permute-start | bytes 86024 | tf_op jit(solution)/shard_map/ppermute | solution.py:239
  22.1 2.5 %collective-permute-start.7 = (f32[56,128]{1,0:T(8,128)S(1)}, f32[56,128]{1,0:T(8,128)S(1)}, u32[]{:S(2)}, u32[]{:S(2)}) collective-permute-start(f32[56,128]{1,0:T(8,128)S(1)} %stats.1.refs_9_), channel_id=1, source_target_pairs={{0,8},{1,9},{2,10},{3,11},{4,12},{5,13},{6,14},{7,15},{8,0},{9,1},... | collective-permute-start | bytes 86024 | tf_op jit(solution)/shard_map/ppermute | solution.py:239
  24.7 0.1 collective-permute-start.6
  24.7 1.4 %collective-permute-done.8.refs_12_ = f32[56,128]{1,0:T(8,128)S(1)} collective-permute-done((f32[56,128]{1,0:T(8,128)S(1)}, f32[56,128]{1,0:T(8,128)S(1)}, u32[]{:S(2)}, u32[]{:S(2)}) %collective-permute-start.8) | collective-permute-done | bytes 28704 | tf_op jit(solution)/shard_map/ppermute | solution.py:239
  26.2 1.5 %collective-permute-done.7.refs_11_ = f32[56,128]{1,0:T(8,128)S(1)} collective-permute-done((f32[56,128]{1,0:T(8,128)S(1)}, f32[56,128]{1,0:T(8,128)S(1)}, u32[]{:S(2)}, u32[]{:S(2)}) %collective-permute-start.7) | collective-permute-done | bytes 28704 | tf_op jit(solution)/shard_map/ppermute | solution.py:239
  27.6 0.0 collective-permute-done.6.refs_10_
  27.6 3.5 %grads.1 = (f32[512,128]{1,0:T(8,128)S(1)}, f32[512,128]{1,0:T(8,128)S(1)}, bf16[1024,128]{1,0:T(8,128)(2,1)S(1)}, f32[1024,128]{1,0:T(8,128)S(1)}, bf16[1024,12...) custom-call(s32[5]{0:T(128)S(1)} %stack.19.info_ref, ...), custom_call_target="tpu_custom_call" | custom-call | tf_op jit(solution)/shard_map/grads/pallas_call | solution.py:285
  31.1 0.1 collective-permute-start.9
  31.2 0.2 collective-permute-start.11
  31.5 2.9 %collective-permute-start.12 = (bf16[1024,128]{1,0:T(8,128)(2,1)S(1)}, bf16[1024,128]{1,0:T(8,128)(2,1)S(1)}, u32[]{:S(2)}, u32[]{:S(2)}) collective-permute-start(bf16[1024,128]{1,0:T(8,128)(2,1)S(1)} %get-tuple-element.24), channel_id=1, source_target_pairs={{0,4},{1,5},{2,6},{3,7},{4,0},{5,1},{6,2},{7,3},{8,12},{9,13},{10,... | collective-permute-start | bytes 786440 | tf_op jit(solution)/shard_map/ppermute | solution.py:239
  34.3 1.7 %collective-permute-start.13 = (bf16[1024,128]{1,0:T(8,128)(2,1)S(1)}, bf16[1024,128]{1,0:T(8,128)(2,1)S(1)}, u32[]{:S(2)}, u32[]{:S(2)}) collective-permute-start(bf16[1024,128]{1,0:T(8,128)(2,1)S(1)} %get-tuple-element.25), channel_id=1, source_target_pairs={{0,6},{1,7},{2,4},{3,5},{4,2},{5,3},{6,0},{7,1},{8,14},{9,15},{10,... | collective-permute-start | bytes 786440 | tf_op jit(solution)/shard_map/ppermute | solution.py:239
  36.0 0.0 collective-permute-done.9.refs_1_
  36.1 2.5 %collective-permute-start.10 = (bf16[512,128]{1,0:T(8,128)(2,1)S(1)}, bf16[512,128]{1,0:T(8,128)(2,1)S(1)}, u32[]{:S(2)}, u32[]{:S(2)}) collective-permute-start(bf16[512,128]{1,0:T(8,128)(2,1)S(1)} %add_convert_fusion), channel_id=1, source_target_pairs={{0,8},{1,9},{2,10},{3,11},{4,12},{5,13},{6,14},{7,15},{8,0},{9,1},... | collective-permute-start | bytes 393224 | tf_op jit(solution)/shard_map/ppermute | solution.py:239
  38.5 17.5 %all_to_all.5.refs_8_ = f32[16,1,128]{2,1,0:T(1,128)S(1)} all-to-all(f32[16,1,128]{2,1,0:T(1,128)S(1)} %get-tuple-element.27), channel_id=1, replica_groups=mesh['prompt'=16,'sample'=16] {'prompt'}, dimensions={0} | all-to-all | bytes 16384 | tf_op jit(solution)/shard_map/all_to_all | solution.py:303
  56.0 0.0 collective-permute-done.11.refs_4_
  56.0 0.0 collective-permute-done.12.refs_5_
  56.0 0.0 collective-permute-done.13.refs_6_
  56.1 0.0 collective-permute-done.10.refs_2_
  56.1 0.9 %finish.1 = (bf16[32,2048]{1,0:T(8,128)(2,1)}, bf16[128,512]{1,0:T(8,128)(2,1)}, bf16[128,512]{1,0:T(8,128)(2,1)}, bf16[32,512]{1,0:T(8,128)(2,1)}, bf16[32,512]{1,0:T(8,128)(2,1)}) custom-call(f32[512,128]{1,0:T(8,128)S(1)} %get-tuple-element.19.refs_0_, bf16[1024,128]{1,0:T(8,128)(2,1)S(1)} %collective-permute-done.9.refs_1_, ...), custom_call_target="tpu_custom_call" | custom-call | tf_op jit(solution)/shard_map/finish/pallas_call | solution.py:305
  (7 shorter events, 0.1 us)
Async XLA Ops:
  1.3 5.1 %copy-start = (bf16[1,1,32,2048]{3,2,1,0:T(8,128)(2,1)S(1)}, bf16[1,1,32,2048]{3,2,1,0:T(8,128)(2,1)}, u32[]{:S(2)}) copy-start(bf16[1,1,32,2048]{3,2,1,0:T(8,128)(2,1)} %param.10) | copy-start | bytes 393220
  2.4 14.3 %collective-permute-start.4 = (bf16[272,512]{1,0:T(8,128)(2,1)S(1)}, bf16[272,512]{1,0:T(8,128)(2,1)S(1)}, u32[]{:S(2)}, u32[]{:S(2)}) collective-permute-start(bf16[272,512]{1,0:T(8,128)(2,1)S(1)} %maximum_maximum_fusion.refs_4_), channel_id=1, source_target_pairs={{0,4},{1,5},{2,6},{3,7},{4,0},{5,1},{6,2},{7,3},{8,12},{9,13},{10,... | collective-permute-start | bytes 835592 | tf_op jit(solution)/shard_map/ppermute | solution.py:239
  6.4 0.9 %copy-start.1 = (bf16[1,1,32,2048]{3,2,1,0:T(8,128)(2,1)S(1)}, bf16[1,1,32,2048]{3,2,1,0:T(8,128)(2,1)}, u32[]{:S(2)}) copy-start(bf16[1,1,32,2048]{3,2,1,0:T(8,128)(2,1)} %param.9) | copy-start | bytes 393220
  7.3 3.4 %copy-start.2 = (bf16[1,1,32,512]{3,2,1,0:T(8,128)(2,1)S(1)}, bf16[1,1,32,512]{3,2,1,0:T(8,128)(2,1)}, u32[]{:S(2)}) copy-start(bf16[1,1,32,512]{3,2,1,0:T(8,128)(2,1)} %param.16) | copy-start | bytes 98308
  7.3 3.4 %copy-start.3 = (bf16[1,1,32,512]{3,2,1,0:T(8,128)(2,1)S(1)}, bf16[1,1,32,512]{3,2,1,0:T(8,128)(2,1)}, u32[]{:S(2)}) copy-start(bf16[1,1,32,512]{3,2,1,0:T(8,128)(2,1)} %param.15) | copy-start | bytes 98308
  7.3 9.4 %collective-permute-start.1 = (bf16[64,2048]{1,0:T(8,128)(2,1)S(1)}, bf16[64,2048]{1,0:T(8,128)(2,1)S(1)}, u32[]{:S(2)}, u32[]{:S(2)}) collective-permute-start(bf16[64,2048]{1,0:T(8,128)(2,1)S(1)} %pad_maximum_fusion.refs_0_), channel_id=1, source_target_pairs={{0,8},{1,9},{2,10},{3,11},{4,12},{5,13},{6,14},{7,15},{8,0},{9,1},... | collective-permute-start | bytes 786440 | tf_op jit(solution)/shard_map/ppermute | solution.py:239
  7.9 8.8 %collective-permute-start = (bf16[64,2048]{1,0:T(8,128)(2,1)S(1)}, bf16[64,2048]{1,0:T(8,128)(2,1)S(1)}, u32[]{:S(2)}, u32[]{:S(2)}) collective-permute-start(bf16[64,2048]{1,0:T(8,128)(2,1)S(1)} %pad_maximum_fusion.refs_0_), channel_id=1, source_target_pairs={{0,1},{1,0},{2,3},{3,2},{4,5},{5,4},{6,7},{7,6},{8,9},{9,8},{10,11... | collective-permute-start | bytes 786440 | tf_op jit(solution)/shard_map/ppermute | solution.py:239
  7.9 11.8 %collective-permute-start.5 = (bf16[272,512]{1,0:T(8,128)(2,1)S(1)}, bf16[272,512]{1,0:T(8,128)(2,1)S(1)}, u32[]{:S(2)}, u32[]{:S(2)}) collective-permute-start(bf16[272,512]{1,0:T(8,128)(2,1)S(1)} %maximum_maximum_fusion.refs_4_), channel_id=1, source_target_pairs={{0,6},{1,7},{2,4},{3,5},{4,2},{5,3},{6,0},{7,1},{8,14},{9,15},{10,... | collective-permute-start | bytes 835592 | tf_op jit(solution)/shard_map/ppermute | solution.py:239
  9.0 10.8 %collective-permute-start.3 = (bf16[272,512]{1,0:T(8,128)(2,1)S(1)}, bf16[272,512]{1,0:T(8,128)(2,1)S(1)}, u32[]{:S(2)}, u32[]{:S(2)}) collective-permute-start(bf16[272,512]{1,0:T(8,128)(2,1)S(1)} %maximum_maximum_fusion.refs_4_), channel_id=1, source_target_pairs={{0,2},{1,3},{2,0},{3,1},{4,6},{5,7},{6,4},{7,5},{8,10},{9,11},{10,... | collective-permute-start | bytes 835592 | tf_op jit(solution)/shard_map/ppermute | solution.py:239
  16.7 1.5 %collective-permute-start.2 = (bf16[64,2048]{1,0:T(8,128)(2,1)S(1)}, bf16[64,2048]{1,0:T(8,128)(2,1)S(1)}, u32[]{:S(2)}, u32[]{:S(2)}) collective-permute-start(bf16[64,2048]{1,0:T(8,128)(2,1)S(1)} %collective-permute-done.1.refs_2_), channel_id=1, source_target_pairs={{0,1},{1,0},{2,3},{3,2},{4,5},{5,4},{6,7},{7,6},{8,9},{9,8},{10,11... | collective-permute-start | bytes 786440 | tf_op jit(solution)/shard_map/ppermute | solution.py:239
  21.3 4.9 %collective-permute-start.8 = (f32[56,128]{1,0:T(8,128)S(1)}, f32[56,128]{1,0:T(8,128)S(1)}, u32[]{:S(2)}, u32[]{:S(2)}) collective-permute-start(f32[56,128]{1,0:T(8,128)S(1)} %stats.1.refs_9_), channel_id=1, source_target_pairs={{0,9},{1,8},{2,11},{3,10},{4,13},{5,12},{6,15},{7,14},{8,1},{9,0},... | collective-permute-start | bytes 86024 | tf_op jit(solution)/shard_map/ppermute | solution.py:239
  22.1 5.5 %collective-permute-start.7 = (f32[56,128]{1,0:T(8,128)S(1)}, f32[56,128]{1,0:T(8,128)S(1)}, u32[]{:S(2)}, u32[]{:S(2)}) collective-permute-start(f32[56,128]{1,0:T(8,128)S(1)} %stats.1.refs_9_), channel_id=1, source_target_pairs={{0,8},{1,9},{2,10},{3,11},{4,12},{5,13},{6,14},{7,15},{8,0},{9,1},... | collective-permute-start | bytes 86024 | tf_op jit(solution)/shard_map/ppermute | solution.py:239
  24.7 3.0 %collective-permute-start.6 = (f32[56,128]{1,0:T(8,128)S(1)}, f32[56,128]{1,0:T(8,128)S(1)}, u32[]{:S(2)}, u32[]{:S(2)}) collective-permute-start(f32[56,128]{1,0:T(8,128)S(1)} %stats.1.refs_9_), channel_id=1, source_target_pairs={{0,1},{1,0},{2,3},{3,2},{4,5},{5,4},{6,7},{7,6},{8,9},{9,8},{10,11... | collective-permute-start | bytes 86024 | tf_op jit(solution)/shard_map/ppermute | solution.py:239
  31.1 4.9 %collective-permute-start.9 = (bf16[1024,128]{1,0:T(8,128)(2,1)S(1)}, bf16[1024,128]{1,0:T(8,128)(2,1)S(1)}, u32[]{:S(2)}, u32[]{:S(2)}) collective-permute-start(bf16[1024,128]{1,0:T(8,128)(2,1)S(1)} %get-tuple-element.20), channel_id=1, source_target_pairs={{0,1},{1,0},{2,3},{3,2},{4,5},{5,4},{6,7},{7,6},{8,9},{9,8},{10,11... | collective-permute-start | bytes 786440 | tf_op jit(solution)/shard_map/ppermute | solution.py:239
  31.2 24.8 %collective-permute-start.11 = (bf16[1024,128]{1,0:T(8,128)(2,1)S(1)}, bf16[1024,128]{1,0:T(8,128)(2,1)S(1)}, u32[]{:S(2)}, u32[]{:S(2)}) collective-permute-start(bf16[1024,128]{1,0:T(8,128)(2,1)S(1)} %get-tuple-element.23), channel_id=1, source_target_pairs={{0,2},{1,3},{2,0},{3,1},{4,6},{5,7},{6,4},{7,5},{8,10},{9,11},{10,... | collective-permute-start | bytes 786440 | tf_op jit(solution)/shard_map/ppermute | solution.py:239
  31.5 24.6 %collective-permute-start.12 = (bf16[1024,128]{1,0:T(8,128)(2,1)S(1)}, bf16[1024,128]{1,0:T(8,128)(2,1)S(1)}, u32[]{:S(2)}, u32[]{:S(2)}) collective-permute-start(bf16[1024,128]{1,0:T(8,128)(2,1)S(1)} %get-tuple-element.24), channel_id=1, source_target_pairs={{0,4},{1,5},{2,6},{3,7},{4,0},{5,1},{6,2},{7,3},{8,12},{9,13},{10,... | collective-permute-start | bytes 786440 | tf_op jit(solution)/shard_map/ppermute | solution.py:239
  34.3 21.7 %collective-permute-start.13 = (bf16[1024,128]{1,0:T(8,128)(2,1)S(1)}, bf16[1024,128]{1,0:T(8,128)(2,1)S(1)}, u32[]{:S(2)}, u32[]{:S(2)}) collective-permute-start(bf16[1024,128]{1,0:T(8,128)(2,1)S(1)} %get-tuple-element.25), channel_id=1, source_target_pairs={{0,6},{1,7},{2,4},{3,5},{4,2},{5,3},{6,0},{7,1},{8,14},{9,15},{10,... | collective-permute-start | bytes 786440 | tf_op jit(solution)/shard_map/ppermute | solution.py:239
  36.1 20.0 %collective-permute-start.10 = (bf16[512,128]{1,0:T(8,128)(2,1)S(1)}, bf16[512,128]{1,0:T(8,128)(2,1)S(1)}, u32[]{:S(2)}, u32[]{:S(2)}) collective-permute-start(bf16[512,128]{1,0:T(8,128)(2,1)S(1)} %add_convert_fusion), channel_id=1, source_target_pairs={{0,8},{1,9},{2,10},{3,11},{4,12},{5,13},{6,14},{7,15},{8,0},{9,1},... | collective-permute-start | bytes 393224 | tf_op jit(solution)/shard_map/ppermute | solution.py:239

commit v5 on v4

--- a/solution.py
+++ b/solution.py
@@ -46,8 +46,7 @@
 
 
 def with_own(blocks, own_ref, part, g):
-    tokens = own_ref.shape[0] // 2
-    own = own_ref[part * tokens : (part + 1) * tokens, g * HD : (g + 1) * HD]
+    own = own_ref[part][:, g * HD : (g + 1) * HD]
     return jnp.concatenate([cols_of(blocks, part, g), own], axis=0)
 
 
@@ -74,10 +73,10 @@
 
 
 def first_stats_kernel(to_log2, where, info_ref, *refs):
-    qg, kvs, own_ref, out_ref = refs[0:4], refs[4:-2], refs[-2], refs[-1]
+    qg, kvs, own_ref, out_ref = refs[0:4], refs[4:-3], refs[-3:-1], refs[-1]
     block = (kvs[0].shape[0] - 16) // 2
     groups = kvs[0].shape[1] // HD
-    tokens = own_ref.shape[0] // 2
+    tokens = own_ref[0].shape[0]
     rows = qg[0].shape[1] // HD // groups * tokens
     bias = jnp.concatenate([block_bias(info_ref, k, block) for k in where], axis=0)
     own = own_bias(tokens, rows)
@@ -112,18 +111,34 @@
                 out_ref[at : at + 1, :] = got[i][:, s * rows : (s + 1) * rows]
 
 
-def grads_kernel(to_log2, info_ref, *refs):
-    qg, kvs, own_ref = refs[0:4], refs[4:8], refs[8]
-    stats = refs[9:13]
-    dq_own, dq_far, dq_sib, dkv_own = refs[13:17]
-    dkv_out = refs[17:20]
-    own_out, tot_out = refs[20:22]
+def terms_kernel(to_log2, info_ref, *refs):
+    qg, kvs, own_ref, score_out, slope_out = refs[0:4], refs[4:8], refs[8:10], refs[10], refs[11]
     block = (kvs[0].shape[0] - 16) // 2
     groups = kvs[0].shape[1] // HD
-    tokens = own_ref.shape[0] // 2
+    tokens = own_ref[0].shape[0]
     rows = qg[0].shape[1] // HD // groups * tokens
     bias = jnp.concatenate([block_bias(info_ref, k, block) for k in range(4)], axis=0)
     own_rows = own_bias(tokens, rows)
+    size = 4 * block + tokens
+    for g in range(groups):
+        at = slice(g * size, (g + 1) * size)
+        score = dot(with_own(kvs, own_ref, 0, g), rows_of(qg, 0, g), NT) * to_log2
+        score_out[at, :] = add_bias(score, bias, own_rows)
+        slope_out[at, :] = dot(with_own(kvs, own_ref, 1, g), rows_of(qg, 1, g), NT)
+
+
+def grads_kernel(*refs):
+    qg, kvs, own_ref = refs[0:4], refs[4:8], refs[8:10]
+    score_ref, slope_ref = refs[10:12]
+    stats = refs[12:16]
+    dq_own, dq_far, dq_sib, dkv_own = refs[16:20]
+    dkv_out = refs[20:23]
+    own_out, tot_out = refs[23:25]
+    block = (kvs[0].shape[0] - 16) // 2
+    groups = kvs[0].shape[1] // HD
+    tokens = own_ref[0].shape[0]
+    rows = qg[0].shape[1] // HD // groups * tokens
+    size = 4 * block + tokens
     shifts, means = [], []
     for s in range(4):
         tops = [stats[e][(s ^ e) * 4 : (s ^ e) * 4 + 4, :] for e in range(4)]
@@ -146,10 +161,9 @@
         w = rows_of(qg, 1, g)
         k = with_own(kvs, own_ref, 0, g)
         sh, mn = shift[g : g + 1, :], mean[g : g + 1, :]
-        score = add_bias(dot(k, q, NT) * to_log2, bias, own_rows)
-        slope = dot(with_own(kvs, own_ref, 1, g), w, NT)
-        p = jnp.exp2(score - sh)
-        ds = (p * (slope - mn)).astype(jnp.bfloat16)
+        span = slice(g * size, (g + 1) * size)
+        p = jnp.exp2(score_ref[span, :] - sh)
+        ds = (p * (slope_ref[span, :] - mn)).astype(jnp.bfloat16)
         dv = dot(p.astype(jnp.bfloat16), w, NN)
         dk = dot(ds, q, NN)
         dq = dot(k.T, ds, NN)
@@ -238,13 +252,14 @@
     def swap(array, mask):
         return lax.ppermute(array, "sample", [(i, i ^ mask) for i in range(samples)])
 
-    at = lax.broadcasted_iota(jnp.int32, (tokens, width), 0)
-    weight = jnp.where(at < comp_len[0, 0], advantage[0, 0], 0.0)
-    weighted = (out_grad[0, 0].astype(f32) * weight).astype(bf16)
+    at = lax.broadcasted_iota(jnp.int32, (2 * tokens, width), 0)
+    weight = jnp.where(at - tokens < comp_len[0, 0], advantage[0, 0], 0.0)
+    weight = jnp.where(at < tokens, 1.0, weight)
+    qg0 = jnp.concatenate([queries[0, 0], out_grad[0, 0]], axis=0)
+    qg0 = (qg0.astype(f32) * weight).astype(bf16)
     mark = jnp.broadcast_to(comp_len.astype(bf16), (16, kv_width))
     kv0 = jnp.concatenate([prefix_keys[0], prefix_values[0], mark], axis=0)
-    qg0 = jnp.concatenate([queries[0, 0], weighted], axis=0)
-    own = jnp.concatenate([own_keys[0, 0], own_values[0, 0]], axis=0)
+    own = [own_keys[0, 0], own_values[0, 0]]
     qg2 = swap(qg0, 8)
     kv = [kv0] + [swap(kv0, 2 * e) for e in (1, 2, 3)]
     kv[2], = pl.pallas_call(
@@ -266,11 +281,11 @@
     first = pl.pallas_call(
         functools.partial(first_stats_kernel, to_log2, early),
         out_shape=shape((16, width * 4 * tokens // HD // groups), f32),
-        in_specs=[smem] + [vmem] * (5 + len(early)),
+        in_specs=[smem] + [vmem] * (6 + len(early)),
         out_specs=vmem,
         compiler_params=params,
         name="stats_first",
-    )(info, *qg, *[kv[k] for k in early], own)
+    )(info, *qg, *[kv[k] for k in early], *own)
     stats0 = pl.pallas_call(
         functools.partial(last_stats_kernel, to_log2, late),
         out_shape=shape((56, HD), f32),
@@ -280,10 +295,19 @@
         name="stats",
     )(info, *qg, *kv, first)
     stats = [stats0, swap(stats0, 1), swap(stats0, 8), swap(stats0, 9)]
+    term_shape = shape((groups * (4 * block + tokens), width * 4 * tokens // HD // groups), f32)
+    terms = pl.pallas_call(
+        functools.partial(terms_kernel, to_log2),
+        out_shape=[term_shape] * 2,
+        in_specs=[smem] + [vmem] * 10,
+        out_specs=[vmem] * 2,
+        compiler_params=params,
+        name="terms",
+    )(info, *qg, *kv, *own)
     kv_rows = 2 * groups * block
     dq_rows = width // HD // 4 * HD
     outs = pl.pallas_call(
-        functools.partial(grads_kernel, to_log2),
+        grads_kernel,
         out_shape=[
             shape((dq_rows, HD), f32),
             shape((dq_rows, HD), f32),
@@ -292,11 +316,11 @@
         ]
         + [shape((kv_rows, HD), bf16)] * 3
         + [shape((2 * tokens, kv_width), f32), shape((prompts, 1, HD), f32)],
-        in_specs=[smem] + [vmem] * 13,
+        in_specs=[vmem] * 16,
         out_specs=[vmem] * 9,
         compiler_params=params,
         name="grads",
-    )(info, *qg, *kv, own, *stats)
+    )(*qg, *kv, *own, *terms, *stats)
     dq_own, dq_far, dq_sib, dkv_own = outs[:4]
     dq_core = swap(dq_sib, 1)
     dq_x = swap((dq_far + dq_core[dq_rows:].astype(f32)).astype(bf16), 8)

time: 57.2 us -> 55.7 us (0.974)
  waiting for transfers between devices: 10.4 us -> 8.55 us
  other arithmetic: 1.26 us -> 2.21 us
  local copies, waits for them, and re-layouts: 0.92 us -> 0.1 us
    ppermute x14, waiting for transfers between devices: 10.4 us -> 8.55 us  [swap(): lax.ppermute(array, 'sample', [(i, i ^ mask) for i in range(samples)])]
    convert_element_type x1, other arithmetic: 0.09 us -> 1.09 us  [per_device(): qg0 = (qg0.astype(f32) * weight).astype(bf16)]
    unnamed x8 -> x4, local copies, waits for them, and re-layouts: 0.82 us -> 0.01 us
    pallas_call x1 -> x2, Pallas kernels: 3.49 us -> 3.73 us  [the longest x1 1.87 us: per_device(): pl.pallas_call(functools.partial(terms_kernel, to_log2), out_shape=[term_...]
  transfers between devices with their start and end apart: 14 -> 14, of which waited for: 4 -> 3; matrix products, arithmetic and copies ran while one was open for 0% -> 2% of each run, Pallas kernels for 3% -> 6%
where the time goes in v5:
time: 55.7 us; the launch traced here: 55.5 us
  blocking collectives  17.5 us (31%)
  starting transfers between devices  16.7 us (30%)
  waiting for transfers between devices  8.55 us (15%)
  Pallas kernels  7.68 us (14%)
  between operations  2.71 us (5%)
  other arithmetic  2.21 us (4%)
    all_to_all x1, blocking collectives, per_device(): total = lax.all_to_all(outs[8], 'prompt', 0, 0, tiled=True)  17.5 us
    ppermute x14, starting transfers between devices, swap(): lax.ppermute(array, 'sample', [(i, i ^ mask) for i in range(samples)])  16.7 us
    ppermute x14, waiting for transfers between devices, swap(): lax.ppermute(array, 'sample', [(i, i ^ mask) for i in range(samples)])  8.55 us
    pallas_call x1, Pallas kernels, per_device(): pl.pallas_call(functools.partial(terms_kernel, to_log2), out_shape=[term_...  1.87 us
    pallas_call x1, Pallas kernels, per_device(): pl.pallas_call(grads_kernel, out_shape=[shape((dq_rows, HD), f32), shape(...  1.85 us
    pallas_call x1, Pallas kernels, per_device(): pl.pallas_call(functools.partial(first_stats_kernel, to_log2, early), out...  1.54 us
    pallas_call x1, Pallas kernels, per_device(): pl.pallas_call(functools.partial(last_stats_kernel, to_log2, late), out_s...  1.51 us
  transfers between devices with their start and end apart: 14, of which 3 were waited for; matrix products, arithmetic and copies ran while one was open for 2% of the time, Pallas kernels for 6%

profile of v5, /device:TPU:4, one launch (start us, length us, event | category | flops | bytes accessed | tf_op | source)
XLA Modules:
  0.0 55.5 jit_solution(11090854435344511568)
XLA Ops:
  1.3 1.1 %maximum_maximum_fusion.refs_4_ = bf16[272,512]{1,0:T(8,128)(2,1)S(1)} fusion(bf16[128,512]{1,0:T(8,128)(2,1)} %bitcast.26, bf16[128,512]{1,0:T(8,128)(2,1)} %bitcast.27, bf16[272]{0:T(512)(128)(2,1)S(1)} %pad.2.clone), kind=kLoop, calls=%fused_computation.1 | loop fusion | flops 835584 | bytes 541216 | tf_op jit(solution)/shard_map/concatenate | solution.py:261
  2.4 3.3 %collective-permute-start.4 = (bf16[272,512]{1,0:T(8,128)(2,1)S(1)}, bf16[272,512]{1,0:T(8,128)(2,1)S(1)}, u32[]{:S(2)}, u32[]{:S(2)}) collective-permute-start(bf16[272,512]{1,0:T(8,128)(2,1)S(1)} %maximum_maximum_fusion.refs_4_), channel_id=1, source_target_pairs={{0,4},{1,5},{2,6},{3,7},{4,0},{5,1},{6,2},{7,3},{8,12},{9,13},{10,... | collective-permute-start | bytes 835592 | tf_op jit(solution)/shard_map/ppermute | solution.py:253
  6.3 1.1 %multiply_convert_fusion.refs_0_ = bf16[64,2048]{1,0:T(8,128)(2,1)S(1)} fusion(bf16[32,2048]{1,0:T(8,128)(2,1)} %bitcast.28, bf16[32,2048]{1,0:T(8,128)(2,1)} %bitcast.29, f32[64]{0:T(128)S(1)} %compare_select_fusion, pred[64]{0:T(512)(128)(4,1)S(1)} %iota_compare_fusion), kind=kLoop, calls=%fused_computation | loop fusion | flops 917504 | bytes 524608 | tf_op jit(solution)/shard_map/convert_element_type | solution.py:259
  7.4 0.6 %collective-permute-start.1 = (bf16[64,2048]{1,0:T(8,128)(2,1)S(1)}, bf16[64,2048]{1,0:T(8,128)(2,1)S(1)}, u32[]{:S(2)}, u32[]{:S(2)}) collective-permute-start(bf16[64,2048]{1,0:T(8,128)(2,1)S(1)} %multiply_convert_fusion.refs_0_), channel_id=1, source_target_pairs={{0,8},{1,9},{2,10},{3,11},{4,12},{5,13},{6,14},{7,15},{8,0},{9,1},... | collective-permute-start | bytes 786440 | tf_op jit(solution)/shard_map/ppermute | solution.py:253
  8.0 0.0 collective-permute-start
  8.0 1.1 %collective-permute-start.5 = (bf16[272,512]{1,0:T(8,128)(2,1)S(1)}, bf16[272,512]{1,0:T(8,128)(2,1)S(1)}, u32[]{:S(2)}, u32[]{:S(2)}) collective-permute-start(bf16[272,512]{1,0:T(8,128)(2,1)S(1)} %maximum_maximum_fusion.refs_4_), channel_id=1, source_target_pairs={{0,6},{1,7},{2,4},{3,5},{4,2},{5,3},{6,0},{7,1},{8,14},{9,15},{10,... | collective-permute-start | bytes 835592 | tf_op jit(solution)/shard_map/ppermute | solution.py:253
  9.1 1.0 %collective-permute-start.3 = (bf16[272,512]{1,0:T(8,128)(2,1)S(1)}, bf16[272,512]{1,0:T(8,128)(2,1)S(1)}, u32[]{:S(2)}, u32[]{:S(2)}) collective-permute-start(bf16[272,512]{1,0:T(8,128)(2,1)S(1)} %maximum_maximum_fusion.refs_4_), channel_id=1, source_target_pairs={{0,2},{1,3},{2,0},{3,1},{4,6},{5,7},{6,4},{7,5},{8,10},{9,11},{10,... | collective-permute-start | bytes 835592 | tf_op jit(solution)/shard_map/ppermute | solution.py:253
  10.7 0.1 stack.19.info_ref
  10.8 0.0 copy-start
  10.8 0.0 copy-start.1
  10.8 6.0 %collective-permute-done.1.refs_2_ = bf16[64,2048]{1,0:T(8,128)(2,1)S(1)} collective-permute-done((bf16[64,2048]{1,0:T(8,128)(2,1)S(1)}, bf16[64,2048]{1,0:T(8,128)(2,1)S(1)}, u32[]{:S(2)}, u32[]{:S(2)}) %collective-permute-start.1) | collective-permute-done | bytes 262176 | tf_op jit(solution)/shard_map/ppermute | solution.py:253
  16.8 0.0 collective-permute-start.2
  16.8 0.0 collective-permute-done.4.refs_0_
  16.8 0.0 collective-permute-done.refs_1_
  16.8 1.5 %collective-permute-done.2.refs_3_ = bf16[64,2048]{1,0:T(8,128)(2,1)S(1)} collective-permute-done((bf16[64,2048]{1,0:T(8,128)(2,1)S(1)}, bf16[64,2048]{1,0:T(8,128)(2,1)S(1)}, u32[]{:S(2)}, u32[]{:S(2)}) %collective-permute-start.2) | collective-permute-done | bytes 262176 | tf_op jit(solution)/shard_map/ppermute | solution.py:253
  18.3 0.0 copy-done
  18.3 0.0 copy-done.1
  18.3 1.5 %stats_first.1.refs_8_ = f32[16,512]{1,0:T(8,128)S(1)} custom-call(s32[5]{0:T(128)S(1)} %stack.19.info_ref, bf16[64,2048]{1,0:T(8,128)(2,1)S(1)} %multiply_convert_fusion.refs_0_, bf16[64,2048]{1,0:T(8,128)(2,1)S(1)} %collective-permute-done.refs_1_, bf16[64,2048]{1,0:T(8,128)(2,1)S(1)} %collective-permute-done.1.refs_2_, ...), custom_call_target="tpu_custom_call" | custom-call | tf_op jit(solution)/shard_map/stats_first/pallas_call | solution.py:281
  19.9 0.0 collective-permute-done.5.refs_7_
  19.9 0.0 collective-permute-done.3.refs_5_
  19.9 1.5 %stats.1.refs_12_ = f32[56,128]{1,0:T(8,128)S(1)} custom-call(s32[5]{0:T(128)S(1)} %stack.19.info_ref, bf16[64,2048]{1,0:T(8,128)(2,1)S(1)} %multiply_convert_fusion.refs_0_, bf16[64,2048]{1,0:T(8,128)(2,1)S(1)} %collective-permute-done.refs_1_, bf16[64,2048]{1,0:T(8,128)(2,1)S(1)} %collective-permute-done.1.refs_2_, ...), custom_call_target="tpu_custom_call" | custom-call | tf_op jit(solution)/shard_map/stats/pallas_call | solution.py:289
  21.4 0.9 %collective-permute-start.8 = (f32[56,128]{1,0:T(8,128)S(1)}, f32[56,128]{1,0:T(8,128)S(1)}, u32[]{:S(2)}, u32[]{:S(2)}) collective-permute-start(f32[56,128]{1,0:T(8,128)S(1)} %stats.1.refs_12_), channel_id=1, source_target_pairs={{0,9},{1,8},{2,11},{3,10},{4,13},{5,12},{6,15},{7,14},{8,1},{9,0},... | collective-permute-start | bytes 86024 | tf_op jit(solution)/shard_map/ppermute | solution.py:253
  22.3 2.5 %collective-permute-start.7 = (f32[56,128]{1,0:T(8,128)S(1)}, f32[56,128]{1,0:T(8,128)S(1)}, u32[]{:S(2)}, u32[]{:S(2)}) collective-permute-start(f32[56,128]{1,0:T(8,128)S(1)} %stats.1.refs_12_), channel_id=1, source_target_pairs={{0,8},{1,9},{2,10},{3,11},{4,12},{5,13},{6,14},{7,15},{8,0},{9,1},... | collective-permute-start | bytes 86024 | tf_op jit(solution)/shard_map/ppermute | solution.py:253
  24.8 0.1 collective-permute-start.6
  24.9 1.9 %terms.1 = (f32[2176,512]{1,0:T(8,128)S(1)}, f32[2176,512]{1,0:T(8,128)S(1)}) custom-call(s32[5]{0:T(128)S(1)} %stack.19.info_ref, bf16[64,2048]{1,0:T(8,128)(2,1)S(1)} %multiply_convert_fusion.refs_0_, bf16[64,2048]{1,0:T(8,128)(2,1)S(1)} %collective-permute-done.refs_1_, bf16[64,2048]{1,0:T(8,128)(2,1)S(1)} %collective-permute-done.1.refs_2_, ...), custom_call_target="tpu_custom_call" | custom-call | tf_op jit(solution)/shard_map/terms/pallas_call | solution.py:299
  26.7 0.0 collective-permute-done.8.refs_15_
  26.8 1.0 %collective-permute-done.7.refs_14_ = f32[56,128]{1,0:T(8,128)S(1)} collective-permute-done((f32[56,128]{1,0:T(8,128)S(1)}, f32[56,128]{1,0:T(8,128)S(1)}, u32[]{:S(2)}, u32[]{:S(2)}) %collective-permute-start.7) | collective-permute-done | bytes 28704 | tf_op jit(solution)/shard_map/ppermute | solution.py:253
  27.8 0.0 collective-permute-done.6.refs_13_
  27.8 1.9 %grads.1 = (f32[512,128]{1,0:T(8,128)S(1)}, f32[512,128]{1,0:T(8,128)S(1)}, bf16[1024,128]{1,0:T(8,128)(2,1)S(1)}, f32[1024,128]{1,0:T(8,128)S(1)}, bf16[1024,12...) custom-call(bf16[64,2048]{1,0:T(8,128)(2,1)S(1)} %multiply_convert_f, ...), custom_call_target="tpu_custom_call" | custom-call | tf_op jit(solution)/shard_map/grads/pallas_call | solution.py:309
  29.6 0.1 collective-permute-start.9
  29.7 0.2 collective-permute-start.11
  30.0 2.8 %collective-permute-start.12 = (bf16[1024,128]{1,0:T(8,128)(2,1)S(1)}, bf16[1024,128]{1,0:T(8,128)(2,1)S(1)}, u32[]{:S(2)}, u32[]{:S(2)}) collective-permute-start(bf16[1024,128]{1,0:T(8,128)(2,1)S(1)} %get-tuple-element.28), channel_id=1, source_target_pairs={{0,4},{1,5},{2,6},{3,7},{4,0},{5,1},{6,2},{7,3},{8,12},{9,13},{10,... | collective-permute-start | bytes 786440 | tf_op jit(solution)/shard_map/ppermute | solution.py:253
  32.8 1.7 %collective-permute-start.13 = (bf16[1024,128]{1,0:T(8,128)(2,1)S(1)}, bf16[1024,128]{1,0:T(8,128)(2,1)S(1)}, u32[]{:S(2)}, u32[]{:S(2)}) collective-permute-start(bf16[1024,128]{1,0:T(8,128)(2,1)S(1)} %get-tuple-element.29), channel_id=1, source_target_pairs={{0,6},{1,7},{2,4},{3,5},{4,2},{5,3},{6,0},{7,1},{8,14},{9,15},{10,... | collective-permute-start | bytes 786440 | tf_op jit(solution)/shard_map/ppermute | solution.py:253
  34.5 0.0 collective-permute-done.9.refs_1_
  34.6 2.5 %collective-permute-start.10 = (bf16[512,128]{1,0:T(8,128)(2,1)S(1)}, bf16[512,128]{1,0:T(8,128)(2,1)S(1)}, u32[]{:S(2)}, u32[]{:S(2)}) collective-permute-start(bf16[512,128]{1,0:T(8,128)(2,1)S(1)} %add_convert_fusion), channel_id=1, source_target_pairs={{0,8},{1,9},{2,10},{3,11},{4,12},{5,13},{6,14},{7,15},{8,0},{9,1},... | collective-permute-start | bytes 393224 | tf_op jit(solution)/shard_map/ppermute | solution.py:253
  37.0 17.5 %all_to_all.5.refs_8_ = f32[16,1,128]{2,1,0:T(1,128)S(1)} all-to-all(f32[16,1,128]{2,1,0:T(1,128)S(1)} %get-tuple-element.31), channel_id=1, replica_groups=mesh['prompt'=16,'sample'=16] {'prompt'}, dimensions={0} | all-to-all | bytes 16384 | tf_op jit(solution)/shard_map/all_to_all | solution.py:327
  54.5 0.0 collective-permute-done.11.refs_4_
  54.5 0.0 collective-permute-done.12.refs_5_
  54.5 0.0 collective-permute-done.13.refs_6_
  54.6 0.0 collective-permute-done.10.refs_2_
  54.6 0.9 %finish.1 = (bf16[32,2048]{1,0:T(8,128)(2,1)}, bf16[128,512]{1,0:T(8,128)(2,1)}, bf16[128,512]{1,0:T(8,128)(2,1)}, bf16[32,512]{1,0:T(8,128)(2,1)}, bf16[32,512]{1,0:T(8,128)(2,1)}) custom-call(f32[512,128]{1,0:T(8,128)S(1)} %get-tuple-element.23.refs_0_, bf16[1024,128]{1,0:T(8,128)(2,1)S(1)} %collective-permute-done.9.refs_1_, ...), custom_call_target="tpu_custom_call" | custom-call | tf_op jit(solution)/shard_map/finish/pallas_call | solution.py:329
  (6 shorter events, 0.1 us)
Async XLA Ops:
  2.4 14.4 %collective-permute-start.4 = (bf16[272,512]{1,0:T(8,128)(2,1)S(1)}, bf16[272,512]{1,0:T(8,128)(2,1)S(1)}, u32[]{:S(2)}, u32[]{:S(2)}) collective-permute-start(bf16[272,512]{1,0:T(8,128)(2,1)S(1)} %maximum_maximum_fusion.refs_4_), channel_id=1, source_target_pairs={{0,4},{1,5},{2,6},{3,7},{4,0},{5,1},{6,2},{7,3},{8,12},{9,13},{10,... | collective-permute-start | bytes 835592 | tf_op jit(solution)/shard_map/ppermute | solution.py:253
  7.4 9.4 %collective-permute-start.1 = (bf16[64,2048]{1,0:T(8,128)(2,1)S(1)}, bf16[64,2048]{1,0:T(8,128)(2,1)S(1)}, u32[]{:S(2)}, u32[]{:S(2)}) collective-permute-start(bf16[64,2048]{1,0:T(8,128)(2,1)S(1)} %multiply_convert_fusion.refs_0_), channel_id=1, source_target_pairs={{0,8},{1,9},{2,10},{3,11},{4,12},{5,13},{6,14},{7,15},{8,0},{9,1},... | collective-permute-start | bytes 786440 | tf_op jit(solution)/shard_map/ppermute | solution.py:253
  8.0 8.8 %collective-permute-start = (bf16[64,2048]{1,0:T(8,128)(2,1)S(1)}, bf16[64,2048]{1,0:T(8,128)(2,1)S(1)}, u32[]{:S(2)}, u32[]{:S(2)}) collective-permute-start(bf16[64,2048]{1,0:T(8,128)(2,1)S(1)} %multiply_convert_fusion.refs_0_), channel_id=1, source_target_pairs={{0,1},{1,0},{2,3},{3,2},{4,5},{5,4},{6,7},{7,6},{8,9},{9,8},{10,11... | collective-permute-start | bytes 786440 | tf_op jit(solution)/shard_map/ppermute | solution.py:253
  8.0 11.8 %collective-permute-start.5 = (bf16[272,512]{1,0:T(8,128)(2,1)S(1)}, bf16[272,512]{1,0:T(8,128)(2,1)S(1)}, u32[]{:S(2)}, u32[]{:S(2)}) collective-permute-start(bf16[272,512]{1,0:T(8,128)(2,1)S(1)} %maximum_maximum_fusion.refs_4_), channel_id=1, source_target_pairs={{0,6},{1,7},{2,4},{3,5},{4,2},{5,3},{6,0},{7,1},{8,14},{9,15},{10,... | collective-permute-start | bytes 835592 | tf_op jit(solution)/shard_map/ppermute | solution.py:253
  9.1 10.8 %collective-permute-start.3 = (bf16[272,512]{1,0:T(8,128)(2,1)S(1)}, bf16[272,512]{1,0:T(8,128)(2,1)S(1)}, u32[]{:S(2)}, u32[]{:S(2)}) collective-permute-start(bf16[272,512]{1,0:T(8,128)(2,1)S(1)} %maximum_maximum_fusion.refs_4_), channel_id=1, source_target_pairs={{0,2},{1,3},{2,0},{3,1},{4,6},{5,7},{6,4},{7,5},{8,10},{9,11},{10,... | collective-permute-start | bytes 835592 | tf_op jit(solution)/shard_map/ppermute | solution.py:253
  10.8 7.5 %copy-start = (bf16[1,1,32,512]{3,2,1,0:T(8,128)(2,1)S(1)}, bf16[1,1,32,512]{3,2,1,0:T(8,128)(2,1)}, u32[]{:S(2)}) copy-start(bf16[1,1,32,512]{3,2,1,0:T(8,128)(2,1)} %param.15) | copy-start | bytes 98308
  10.8 7.5 %copy-start.1 = (bf16[1,1,32,512]{3,2,1,0:T(8,128)(2,1)S(1)}, bf16[1,1,32,512]{3,2,1,0:T(8,128)(2,1)}, u32[]{:S(2)}) copy-start(bf16[1,1,32,512]{3,2,1,0:T(8,128)(2,1)} %param.16) | copy-start | bytes 98308
  16.8 1.5 %collective-permute-start.2 = (bf16[64,2048]{1,0:T(8,128)(2,1)S(1)}, bf16[64,2048]{1,0:T(8,128)(2,1)S(1)}, u32[]{:S(2)}, u32[]{:S(2)}) collective-permute-start(bf16[64,2048]{1,0:T(8,128)(2,1)S(1)} %collective-permute-done.1.refs_2_), channel_id=1, source_target_pairs={{0,1},{1,0},{2,3},{3,2},{4,5},{5,4},{6,7},{7,6},{8,9},{9,8},{10,11... | collective-permute-start | bytes 786440 | tf_op jit(solution)/shard_map/ppermute | solution.py:253
  21.4 5.3 %collective-permute-start.8 = (f32[56,128]{1,0:T(8,128)S(1)}, f32[56,128]{1,0:T(8,128)S(1)}, u32[]{:S(2)}, u32[]{:S(2)}) collective-permute-start(f32[56,128]{1,0:T(8,128)S(1)} %stats.1.refs_12_), channel_id=1, source_target_pairs={{0,9},{1,8},{2,11},{3,10},{4,13},{5,12},{6,15},{7,14},{8,1},{9,0},... | collective-permute-start | bytes 86024 | tf_op jit(solution)/shard_map/ppermute | solution.py:253
  22.3 5.5 %collective-permute-start.7 = (f32[56,128]{1,0:T(8,128)S(1)}, f32[56,128]{1,0:T(8,128)S(1)}, u32[]{:S(2)}, u32[]{:S(2)}) collective-permute-start(f32[56,128]{1,0:T(8,128)S(1)} %stats.1.refs_12_), channel_id=1, source_target_pairs={{0,8},{1,9},{2,10},{3,11},{4,12},{5,13},{6,14},{7,15},{8,0},{9,1},... | collective-permute-start | bytes 86024 | tf_op jit(solution)/shard_map/ppermute | solution.py:253
  24.8 3.0 %collective-permute-start.6 = (f32[56,128]{1,0:T(8,128)S(1)}, f32[56,128]{1,0:T(8,128)S(1)}, u32[]{:S(2)}, u32[]{:S(2)}) collective-permute-start(f32[56,128]{1,0:T(8,128)S(1)} %stats.1.refs_12_), channel_id=1, source_target_pairs={{0,1},{1,0},{2,3},{3,2},{4,5},{5,4},{6,7},{7,6},{8,9},{9,8},{10,11... | collective-permute-start | bytes 86024 | tf_op jit(solution)/shard_map/ppermute | solution.py:253
  29.6 4.9 %collective-permute-start.9 = (bf16[1024,128]{1,0:T(8,128)(2,1)S(1)}, bf16[1024,128]{1,0:T(8,128)(2,1)S(1)}, u32[]{:S(2)}, u32[]{:S(2)}) collective-permute-start(bf16[1024,128]{1,0:T(8,128)(2,1)S(1)} %get-tuple-element.24), channel_id=1, source_target_pairs={{0,1},{1,0},{2,3},{3,2},{4,5},{5,4},{6,7},{7,6},{8,9},{9,8},{10,11... | collective-permute-start | bytes 786440 | tf_op jit(solution)/shard_map/ppermute | solution.py:253
  29.7 24.8 %collective-permute-start.11 = (bf16[1024,128]{1,0:T(8,128)(2,1)S(1)}, bf16[1024,128]{1,0:T(8,128)(2,1)S(1)}, u32[]{:S(2)}, u32[]{:S(2)}) collective-permute-start(bf16[1024,128]{1,0:T(8,128)(2,1)S(1)} %get-tuple-element.27), channel_id=1, source_target_pairs={{0,2},{1,3},{2,0},{3,1},{4,6},{5,7},{6,4},{7,5},{8,10},{9,11},{10,... | collective-permute-start | bytes 786440 | tf_op jit(solution)/shard_map/ppermute | solution.py:253
  30.0 24.6 %collective-permute-start.12 = (bf16[1024,128]{1,0:T(8,128)(2,1)S(1)}, bf16[1024,128]{1,0:T(8,128)(2,1)S(1)}, u32[]{:S(2)}, u32[]{:S(2)}) collective-permute-start(bf16[1024,128]{1,0:T(8,128)(2,1)S(1)} %get-tuple-element.28), channel_id=1, source_target_pairs={{0,4},{1,5},{2,6},{3,7},{4,0},{5,1},{6,2},{7,3},{8,12},{9,13},{10,... | collective-permute-start | bytes 786440 | tf_op jit(solution)/shard_map/ppermute | solution.py:253
  32.8 21.8 %collective-permute-start.13 = (bf16[1024,128]{1,0:T(8,128)(2,1)S(1)}, bf16[1024,128]{1,0:T(8,128)(2,1)S(1)}, u32[]{:S(2)}, u32[]{:S(2)}) collective-permute-start(bf16[1024,128]{1,0:T(8,128)(2,1)S(1)} %get-tuple-element.29), channel_id=1, source_target_pairs={{0,6},{1,7},{2,4},{3,5},{4,2},{5,3},{6,0},{7,1},{8,14},{9,15},{10,... | collective-permute-start | bytes 786440 | tf_op jit(solution)/shard_map/ppermute | solution.py:253
  34.6 20.0 %collective-permute-start.10 = (bf16[512,128]{1,0:T(8,128)(2,1)S(1)}, bf16[512,128]{1,0:T(8,128)(2,1)S(1)}, u32[]{:S(2)}, u32[]{:S(2)}) collective-permute-start(bf16[512,128]{1,0:T(8,128)(2,1)S(1)} %add_convert_fusion), channel_id=1, source_target_pairs={{0,8},{1,9},{2,10},{3,11},{4,12},{5,13},{6,14},{7,15},{8,0},{9,1},... | collective-permute-start | bytes 393224 | tf_op jit(solution)/shard_map/ppermute | solution.py:253

commit v6 on v5

--- a/solution.py
+++ b/solution.py
@@ -139,7 +139,7 @@
     tokens = own_ref[0].shape[0]
     rows = qg[0].shape[1] // HD // groups * tokens
     size = 4 * block + tokens
-    shifts, means = [], []
+    peaks, logs, means = [], [], []
     for s in range(4):
         tops = [stats[e][(s ^ e) * 4 : (s ^ e) * 4 + 4, :] for e in range(4)]
         top = functools.reduce(jnp.maximum, tops)
@@ -149,9 +149,11 @@
             at = (s ^ e) * 4
             total += stats[e][16 + at : 20 + at, :] * factor
             mixed += stats[e][32 + at : 36 + at, :] * factor
-        shifts.append(top + jnp.log2(total))
+        peaks.append(top)
+        logs.append(jnp.log2(total))
         means.append(mixed / total)
-    shift = jnp.concatenate(shifts, axis=1)
+    peak = jnp.concatenate(peaks, axis=1)
+    log = jnp.concatenate(logs, axis=1)
     mean = jnp.concatenate(means, axis=1)
     half = groups * block
     for i in range(tot_out.shape[0]):
@@ -160,9 +162,9 @@
         q = rows_of(qg, 0, g)
         w = rows_of(qg, 1, g)
         k = with_own(kvs, own_ref, 0, g)
-        sh, mn = shift[g : g + 1, :], mean[g : g + 1, :]
+        pk, lg, mn = (x[g : g + 1, :] for x in (peak, log, mean))
         span = slice(g * size, (g + 1) * size)
-        p = jnp.exp2(score_ref[span, :] - sh)
+        p = jnp.exp2((score_ref[span, :] - pk) - lg)
         ds = (p * (slope_ref[span, :] - mn)).astype(jnp.bfloat16)
         dv = dot(p.astype(jnp.bfloat16), w, NN)
         dk = dot(ds, q, NN)

time: 55.7 us -> 55.7 us (level)
  no operation moved by 1% of the time
where the time goes in v6:
time: 55.7 us; the launch traced here: 55.5 us
  blocking collectives  17.5 us (31%)
  starting transfers between devices  16.7 us (30%)
  waiting for transfers between devices  8.55 us (15%)
  Pallas kernels  7.68 us (14%)
  between operations  2.71 us (5%)
  other arithmetic  2.21 us (4%)
    all_to_all x1, blocking collectives, per_device(): total = lax.all_to_all(outs[8], 'prompt', 0, 0, tiled=True)  17.5 us
    ppermute x14, starting transfers between devices, swap(): lax.ppermute(array, 'sample', [(i, i ^ mask) for i in range(samples)])  16.7 us
    ppermute x14, waiting for transfers between devices, swap(): lax.ppermute(array, 'sample', [(i, i ^ mask) for i in range(samples)])  8.55 us
    pallas_call x1, Pallas kernels, per_device(): pl.pallas_call(functools.partial(terms_kernel, to_log2), out_shape=[term_...  1.87 us
    pallas_call x1, Pallas kernels, per_device(): pl.pallas_call(grads_kernel, out_shape=[shape((dq_rows, HD), f32), shape(...  1.85 us
    pallas_call x1, Pallas kernels, per_device(): pl.pallas_call(functools.partial(first_stats_kernel, to_log2, early), out...  1.54 us
    pallas_call x1, Pallas kernels, per_device(): pl.pallas_call(functools.partial(last_stats_kernel, to_log2, late), out_s...  1.51 us
  transfers between devices with their start and end apart: 14, of which 3 were waited for; matrix products, arithmetic and copies ran while one was open for 2% of the time, Pallas kernels for 6%

profile of v6, /device:TPU:4, one launch (start us, length us, event | category | flops | bytes accessed | tf_op | source)
XLA Modules:
  0.0 55.5 jit_solution(9299085714231986306)
XLA Ops:
  1.3 1.1 %maximum_maximum_fusion.refs_4_ = bf16[272,512]{1,0:T(8,128)(2,1)S(1)} fusion(bf16[128,512]{1,0:T(8,128)(2,1)} %bitcast.26, bf16[128,512]{1,0:T(8,128)(2,1)} %bitcast.27, bf16[272]{0:T(512)(128)(2,1)S(1)} %pad.2.clone), kind=kLoop, calls=%fused_computation.1 | loop fusion | flops 835584 | bytes 541216 | tf_op jit(solution)/shard_map/concatenate | solution.py:263
  2.4 3.3 %collective-permute-start.4 = (bf16[272,512]{1,0:T(8,128)(2,1)S(1)}, bf16[272,512]{1,0:T(8,128)(2,1)S(1)}, u32[]{:S(2)}, u32[]{:S(2)}) collective-permute-start(bf16[272,512]{1,0:T(8,128)(2,1)S(1)} %maximum_maximum_fusion.refs_4_), channel_id=1, source_target_pairs={{0,4},{1,5},{2,6},{3,7},{4,0},{5,1},{6,2},{7,3},{8,12},{9,13},{10,... | collective-permute-start | bytes 835592 | tf_op jit(solution)/shard_map/ppermute | solution.py:255
  6.3 1.1 %multiply_convert_fusion.refs_0_ = bf16[64,2048]{1,0:T(8,128)(2,1)S(1)} fusion(bf16[32,2048]{1,0:T(8,128)(2,1)} %bitcast.28, bf16[32,2048]{1,0:T(8,128)(2,1)} %bitcast.29, f32[64]{0:T(128)S(1)} %compare_select_fusion, pred[64]{0:T(512)(128)(4,1)S(1)} %iota_compare_fusion), kind=kLoop, calls=%fused_computation | loop fusion | flops 917504 | bytes 524608 | tf_op jit(solution)/shard_map/convert_element_type | solution.py:261
  7.4 0.6 %collective-permute-start.1 = (bf16[64,2048]{1,0:T(8,128)(2,1)S(1)}, bf16[64,2048]{1,0:T(8,128)(2,1)S(1)}, u32[]{:S(2)}, u32[]{:S(2)}) collective-permute-start(bf16[64,2048]{1,0:T(8,128)(2,1)S(1)} %multiply_convert_fusion.refs_0_), channel_id=1, source_target_pairs={{0,8},{1,9},{2,10},{3,11},{4,12},{5,13},{6,14},{7,15},{8,0},{9,1},... | collective-permute-start | bytes 786440 | tf_op jit(solution)/shard_map/ppermute | solution.py:255
  8.0 0.0 collective-permute-start
  8.0 1.1 %collective-permute-start.5 = (bf16[272,512]{1,0:T(8,128)(2,1)S(1)}, bf16[272,512]{1,0:T(8,128)(2,1)S(1)}, u32[]{:S(2)}, u32[]{:S(2)}) collective-permute-start(bf16[272,512]{1,0:T(8,128)(2,1)S(1)} %maximum_maximum_fusion.refs_4_), channel_id=1, source_target_pairs={{0,6},{1,7},{2,4},{3,5},{4,2},{5,3},{6,0},{7,1},{8,14},{9,15},{10,... | collective-permute-start | bytes 835592 | tf_op jit(solution)/shard_map/ppermute | solution.py:255
  9.1 1.0 %collective-permute-start.3 = (bf16[272,512]{1,0:T(8,128)(2,1)S(1)}, bf16[272,512]{1,0:T(8,128)(2,1)S(1)}, u32[]{:S(2)}, u32[]{:S(2)}) collective-permute-start(bf16[272,512]{1,0:T(8,128)(2,1)S(1)} %maximum_maximum_fusion.refs_4_), channel_id=1, source_target_pairs={{0,2},{1,3},{2,0},{3,1},{4,6},{5,7},{6,4},{7,5},{8,10},{9,11},{10,... | collective-permute-start | bytes 835592 | tf_op jit(solution)/shard_map/ppermute | solution.py:255
  10.7 0.1 stack.19.info_ref
  10.8 0.0 copy-start
  10.8 0.0 copy-start.1
  10.8 6.0 %collective-permute-done.1.refs_2_ = bf16[64,2048]{1,0:T(8,128)(2,1)S(1)} collective-permute-done((bf16[64,2048]{1,0:T(8,128)(2,1)S(1)}, bf16[64,2048]{1,0:T(8,128)(2,1)S(1)}, u32[]{:S(2)}, u32[]{:S(2)}) %collective-permute-start.1) | collective-permute-done | bytes 262176 | tf_op jit(solution)/shard_map/ppermute | solution.py:255
  16.8 0.0 collective-permute-start.2
  16.8 0.0 collective-permute-done.4.refs_0_
  16.8 0.0 collective-permute-done.refs_1_
  16.8 1.5 %collective-permute-done.2.refs_3_ = bf16[64,2048]{1,0:T(8,128)(2,1)S(1)} collective-permute-done((bf16[64,2048]{1,0:T(8,128)(2,1)S(1)}, bf16[64,2048]{1,0:T(8,128)(2,1)S(1)}, u32[]{:S(2)}, u32[]{:S(2)}) %collective-permute-start.2) | collective-permute-done | bytes 262176 | tf_op jit(solution)/shard_map/ppermute | solution.py:255
  18.3 0.0 copy-done
  18.3 0.0 copy-done.1
  18.3 1.5 %stats_first.1.refs_8_ = f32[16,512]{1,0:T(8,128)S(1)} custom-call(s32[5]{0:T(128)S(1)} %stack.19.info_ref, bf16[64,2048]{1,0:T(8,128)(2,1)S(1)} %multiply_convert_fusion.refs_0_, bf16[64,2048]{1,0:T(8,128)(2,1)S(1)} %collective-permute-done.refs_1_, bf16[64,2048]{1,0:T(8,128)(2,1)S(1)} %collective-permute-done.1.refs_2_, ...), custom_call_target="tpu_custom_call" | custom-call | tf_op jit(solution)/shard_map/stats_first/pallas_call | solution.py:283
  19.9 0.0 collective-permute-done.5.refs_7_
  19.9 0.0 collective-permute-done.3.refs_5_
  19.9 1.5 %stats.1.refs_12_ = f32[56,128]{1,0:T(8,128)S(1)} custom-call(s32[5]{0:T(128)S(1)} %stack.19.info_ref, bf16[64,2048]{1,0:T(8,128)(2,1)S(1)} %multiply_convert_fusion.refs_0_, bf16[64,2048]{1,0:T(8,128)(2,1)S(1)} %collective-permute-done.refs_1_, bf16[64,2048]{1,0:T(8,128)(2,1)S(1)} %collective-permute-done.1.refs_2_, ...), custom_call_target="tpu_custom_call" | custom-call | tf_op jit(solution)/shard_map/stats/pallas_call | solution.py:291
  21.4 0.9 %collective-permute-start.8 = (f32[56,128]{1,0:T(8,128)S(1)}, f32[56,128]{1,0:T(8,128)S(1)}, u32[]{:S(2)}, u32[]{:S(2)}) collective-permute-start(f32[56,128]{1,0:T(8,128)S(1)} %stats.1.refs_12_), channel_id=1, source_target_pairs={{0,9},{1,8},{2,11},{3,10},{4,13},{5,12},{6,15},{7,14},{8,1},{9,0},... | collective-permute-start | bytes 86024 | tf_op jit(solution)/shard_map/ppermute | solution.py:255
  22.3 2.5 %collective-permute-start.7 = (f32[56,128]{1,0:T(8,128)S(1)}, f32[56,128]{1,0:T(8,128)S(1)}, u32[]{:S(2)}, u32[]{:S(2)}) collective-permute-start(f32[56,128]{1,0:T(8,128)S(1)} %stats.1.refs_12_), channel_id=1, source_target_pairs={{0,8},{1,9},{2,10},{3,11},{4,12},{5,13},{6,14},{7,15},{8,0},{9,1},... | collective-permute-start | bytes 86024 | tf_op jit(solution)/shard_map/ppermute | solution.py:255
  24.8 0.1 collective-permute-start.6
  24.9 1.9 %terms.1 = (f32[2176,512]{1,0:T(8,128)S(1)}, f32[2176,512]{1,0:T(8,128)S(1)}) custom-call(s32[5]{0:T(128)S(1)} %stack.19.info_ref, bf16[64,2048]{1,0:T(8,128)(2,1)S(1)} %multiply_convert_fusion.refs_0_, bf16[64,2048]{1,0:T(8,128)(2,1)S(1)} %collective-permute-done.refs_1_, bf16[64,2048]{1,0:T(8,128)(2,1)S(1)} %collective-permute-done.1.refs_2_, ...), custom_call_target="tpu_custom_call" | custom-call | tf_op jit(solution)/shard_map/terms/pallas_call | solution.py:301
  26.7 0.0 collective-permute-done.8.refs_15_
  26.8 1.0 %collective-permute-done.7.refs_14_ = f32[56,128]{1,0:T(8,128)S(1)} collective-permute-done((f32[56,128]{1,0:T(8,128)S(1)}, f32[56,128]{1,0:T(8,128)S(1)}, u32[]{:S(2)}, u32[]{:S(2)}) %collective-permute-start.7) | collective-permute-done | bytes 28704 | tf_op jit(solution)/shard_map/ppermute | solution.py:255
  27.8 0.0 collective-permute-done.6.refs_13_
  27.8 1.9 %grads.1 = (f32[512,128]{1,0:T(8,128)S(1)}, f32[512,128]{1,0:T(8,128)S(1)}, bf16[1024,128]{1,0:T(8,128)(2,1)S(1)}, f32[1024,128]{1,0:T(8,128)S(1)}, bf16[1024,12...) custom-call(bf16[64,2048]{1,0:T(8,128)(2,1)S(1)} %multiply_convert_f, ...), custom_call_target="tpu_custom_call" | custom-call | tf_op jit(solution)/shard_map/grads/pallas_call | solution.py:311
  29.6 0.1 collective-permute-start.9
  29.7 0.2 collective-permute-start.11
  30.0 2.8 %collective-permute-start.12 = (bf16[1024,128]{1,0:T(8,128)(2,1)S(1)}, bf16[1024,128]{1,0:T(8,128)(2,1)S(1)}, u32[]{:S(2)}, u32[]{:S(2)}) collective-permute-start(bf16[1024,128]{1,0:T(8,128)(2,1)S(1)} %get-tuple-element.28), channel_id=1, source_target_pairs={{0,4},{1,5},{2,6},{3,7},{4,0},{5,1},{6,2},{7,3},{8,12},{9,13},{10,... | collective-permute-start | bytes 786440 | tf_op jit(solution)/shard_map/ppermute | solution.py:255
  32.8 1.7 %collective-permute-start.13 = (bf16[1024,128]{1,0:T(8,128)(2,1)S(1)}, bf16[1024,128]{1,0:T(8,128)(2,1)S(1)}, u32[]{:S(2)}, u32[]{:S(2)}) collective-permute-start(bf16[1024,128]{1,0:T(8,128)(2,1)S(1)} %get-tuple-element.29), channel_id=1, source_target_pairs={{0,6},{1,7},{2,4},{3,5},{4,2},{5,3},{6,0},{7,1},{8,14},{9,15},{10,... | collective-permute-start | bytes 786440 | tf_op jit(solution)/shard_map/ppermute | solution.py:255
  34.5 0.0 collective-permute-done.9.refs_1_
  34.6 2.5 %collective-permute-start.10 = (bf16[512,128]{1,0:T(8,128)(2,1)S(1)}, bf16[512,128]{1,0:T(8,128)(2,1)S(1)}, u32[]{:S(2)}, u32[]{:S(2)}) collective-permute-start(bf16[512,128]{1,0:T(8,128)(2,1)S(1)} %add_convert_fusion), channel_id=1, source_target_pairs={{0,8},{1,9},{2,10},{3,11},{4,12},{5,13},{6,14},{7,15},{8,0},{9,1},... | collective-permute-start | bytes 393224 | tf_op jit(solution)/shard_map/ppermute | solution.py:255
  37.0 17.5 %all_to_all.5.refs_8_ = f32[16,1,128]{2,1,0:T(1,128)S(1)} all-to-all(f32[16,1,128]{2,1,0:T(1,128)S(1)} %get-tuple-element.31), channel_id=1, replica_groups=mesh['prompt'=16,'sample'=16] {'prompt'}, dimensions={0} | all-to-all | bytes 16384 | tf_op jit(solution)/shard_map/all_to_all | solution.py:329
  54.5 0.0 collective-permute-done.11.refs_4_
  54.5 0.0 collective-permute-done.12.refs_5_
  54.5 0.0 collective-permute-done.13.refs_6_
  54.6 0.0 collective-permute-done.10.refs_2_
  54.6 0.9 %finish.1 = (bf16[32,2048]{1,0:T(8,128)(2,1)}, bf16[128,512]{1,0:T(8,128)(2,1)}, bf16[128,512]{1,0:T(8,128)(2,1)}, bf16[32,512]{1,0:T(8,128)(2,1)}, bf16[32,512]{1,0:T(8,128)(2,1)}) custom-call(f32[512,128]{1,0:T(8,128)S(1)} %get-tuple-element.23.refs_0_, bf16[1024,128]{1,0:T(8,128)(2,1)S(1)} %collective-permute-done.9.refs_1_, ...), custom_call_target="tpu_custom_call" | custom-call | tf_op jit(solution)/shard_map/finish/pallas_call | solution.py:331
  (6 shorter events, 0.1 us)
Async XLA Ops:
  2.4 14.4 %collective-permute-start.4 = (bf16[272,512]{1,0:T(8,128)(2,1)S(1)}, bf16[272,512]{1,0:T(8,128)(2,1)S(1)}, u32[]{:S(2)}, u32[]{:S(2)}) collective-permute-start(bf16[272,512]{1,0:T(8,128)(2,1)S(1)} %maximum_maximum_fusion.refs_4_), channel_id=1, source_target_pairs={{0,4},{1,5},{2,6},{3,7},{4,0},{5,1},{6,2},{7,3},{8,12},{9,13},{10,... | collective-permute-start | bytes 835592 | tf_op jit(solution)/shard_map/ppermute | solution.py:255
  7.4 9.4 %collective-permute-start.1 = (bf16[64,2048]{1,0:T(8,128)(2,1)S(1)}, bf16[64,2048]{1,0:T(8,128)(2,1)S(1)}, u32[]{:S(2)}, u32[]{:S(2)}) collective-permute-start(bf16[64,2048]{1,0:T(8,128)(2,1)S(1)} %multiply_convert_fusion.refs_0_), channel_id=1, source_target_pairs={{0,8},{1,9},{2,10},{3,11},{4,12},{5,13},{6,14},{7,15},{8,0},{9,1},... | collective-permute-start | bytes 786440 | tf_op jit(solution)/shard_map/ppermute | solution.py:255
  8.0 8.8 %collective-permute-start = (bf16[64,2048]{1,0:T(8,128)(2,1)S(1)}, bf16[64,2048]{1,0:T(8,128)(2,1)S(1)}, u32[]{:S(2)}, u32[]{:S(2)}) collective-permute-start(bf16[64,2048]{1,0:T(8,128)(2,1)S(1)} %multiply_convert_fusion.refs_0_), channel_id=1, source_target_pairs={{0,1},{1,0},{2,3},{3,2},{4,5},{5,4},{6,7},{7,6},{8,9},{9,8},{10,11... | collective-permute-start | bytes 786440 | tf_op jit(solution)/shard_map/ppermute | solution.py:255
  8.0 11.8 %collective-permute-start.5 = (bf16[272,512]{1,0:T(8,128)(2,1)S(1)}, bf16[272,512]{1,0:T(8,128)(2,1)S(1)}, u32[]{:S(2)}, u32[]{:S(2)}) collective-permute-start(bf16[272,512]{1,0:T(8,128)(2,1)S(1)} %maximum_maximum_fusion.refs_4_), channel_id=1, source_target_pairs={{0,6},{1,7},{2,4},{3,5},{4,2},{5,3},{6,0},{7,1},{8,14},{9,15},{10,... | collective-permute-start | bytes 835592 | tf_op jit(solution)/shard_map/ppermute | solution.py:255
  9.1 10.8 %collective-permute-start.3 = (bf16[272,512]{1,0:T(8,128)(2,1)S(1)}, bf16[272,512]{1,0:T(8,128)(2,1)S(1)}, u32[]{:S(2)}, u32[]{:S(2)}) collective-permute-start(bf16[272,512]{1,0:T(8,128)(2,1)S(1)} %maximum_maximum_fusion.refs_4_), channel_id=1, source_target_pairs={{0,2},{1,3},{2,0},{3,1},{4,6},{5,7},{6,4},{7,5},{8,10},{9,11},{10,... | collective-permute-start | bytes 835592 | tf_op jit(solution)/shard_map/ppermute | solution.py:255
  10.8 7.5 %copy-start = (bf16[1,1,32,512]{3,2,1,0:T(8,128)(2,1)S(1)}, bf16[1,1,32,512]{3,2,1,0:T(8,128)(2,1)}, u32[]{:S(2)}) copy-start(bf16[1,1,32,512]{3,2,1,0:T(8,128)(2,1)} %param.15) | copy-start | bytes 98308
  10.8 7.5 %copy-start.1 = (bf16[1,1,32,512]{3,2,1,0:T(8,128)(2,1)S(1)}, bf16[1,1,32,512]{3,2,1,0:T(8,128)(2,1)}, u32[]{:S(2)}) copy-start(bf16[1,1,32,512]{3,2,1,0:T(8,128)(2,1)} %param.16) | copy-start | bytes 98308
  16.8 1.5 %collective-permute-start.2 = (bf16[64,2048]{1,0:T(8,128)(2,1)S(1)}, bf16[64,2048]{1,0:T(8,128)(2,1)S(1)}, u32[]{:S(2)}, u32[]{:S(2)}) collective-permute-start(bf16[64,2048]{1,0:T(8,128)(2,1)S(1)} %collective-permute-done.1.refs_2_), channel_id=1, source_target_pairs={{0,1},{1,0},{2,3},{3,2},{4,5},{5,4},{6,7},{7,6},{8,9},{9,8},{10,11... | collective-permute-start | bytes 786440 | tf_op jit(solution)/shard_map/ppermute | solution.py:255
  21.4 5.3 %collective-permute-start.8 = (f32[56,128]{1,0:T(8,128)S(1)}, f32[56,128]{1,0:T(8,128)S(1)}, u32[]{:S(2)}, u32[]{:S(2)}) collective-permute-start(f32[56,128]{1,0:T(8,128)S(1)} %stats.1.refs_12_), channel_id=1, source_target_pairs={{0,9},{1,8},{2,11},{3,10},{4,13},{5,12},{6,15},{7,14},{8,1},{9,0},... | collective-permute-start | bytes 86024 | tf_op jit(solution)/shard_map/ppermute | solution.py:255
  22.3 5.5 %collective-permute-start.7 = (f32[56,128]{1,0:T(8,128)S(1)}, f32[56,128]{1,0:T(8,128)S(1)}, u32[]{:S(2)}, u32[]{:S(2)}) collective-permute-start(f32[56,128]{1,0:T(8,128)S(1)} %stats.1.refs_12_), channel_id=1, source_target_pairs={{0,8},{1,9},{2,10},{3,11},{4,12},{5,13},{6,14},{7,15},{8,0},{9,1},... | collective-permute-start | bytes 86024 | tf_op jit(solution)/shard_map/ppermute | solution.py:255
  24.8 3.0 %collective-permute-start.6 = (f32[56,128]{1,0:T(8,128)S(1)}, f32[56,128]{1,0:T(8,128)S(1)}, u32[]{:S(2)}, u32[]{:S(2)}) collective-permute-start(f32[56,128]{1,0:T(8,128)S(1)} %stats.1.refs_12_), channel_id=1, source_target_pairs={{0,1},{1,0},{2,3},{3,2},{4,5},{5,4},{6,7},{7,6},{8,9},{9,8},{10,11... | collective-permute-start | bytes 86024 | tf_op jit(solution)/shard_map/ppermute | solution.py:255
  29.6 4.9 %collective-permute-start.9 = (bf16[1024,128]{1,0:T(8,128)(2,1)S(1)}, bf16[1024,128]{1,0:T(8,128)(2,1)S(1)}, u32[]{:S(2)}, u32[]{:S(2)}) collective-permute-start(bf16[1024,128]{1,0:T(8,128)(2,1)S(1)} %get-tuple-element.24), channel_id=1, source_target_pairs={{0,1},{1,0},{2,3},{3,2},{4,5},{5,4},{6,7},{7,6},{8,9},{9,8},{10,11... | collective-permute-start | bytes 786440 | tf_op jit(solution)/shard_map/ppermute | solution.py:255
  29.7 24.8 %collective-permute-start.11 = (bf16[1024,128]{1,0:T(8,128)(2,1)S(1)}, bf16[1024,128]{1,0:T(8,128)(2,1)S(1)}, u32[]{:S(2)}, u32[]{:S(2)}) collective-permute-start(bf16[1024,128]{1,0:T(8,128)(2,1)S(1)} %get-tuple-element.27), channel_id=1, source_target_pairs={{0,2},{1,3},{2,0},{3,1},{4,6},{5,7},{6,4},{7,5},{8,10},{9,11},{10,... | collective-permute-start | bytes 786440 | tf_op jit(solution)/shard_map/ppermute | solution.py:255
  30.0 24.6 %collective-permute-start.12 = (bf16[1024,128]{1,0:T(8,128)(2,1)S(1)}, bf16[1024,128]{1,0:T(8,128)(2,1)S(1)}, u32[]{:S(2)}, u32[]{:S(2)}) collective-permute-start(bf16[1024,128]{1,0:T(8,128)(2,1)S(1)} %get-tuple-element.28), channel_id=1, source_target_pairs={{0,4},{1,5},{2,6},{3,7},{4,0},{5,1},{6,2},{7,3},{8,12},{9,13},{10,... | collective-permute-start | bytes 786440 | tf_op jit(solution)/shard_map/ppermute | solution.py:255
  32.8 21.8 %collective-permute-start.13 = (bf16[1024,128]{1,0:T(8,128)(2,1)S(1)}, bf16[1024,128]{1,0:T(8,128)(2,1)S(1)}, u32[]{:S(2)}, u32[]{:S(2)}) collective-permute-start(bf16[1024,128]{1,0:T(8,128)(2,1)S(1)} %get-tuple-element.29), channel_id=1, source_target_pairs={{0,6},{1,7},{2,4},{3,5},{4,2},{5,3},{6,0},{7,1},{8,14},{9,15},{10,... | collective-permute-start | bytes 786440 | tf_op jit(solution)/shard_map/ppermute | solution.py:255
  34.6 20.0 %collective-permute-start.10 = (bf16[512,128]{1,0:T(8,128)(2,1)S(1)}, bf16[512,128]{1,0:T(8,128)(2,1)S(1)}, u32[]{:S(2)}, u32[]{:S(2)}) collective-permute-start(bf16[512,128]{1,0:T(8,128)(2,1)S(1)} %add_convert_fusion), channel_id=1, source_target_pairs={{0,8},{1,9},{2,10},{3,11},{4,12},{5,13},{6,14},{7,15},{8,0},{9,1},... | collective-permute-start | bytes 393224 | tf_op jit(solution)/shard_map/ppermute | solution.py:255

commit v7 on v6

--- a/solution.py
+++ b/solution.py
@@ -157,7 +157,7 @@
     mean = jnp.concatenate(means, axis=1)
     half = groups * block
     for i in range(tot_out.shape[0]):
-        tot_out[i] = sum(stats[e][48:49, :] for e in range(4))
+        tot_out[i] = sum(stats[e][48:49, :1] for e in range(4))
     for g in range(groups):
         q = rows_of(qg, 0, g)
         w = rows_of(qg, 1, g)
@@ -317,7 +317,7 @@
             shape((kv_rows, HD), f32),
         ]
         + [shape((kv_rows, HD), bf16)] * 3
-        + [shape((2 * tokens, kv_width), f32), shape((prompts, 1, HD), f32)],
+        + [shape((2 * tokens, kv_width), f32), shape((prompts, 1, 1), f32)],
         in_specs=[vmem] * 16,
         out_specs=[vmem] * 9,
         compiler_params=params,

time: 55.7 us -> 55.7 us (level)
  no operation moved by 1% of the time
where the time goes in v7:
time: 55.7 us; the launch traced here: 55.5 us
  blocking collectives  17.5 us (31%)
  starting transfers between devices  16.7 us (30%)
  waiting for transfers between devices  8.55 us (15%)
  Pallas kernels  7.69 us (14%)
  between operations  2.71 us (5%)
  other arithmetic  2.21 us (4%)
    all_to_all x1, blocking collectives, per_device(): total = lax.all_to_all(outs[8], 'prompt', 0, 0, tiled=True)  17.5 us
    ppermute x14, starting transfers between devices, swap(): lax.ppermute(array, 'sample', [(i, i ^ mask) for i in range(samples)])  16.7 us
    ppermute x14, waiting for transfers between devices, swap(): lax.ppermute(array, 'sample', [(i, i ^ mask) for i in range(samples)])  8.55 us
    pallas_call x1, Pallas kernels, per_device(): pl.pallas_call(functools.partial(terms_kernel, to_log2), out_shape=[term_...  1.87 us
    pallas_call x1, Pallas kernels, per_device(): pl.pallas_call(grads_kernel, out_shape=[shape((dq_rows, HD), f32), shape(...  1.85 us
    pallas_call x1, Pallas kernels, per_device(): pl.pallas_call(functools.partial(first_stats_kernel, to_log2, early), out...  1.54 us
    pallas_call x1, Pallas kernels, per_device(): pl.pallas_call(functools.partial(last_stats_kernel, to_log2, late), out_s...  1.51 us
  transfers between devices with their start and end apart: 14, of which 3 were waited for; matrix products, arithmetic and copies ran while one was open for 2% of the time, Pallas kernels for 6%

profile of v7, /device:TPU:4, one launch (start us, length us, event | category | flops | bytes accessed | tf_op | source)
XLA Modules:
  0.0 55.5 jit_solution(9303611430558830463)
XLA Ops:
  1.3 1.1 %maximum_maximum_fusion.refs_4_ = bf16[272,512]{1,0:T(8,128)(2,1)S(1)} fusion(bf16[128,512]{1,0:T(8,128)(2,1)} %bitcast.26, bf16[128,512]{1,0:T(8,128)(2,1)} %bitcast.27, bf16[272]{0:T(512)(128)(2,1)S(1)} %pad.2.clone), kind=kLoop, calls=%fused_computation.1 | loop fusion | flops 835584 | bytes 541216 | tf_op jit(solution)/shard_map/concatenate | solution.py:263
  2.4 3.3 %collective-permute-start.4 = (bf16[272,512]{1,0:T(8,128)(2,1)S(1)}, bf16[272,512]{1,0:T(8,128)(2,1)S(1)}, u32[]{:S(2)}, u32[]{:S(2)}) collective-permute-start(bf16[272,512]{1,0:T(8,128)(2,1)S(1)} %maximum_maximum_fusion.refs_4_), channel_id=1, source_target_pairs={{0,4},{1,5},{2,6},{3,7},{4,0},{5,1},{6,2},{7,3},{8,12},{9,13},{10,... | collective-permute-start | bytes 835592 | tf_op jit(solution)/shard_map/ppermute | solution.py:255
  6.3 1.1 %multiply_convert_fusion.refs_0_ = bf16[64,2048]{1,0:T(8,128)(2,1)S(1)} fusion(bf16[32,2048]{1,0:T(8,128)(2,1)} %bitcast.28, bf16[32,2048]{1,0:T(8,128)(2,1)} %bitcast.29, f32[64]{0:T(128)S(1)} %compare_select_fusion, pred[64]{0:T(512)(128)(4,1)S(1)} %iota_compare_fusion), kind=kLoop, calls=%fused_computation | loop fusion | flops 917504 | bytes 524608 | tf_op jit(solution)/shard_map/convert_element_type | solution.py:261
  7.4 0.6 %collective-permute-start.1 = (bf16[64,2048]{1,0:T(8,128)(2,1)S(1)}, bf16[64,2048]{1,0:T(8,128)(2,1)S(1)}, u32[]{:S(2)}, u32[]{:S(2)}) collective-permute-start(bf16[64,2048]{1,0:T(8,128)(2,1)S(1)} %multiply_convert_fusion.refs_0_), channel_id=1, source_target_pairs={{0,8},{1,9},{2,10},{3,11},{4,12},{5,13},{6,14},{7,15},{8,0},{9,1},... | collective-permute-start | bytes 786440 | tf_op jit(solution)/shard_map/ppermute | solution.py:255
  8.0 0.0 collective-permute-start
  8.0 1.1 %collective-permute-start.5 = (bf16[272,512]{1,0:T(8,128)(2,1)S(1)}, bf16[272,512]{1,0:T(8,128)(2,1)S(1)}, u32[]{:S(2)}, u32[]{:S(2)}) collective-permute-start(bf16[272,512]{1,0:T(8,128)(2,1)S(1)} %maximum_maximum_fusion.refs_4_), channel_id=1, source_target_pairs={{0,6},{1,7},{2,4},{3,5},{4,2},{5,3},{6,0},{7,1},{8,14},{9,15},{10,... | collective-permute-start | bytes 835592 | tf_op jit(solution)/shard_map/ppermute | solution.py:255
  9.1 1.0 %collective-permute-start.3 = (bf16[272,512]{1,0:T(8,128)(2,1)S(1)}, bf16[272,512]{1,0:T(8,128)(2,1)S(1)}, u32[]{:S(2)}, u32[]{:S(2)}) collective-permute-start(bf16[272,512]{1,0:T(8,128)(2,1)S(1)} %maximum_maximum_fusion.refs_4_), channel_id=1, source_target_pairs={{0,2},{1,3},{2,0},{3,1},{4,6},{5,7},{6,4},{7,5},{8,10},{9,11},{10,... | collective-permute-start | bytes 835592 | tf_op jit(solution)/shard_map/ppermute | solution.py:255
  10.7 0.1 stack.19.info_ref
  10.8 0.0 copy-start
  10.8 0.0 copy-start.1
  10.8 6.0 %collective-permute-done.1.refs_2_ = bf16[64,2048]{1,0:T(8,128)(2,1)S(1)} collective-permute-done((bf16[64,2048]{1,0:T(8,128)(2,1)S(1)}, bf16[64,2048]{1,0:T(8,128)(2,1)S(1)}, u32[]{:S(2)}, u32[]{:S(2)}) %collective-permute-start.1) | collective-permute-done | bytes 262176 | tf_op jit(solution)/shard_map/ppermute | solution.py:255
  16.8 0.0 collective-permute-start.2
  16.8 0.0 collective-permute-done.4.refs_0_
  16.8 0.0 collective-permute-done.refs_1_
  16.8 1.5 %collective-permute-done.2.refs_3_ = bf16[64,2048]{1,0:T(8,128)(2,1)S(1)} collective-permute-done((bf16[64,2048]{1,0:T(8,128)(2,1)S(1)}, bf16[64,2048]{1,0:T(8,128)(2,1)S(1)}, u32[]{:S(2)}, u32[]{:S(2)}) %collective-permute-start.2) | collective-permute-done | bytes 262176 | tf_op jit(solution)/shard_map/ppermute | solution.py:255
  18.3 0.0 copy-done
  18.3 0.0 copy-done.1
  18.3 1.5 %stats_first.1.refs_8_ = f32[16,512]{1,0:T(8,128)S(1)} custom-call(s32[5]{0:T(128)S(1)} %stack.19.info_ref, bf16[64,2048]{1,0:T(8,128)(2,1)S(1)} %multiply_convert_fusion.refs_0_, bf16[64,2048]{1,0:T(8,128)(2,1)S(1)} %collective-permute-done.refs_1_, bf16[64,2048]{1,0:T(8,128)(2,1)S(1)} %collective-permute-done.1.refs_2_, ...), custom_call_target="tpu_custom_call" | custom-call | tf_op jit(solution)/shard_map/stats_first/pallas_call | solution.py:283
  19.9 0.0 collective-permute-done.5.refs_7_
  19.9 0.0 collective-permute-done.3.refs_5_
  19.9 1.5 %stats.1.refs_12_ = f32[56,128]{1,0:T(8,128)S(1)} custom-call(s32[5]{0:T(128)S(1)} %stack.19.info_ref, bf16[64,2048]{1,0:T(8,128)(2,1)S(1)} %multiply_convert_fusion.refs_0_, bf16[64,2048]{1,0:T(8,128)(2,1)S(1)} %collective-permute-done.refs_1_, bf16[64,2048]{1,0:T(8,128)(2,1)S(1)} %collective-permute-done.1.refs_2_, ...), custom_call_target="tpu_custom_call" | custom-call | tf_op jit(solution)/shard_map/stats/pallas_call | solution.py:291
  21.4 0.9 %collective-permute-start.8 = (f32[56,128]{1,0:T(8,128)S(1)}, f32[56,128]{1,0:T(8,128)S(1)}, u32[]{:S(2)}, u32[]{:S(2)}) collective-permute-start(f32[56,128]{1,0:T(8,128)S(1)} %stats.1.refs_12_), channel_id=1, source_target_pairs={{0,9},{1,8},{2,11},{3,10},{4,13},{5,12},{6,15},{7,14},{8,1},{9,0},... | collective-permute-start | bytes 86024 | tf_op jit(solution)/shard_map/ppermute | solution.py:255
  22.3 2.5 %collective-permute-start.7 = (f32[56,128]{1,0:T(8,128)S(1)}, f32[56,128]{1,0:T(8,128)S(1)}, u32[]{:S(2)}, u32[]{:S(2)}) collective-permute-start(f32[56,128]{1,0:T(8,128)S(1)} %stats.1.refs_12_), channel_id=1, source_target_pairs={{0,8},{1,9},{2,10},{3,11},{4,12},{5,13},{6,14},{7,15},{8,0},{9,1},... | collective-permute-start | bytes 86024 | tf_op jit(solution)/shard_map/ppermute | solution.py:255
  24.8 0.1 collective-permute-start.6
  24.9 1.9 %terms.1 = (f32[2176,512]{1,0:T(8,128)S(1)}, f32[2176,512]{1,0:T(8,128)S(1)}) custom-call(s32[5]{0:T(128)S(1)} %stack.19.info_ref, bf16[64,2048]{1,0:T(8,128)(2,1)S(1)} %multiply_convert_fusion.refs_0_, bf16[64,2048]{1,0:T(8,128)(2,1)S(1)} %collective-permute-done.refs_1_, bf16[64,2048]{1,0:T(8,128)(2,1)S(1)} %collective-permute-done.1.refs_2_, ...), custom_call_target="tpu_custom_call" | custom-call | tf_op jit(solution)/shard_map/terms/pallas_call | solution.py:301
  26.7 0.0 collective-permute-done.8.refs_15_
  26.8 1.0 %collective-permute-done.7.refs_14_ = f32[56,128]{1,0:T(8,128)S(1)} collective-permute-done((f32[56,128]{1,0:T(8,128)S(1)}, f32[56,128]{1,0:T(8,128)S(1)}, u32[]{:S(2)}, u32[]{:S(2)}) %collective-permute-start.7) | collective-permute-done | bytes 28704 | tf_op jit(solution)/shard_map/ppermute | solution.py:255
  27.8 0.0 collective-permute-done.6.refs_13_
  27.8 1.9 %grads.1 = (f32[512,128]{1,0:T(8,128)S(1)}, f32[512,128]{1,0:T(8,128)S(1)}, bf16[1024,128]{1,0:T(8,128)(2,1)S(1)}, f32[1024,128]{1,0:T(8,128)S(1)}, bf16[1024,12...) custom-call(bf16[64,2048]{1,0:T(8,128)(2,1)S(1)} %multiply_convert_f, ...), custom_call_target="tpu_custom_call" | custom-call | tf_op jit(solution)/shard_map/grads/pallas_call | solution.py:311
  29.6 0.1 collective-permute-start.9
  29.7 0.2 collective-permute-start.11
  30.0 2.8 %collective-permute-start.12 = (bf16[1024,128]{1,0:T(8,128)(2,1)S(1)}, bf16[1024,128]{1,0:T(8,128)(2,1)S(1)}, u32[]{:S(2)}, u32[]{:S(2)}) collective-permute-start(bf16[1024,128]{1,0:T(8,128)(2,1)S(1)} %get-tuple-element.28), channel_id=1, source_target_pairs={{0,4},{1,5},{2,6},{3,7},{4,0},{5,1},{6,2},{7,3},{8,12},{9,13},{10,... | collective-permute-start | bytes 786440 | tf_op jit(solution)/shard_map/ppermute | solution.py:255
  32.8 1.7 %collective-permute-start.13 = (bf16[1024,128]{1,0:T(8,128)(2,1)S(1)}, bf16[1024,128]{1,0:T(8,128)(2,1)S(1)}, u32[]{:S(2)}, u32[]{:S(2)}) collective-permute-start(bf16[1024,128]{1,0:T(8,128)(2,1)S(1)} %get-tuple-element.29), channel_id=1, source_target_pairs={{0,6},{1,7},{2,4},{3,5},{4,2},{5,3},{6,0},{7,1},{8,14},{9,15},{10,... | collective-permute-start | bytes 786440 | tf_op jit(solution)/shard_map/ppermute | solution.py:255
  34.5 0.0 collective-permute-done.9.refs_1_
  34.6 2.5 %collective-permute-start.10 = (bf16[512,128]{1,0:T(8,128)(2,1)S(1)}, bf16[512,128]{1,0:T(8,128)(2,1)S(1)}, u32[]{:S(2)}, u32[]{:S(2)}) collective-permute-start(bf16[512,128]{1,0:T(8,128)(2,1)S(1)} %add_convert_fusion), channel_id=1, source_target_pairs={{0,8},{1,9},{2,10},{3,11},{4,12},{5,13},{6,14},{7,15},{8,0},{9,1},... | collective-permute-start | bytes 393224 | tf_op jit(solution)/shard_map/ppermute | solution.py:255
  37.0 17.5 %all_to_all.5.refs_8_ = f32[16,1,1]{2,1,0:T(1,128)S(1)} all-to-all(f32[16,1,1]{2,1,0:T(1,128)S(1)} %get-tuple-element.31), channel_id=1, replica_groups=mesh['prompt'=16,'sample'=16] {'prompt'}, dimensions={0} | all-to-all | bytes 128 | tf_op jit(solution)/shard_map/all_to_all | solution.py:329
  54.5 0.0 collective-permute-done.11.refs_4_
  54.5 0.0 collective-permute-done.12.refs_5_
  54.5 0.0 collective-permute-done.13.refs_6_
  54.6 0.0 collective-permute-done.10.refs_2_
  54.6 0.9 %finish.1 = (bf16[32,2048]{1,0:T(8,128)(2,1)}, bf16[128,512]{1,0:T(8,128)(2,1)}, bf16[128,512]{1,0:T(8,128)(2,1)}, bf16[32,512]{1,0:T(8,128)(2,1)}, bf16[32,512]{1,0:T(8,128)(2,1)}) custom-call(f32[512,128]{1,0:T(8,128)S(1)} %get-tuple-element.23.refs_0_, bf16[1024,128]{1,0:T(8,128)(2,1)S(1)} %collective-permute-done.9.refs_1_, ...), custom_call_target="tpu_custom_call" | custom-call | tf_op jit(solution)/shard_map/finish/pallas_call | solution.py:331
  (6 shorter events, 0.1 us)
Async XLA Ops:
  2.4 14.4 %collective-permute-start.4 = (bf16[272,512]{1,0:T(8,128)(2,1)S(1)}, bf16[272,512]{1,0:T(8,128)(2,1)S(1)}, u32[]{:S(2)}, u32[]{:S(2)}) collective-permute-start(bf16[272,512]{1,0:T(8,128)(2,1)S(1)} %maximum_maximum_fusion.refs_4_), channel_id=1, source_target_pairs={{0,4},{1,5},{2,6},{3,7},{4,0},{5,1},{6,2},{7,3},{8,12},{9,13},{10,... | collective-permute-start | bytes 835592 | tf_op jit(solution)/shard_map/ppermute | solution.py:255
  7.4 9.4 %collective-permute-start.1 = (bf16[64,2048]{1,0:T(8,128)(2,1)S(1)}, bf16[64,2048]{1,0:T(8,128)(2,1)S(1)}, u32[]{:S(2)}, u32[]{:S(2)}) collective-permute-start(bf16[64,2048]{1,0:T(8,128)(2,1)S(1)} %multiply_convert_fusion.refs_0_), channel_id=1, source_target_pairs={{0,8},{1,9},{2,10},{3,11},{4,12},{5,13},{6,14},{7,15},{8,0},{9,1},... | collective-permute-start | bytes 786440 | tf_op jit(solution)/shard_map/ppermute | solution.py:255
  8.0 8.8 %collective-permute-start = (bf16[64,2048]{1,0:T(8,128)(2,1)S(1)}, bf16[64,2048]{1,0:T(8,128)(2,1)S(1)}, u32[]{:S(2)}, u32[]{:S(2)}) collective-permute-start(bf16[64,2048]{1,0:T(8,128)(2,1)S(1)} %multiply_convert_fusion.refs_0_), channel_id=1, source_target_pairs={{0,1},{1,0},{2,3},{3,2},{4,5},{5,4},{6,7},{7,6},{8,9},{9,8},{10,11... | collective-permute-start | bytes 786440 | tf_op jit(solution)/shard_map/ppermute | solution.py:255
  8.0 11.8 %collective-permute-start.5 = (bf16[272,512]{1,0:T(8,128)(2,1)S(1)}, bf16[272,512]{1,0:T(8,128)(2,1)S(1)}, u32[]{:S(2)}, u32[]{:S(2)}) collective-permute-start(bf16[272,512]{1,0:T(8,128)(2,1)S(1)} %maximum_maximum_fusion.refs_4_), channel_id=1, source_target_pairs={{0,6},{1,7},{2,4},{3,5},{4,2},{5,3},{6,0},{7,1},{8,14},{9,15},{10,... | collective-permute-start | bytes 835592 | tf_op jit(solution)/shard_map/ppermute | solution.py:255
  9.1 10.8 %collective-permute-start.3 = (bf16[272,512]{1,0:T(8,128)(2,1)S(1)}, bf16[272,512]{1,0:T(8,128)(2,1)S(1)}, u32[]{:S(2)}, u32[]{:S(2)}) collective-permute-start(bf16[272,512]{1,0:T(8,128)(2,1)S(1)} %maximum_maximum_fusion.refs_4_), channel_id=1, source_target_pairs={{0,2},{1,3},{2,0},{3,1},{4,6},{5,7},{6,4},{7,5},{8,10},{9,11},{10,... | collective-permute-start | bytes 835592 | tf_op jit(solution)/shard_map/ppermute | solution.py:255
  10.8 7.5 %copy-start = (bf16[1,1,32,512]{3,2,1,0:T(8,128)(2,1)S(1)}, bf16[1,1,32,512]{3,2,1,0:T(8,128)(2,1)}, u32[]{:S(2)}) copy-start(bf16[1,1,32,512]{3,2,1,0:T(8,128)(2,1)} %param.15) | copy-start | bytes 98308
  10.8 7.5 %copy-start.1 = (bf16[1,1,32,512]{3,2,1,0:T(8,128)(2,1)S(1)}, bf16[1,1,32,512]{3,2,1,0:T(8,128)(2,1)}, u32[]{:S(2)}) copy-start(bf16[1,1,32,512]{3,2,1,0:T(8,128)(2,1)} %param.16) | copy-start | bytes 98308
  16.8 1.5 %collective-permute-start.2 = (bf16[64,2048]{1,0:T(8,128)(2,1)S(1)}, bf16[64,2048]{1,0:T(8,128)(2,1)S(1)}, u32[]{:S(2)}, u32[]{:S(2)}) collective-permute-start(bf16[64,2048]{1,0:T(8,128)(2,1)S(1)} %collective-permute-done.1.refs_2_), channel_id=1, source_target_pairs={{0,1},{1,0},{2,3},{3,2},{4,5},{5,4},{6,7},{7,6},{8,9},{9,8},{10,11... | collective-permute-start | bytes 786440 | tf_op jit(solution)/shard_map/ppermute | solution.py:255
  21.4 5.3 %collective-permute-start.8 = (f32[56,128]{1,0:T(8,128)S(1)}, f32[56,128]{1,0:T(8,128)S(1)}, u32[]{:S(2)}, u32[]{:S(2)}) collective-permute-start(f32[56,128]{1,0:T(8,128)S(1)} %stats.1.refs_12_), channel_id=1, source_target_pairs={{0,9},{1,8},{2,11},{3,10},{4,13},{5,12},{6,15},{7,14},{8,1},{9,0},... | collective-permute-start | bytes 86024 | tf_op jit(solution)/shard_map/ppermute | solution.py:255
  22.3 5.5 %collective-permute-start.7 = (f32[56,128]{1,0:T(8,128)S(1)}, f32[56,128]{1,0:T(8,128)S(1)}, u32[]{:S(2)}, u32[]{:S(2)}) collective-permute-start(f32[56,128]{1,0:T(8,128)S(1)} %stats.1.refs_12_), channel_id=1, source_target_pairs={{0,8},{1,9},{2,10},{3,11},{4,12},{5,13},{6,14},{7,15},{8,0},{9,1},... | collective-permute-start | bytes 86024 | tf_op jit(solution)/shard_map/ppermute | solution.py:255
  24.8 3.0 %collective-permute-start.6 = (f32[56,128]{1,0:T(8,128)S(1)}, f32[56,128]{1,0:T(8,128)S(1)}, u32[]{:S(2)}, u32[]{:S(2)}) collective-permute-start(f32[56,128]{1,0:T(8,128)S(1)} %stats.1.refs_12_), channel_id=1, source_target_pairs={{0,1},{1,0},{2,3},{3,2},{4,5},{5,4},{6,7},{7,6},{8,9},{9,8},{10,11... | collective-permute-start | bytes 86024 | tf_op jit(solution)/shard_map/ppermute | solution.py:255
  29.6 4.9 %collective-permute-start.9 = (bf16[1024,128]{1,0:T(8,128)(2,1)S(1)}, bf16[1024,128]{1,0:T(8,128)(2,1)S(1)}, u32[]{:S(2)}, u32[]{:S(2)}) collective-permute-start(bf16[1024,128]{1,0:T(8,128)(2,1)S(1)} %get-tuple-element.24), channel_id=1, source_target_pairs={{0,1},{1,0},{2,3},{3,2},{4,5},{5,4},{6,7},{7,6},{8,9},{9,8},{10,11... | collective-permute-start | bytes 786440 | tf_op jit(solution)/shard_map/ppermute | solution.py:255
  29.7 24.8 %collective-permute-start.11 = (bf16[1024,128]{1,0:T(8,128)(2,1)S(1)}, bf16[1024,128]{1,0:T(8,128)(2,1)S(1)}, u32[]{:S(2)}, u32[]{:S(2)}) collective-permute-start(bf16[1024,128]{1,0:T(8,128)(2,1)S(1)} %get-tuple-element.27), channel_id=1, source_target_pairs={{0,2},{1,3},{2,0},{3,1},{4,6},{5,7},{6,4},{7,5},{8,10},{9,11},{10,... | collective-permute-start | bytes 786440 | tf_op jit(solution)/shard_map/ppermute | solution.py:255
  30.0 24.6 %collective-permute-start.12 = (bf16[1024,128]{1,0:T(8,128)(2,1)S(1)}, bf16[1024,128]{1,0:T(8,128)(2,1)S(1)}, u32[]{:S(2)}, u32[]{:S(2)}) collective-permute-start(bf16[1024,128]{1,0:T(8,128)(2,1)S(1)} %get-tuple-element.28), channel_id=1, source_target_pairs={{0,4},{1,5},{2,6},{3,7},{4,0},{5,1},{6,2},{7,3},{8,12},{9,13},{10,... | collective-permute-start | bytes 786440 | tf_op jit(solution)/shard_map/ppermute | solution.py:255
  32.8 21.8 %collective-permute-start.13 = (bf16[1024,128]{1,0:T(8,128)(2,1)S(1)}, bf16[1024,128]{1,0:T(8,128)(2,1)S(1)}, u32[]{:S(2)}, u32[]{:S(2)}) collective-permute-start(bf16[1024,128]{1,0:T(8,128)(2,1)S(1)} %get-tuple-element.29), channel_id=1, source_target_pairs={{0,6},{1,7},{2,4},{3,5},{4,2},{5,3},{6,0},{7,1},{8,14},{9,15},{10,... | collective-permute-start | bytes 786440 | tf_op jit(solution)/shard_map/ppermute | solution.py:255
  34.6 20.0 %collective-permute-start.10 = (bf16[512,128]{1,0:T(8,128)(2,1)S(1)}, bf16[512,128]{1,0:T(8,128)(2,1)S(1)}, u32[]{:S(2)}, u32[]{:S(2)}) collective-permute-start(bf16[512,128]{1,0:T(8,128)(2,1)S(1)} %add_convert_fusion), channel_id=1, source_target_pairs={{0,8},{1,9},{2,10},{3,11},{4,12},{5,13},{6,14},{7,15},{8,0},{9,1},... | collective-permute-start | bytes 393224 | tf_op jit(solution)/shard_map/ppermute | solution.py:255
